TPU v7x, 128 devices: a whole 4x4x4 slice. The times are simulated.
128 devices in a mesh: gx: 4 (over y_hi, core), gy: 32 (over x, z, y_lo).
Axes of the slice: x: 4, y: 4 (y_hi: 2, y_lo: 2; y = y_hi * 2 + y_lo), z: 4, core: 2. Of those that a mesh axis runs over, the one named last changes fastest.
Arguments:
- right_side: float32 [32, 256, 128, 128], P('gx', 'gy'), may hold values from -6 to 6
- diag_blocks: float32 [32, 256, 128, 128], P('gx', 'gy'), as said below
- smoother: float32 [32, 256, 128, 128], P('gx', 'gy'), as said below
- face_weight: float32 [32, 256, 4, 128], P('gx', 'gy'), may hold values from 0.3 to 1.5
- restrict_weight: float32 [32, 256, 128], P('gx', 'gy'), may hold values from 0.2 to 1
- prolong_weight: float32 [32, 256, 128], P('gx', 'gy'), may hold values from 0.3 to 1.2
- block_owner: int32 [32, 256], P('gx', 'gy'), may hold values from 0 to 31, as said below
- block_aggregate: int32 [32, 256], P('gx', 'gy'), may hold values from 0 to 31, as said below
- coarse_diag: float32 [1024, 128, 128], P('gy'), as said below
- coarse_smooth: float32 [1024, 128, 128], P('gy'), as said below
- neighbors: int32 [1024, 6], P('gy'), may hold values from 0 to 1023, as said below
- neighbor_weight: float32 [1024, 6, 128], P('gy'), may hold values from 0.2 to 1
Outputs:
- solution: float32 [32, 256, 128, 128], P('gx', 'gy')
- fine_residual: float32 [32, 256, 128, 128], P('gx', 'gy')
Inputs may be any that keep to these rules, and one draw needn't show every extreme that they name: block_owner[p,q] differs from q // 8 by at most one. Within one device's blocks, 1 to 16 name the lower neighbouring owner and 1 to 16 the upper one (none beyond the ends of gy), and for every index of gy some device sends exactly 16 each way that exists. block_aggregate[p,q] differs from p * 1 by at most one. neighbors[a,n] // 32 differs from a // 32 by at most one. `diag_blocks`: each matrix has its diagonal between 4 and 8 and off-diagonal entries within 0.2 in magnitude. `smoother`: each matrix has its diagonal between 0.12 and 0.25 and off-diagonal entries within 0.006 in magnitude. `coarse_diag`: each matrix has its diagonal between 4 and 8 and off-diagonal entries within 0.2 in magnitude. `coarse_smooth`: each matrix has its diagonal between 0.12 and 0.25 and off-diagonal entries within 0.006 in magnitude.
All inputs are finite; a program needn't handle non-finite values.
Results may differ from a plain program's by a relative error of at most 0.000073.
Values sent between devices are 32-bit elements; how exact they have to be, the bound alone decides.
No kernel may reach another device: no remote copies, remote signals or barrier semaphores. Data moves between devices by JAX's collectives and lax.ppermute only.
A program may use at most 320 MiB of HBM per device.

v0:
```python
import jax
import jax.numpy as jnp
from jax import lax
from jax.sharding import PartitionSpec as P

HIGHEST = lax.Precision.HIGHEST


def extended(block, sides, width):
    for axis, dim in sides:
        count = lax.axis_size(axis)
        forward = [(i, i + 1) for i in range(count - 1)]
        backward = [(target, source) for source, target in forward]
        low = lax.ppermute(
            lax.slice_in_dim(block, block.shape[dim] - width, None, axis=dim), axis, forward
        )
        high = lax.ppermute(lax.slice_in_dim(block, 0, width, axis=dim), axis, backward)
        block = jnp.concatenate([low, block, high], axis=dim)
    return block


def passed_along(array, axis, by):
    size = lax.axis_size(axis)
    pairs = [(i, i + by) for i in range(size) if 0 <= i + by < size]
    return lax.ppermute(array, axis, pairs)


def apply_blocks(matrices, vector):
    return jnp.einsum("...ij,...kj->...ki", matrices, vector, precision=HIGHEST)


def fine_apply(vector, diag_blocks, face_weight):
    padded = extended(vector, (("gx", 0), ("gy", 1)), 1)
    result = apply_blocks(diag_blocks, vector)
    result = result - face_weight[:, :, 0, None, :] * padded[:-2, 1:-1]
    result = result - face_weight[:, :, 1, None, :] * padded[2:, 1:-1]
    result = result - face_weight[:, :, 2, None, :] * padded[1:-1, :-2]
    result = result - face_weight[:, :, 3, None, :] * padded[1:-1, 2:]
    return result


def coarse_cycle(coarse_diag, coarse_smooth, neighbors, neighbor_weight, coarse_rhs):
    agg_count = coarse_rhs.shape[0]
    nbr_count = neighbors.shape[1]
    first_pass = apply_blocks(coarse_smooth, coarse_rhs)
    window = extended(first_pass, (("gy", 0),), agg_count)
    offsets = neighbors - (lax.axis_index("gy") - 1) * agg_count
    gathered = jnp.take(window, offsets.reshape(-1), axis=0)
    gathered = gathered.reshape(agg_count, nbr_count, coarse_rhs.shape[1], coarse_rhs.shape[2])
    coupling = jnp.sum(neighbor_weight[:, :, None, :] * gathered, axis=1)
    image = apply_blocks(coarse_diag, first_pass) - coupling
    return first_pass + apply_blocks(coarse_smooth, coarse_rhs - image)


def pack_slots(mask, weighted, local_ids, capacity):
    block_count = mask.shape[0]
    flags = mask.astype(jnp.int32)
    ranks = jnp.cumsum(flags) - flags
    hits = mask[None, :] & (ranks[None, :] == jnp.arange(capacity, dtype=jnp.int32)[:, None])
    valid = jnp.any(hits, axis=1)
    chosen = jnp.sum(
        hits.astype(jnp.int32) * jnp.arange(block_count, dtype=jnp.int32)[None, :], axis=1
    )
    rows = jnp.take(weighted, chosen, axis=0) * valid[:, None].astype(jnp.float32)
    slot_ids = jnp.where(valid, jnp.take(local_ids, chosen), 0)
    return (rows, slot_ids, ranks)


def body(
    right_side,
    diag_blocks,
    smoother,
    face_weight,
    restrict_weight,
    prolong_weight,
    block_owner,
    block_aggregate,
    coarse_diag,
    coarse_smooth,
    neighbors,
    neighbor_weight,
):
    blocks_x, blocks_y, rhs_count, block_size = right_side.shape
    block_count = blocks_x * blocks_y
    row_width = rhs_count * block_size
    agg_count = coarse_diag.shape[0]
    capacity = max(2, block_count // 4)
    first_sweep = apply_blocks(smoother, right_side)
    fine_part = first_sweep + apply_blocks(
        smoother, right_side - fine_apply(first_sweep, diag_blocks, face_weight)
    )
    owners_flat = block_owner.reshape(block_count)
    local_ids = block_aggregate.reshape(block_count)
    weighted = (restrict_weight[:, :, None, :] * right_side).reshape(block_count, row_width)
    my_index = lax.axis_index("gy")
    own_mask = owners_flat == my_index
    lower_mask = owners_flat == my_index - 1
    upper_mask = owners_flat == my_index + 1
    down_rows, down_ids, lower_rank = pack_slots(lower_mask, weighted, local_ids, capacity)
    up_rows, up_ids, upper_rank = pack_slots(upper_mask, weighted, local_ids, capacity)
    above_rows, above_ids = passed_along((down_rows, down_ids), "gy", -1)
    below_rows, below_ids = passed_along((up_rows, up_ids), "gy", 1)
    all_rows = jnp.concatenate(
        [weighted * own_mask[:, None].astype(jnp.float32), above_rows, below_rows], axis=0
    )
    all_ids = jnp.concatenate([local_ids, above_ids, below_ids], axis=0)
    collect = (all_ids[None, :] == jnp.arange(agg_count, dtype=jnp.int32)[:, None]).astype(
        jnp.float32
    )
    partial_value = jnp.dot(collect, all_rows, precision=HIGHEST).reshape(
        agg_count, rhs_count, block_size
    )
    coarse_rhs = lax.psum(partial_value, "gx")
    coarse_corr = coarse_cycle(coarse_diag, coarse_smooth, neighbors, neighbor_weight, coarse_rhs)
    coarse_flat = coarse_corr.reshape(agg_count, row_width)
    answers_above = jnp.take(coarse_flat, above_ids, axis=0)
    answers_below = jnp.take(coarse_flat, below_ids, axis=0)
    from_lower = passed_along(answers_above, "gy", 1)
    from_upper = passed_along(answers_below, "gy", -1)
    table = jnp.concatenate([coarse_flat, from_lower, from_upper], axis=0)
    lookup = jnp.where(
        own_mask,
        local_ids,
        jnp.where(lower_mask, agg_count + lower_rank, agg_count + capacity + upper_rank),
    )
    spread = jnp.take(table, lookup, axis=0)
    spread = spread.reshape(blocks_x, blocks_y, rhs_count, block_size)
    solution = fine_part + prolong_weight[:, :, None, :] * spread
    fine_residual = right_side - fine_apply(solution, diag_blocks, face_weight)
    return (solution, fine_residual)


def solution(mesh):
    return jax.shard_map(
        body,
        mesh=mesh,
        in_specs=(
            P("gx", "gy", None, None),
            P("gx", "gy", None, None),
            P("gx", "gy", None, None),
            P("gx", "gy", None, None),
            P("gx", "gy", None),
            P("gx", "gy", None),
            P("gx", "gy"),
            P("gx", "gy"),
            P("gy", None, None),
            P("gy", None, None),
            P("gy", None),
            P("gy", None, None),
        ),
        out_specs=(P("gx", "gy", None, None), P("gx", "gy", None, None)),
        check_vma=False,
    )
```

profile of v0, /device:TPU:1, one launch (start us, length us, event | category | flops | bytes accessed | tf_op | source)
XLA Modules:
  0.0 457.1 jit_solution(1802889953453130226)
XLA Ops:
  32.0 4.7 %collective-permute-start.7 = (f32[16,16384]{1,0:T(8,128)}, f32[16,16384]{1,0:T(8,128)S(1)}, u32[]{:S(2)}, u32[]{:S(2)}) collective-permute-start(f32[16,16384]{1,0:T(8,128)} %select_multiply_fusion), channel_id=1, source_target_pairs={{0,1},{1,2},{2,3},{3,4},{4,5},{5,6},{6,7},{7,8},{8,9},{9,10},{10,1... | collective-permute-start | bytes 3145736 | tf_op jit(solution)/shard_map/ppermute | solution.py:25
  38.0 5.0 %collective-permute-start.5 = (s32[16]{0:T(128)S(1)}, s32[16]{0:T(128)S(1)}, u32[]{:S(2)}, u32[]{:S(2)}) collective-permute-start(s32[16]{0:T(128)S(1)} %get-tuple-element.12), channel_id=1, source_target_pairs={{0,1},{1,2},{2,3},{3,4},{4,5},{5,6},{6,7},{7,8},{8,9},{9,10},{10,1... | collective-permute-start | bytes 200 | tf_op jit(solution)/shard_map/ppermute | solution.py:25
  43.1 4.8 %broadcast_multiply_fusion = f32[64,16384]{1,0:T(8,128)S(1)} fusion(f32[64]{0:T(128)S(1)} %reshape.258, f32[8,8,128,128]{3,2,1,0:T(8,128)} %copy-done.3), kind=kLoop, calls=%fused_computation.65 | loop fusion | flops 1048576 | bytes 8388864 | tf_op jit(solution)/shard_map/mul | solution.py:104
  47.9 26.0 %collective-permute-done.4 = s32[16]{0:T(128)S(1)} collective-permute-done((s32[16]{0:T(128)S(1)}, s32[16]{0:T(128)S(1)}, u32[]{:S(2)}, u32[]{:S(2)}) %collective-permute-start.4) | collective-permute-done | bytes 96 | tf_op jit(solution)/shard_map/ppermute | solution.py:25
  74.0 5.2 %collective-permute-done.5 = s32[16]{0:T(128)S(1)} collective-permute-done((s32[16]{0:T(128)S(1)}, s32[16]{0:T(128)S(1)}, u32[]{:S(2)}, u32[]{:S(2)}) %collective-permute-start.5) | collective-permute-done | bytes 96 | tf_op jit(solution)/shard_map/ppermute | solution.py:25
  84.8 14.4 %fusion.63 = f32[8,8,128,128]{3,2,1,0:T(8,128)} fusion(f32[8,8,128,128]{3,2,1,0:T(8,128)} %param.18, f32[8,8,128,128]{3,2,1,0:T(8,128)} %param.20), kind=kOutput, calls=%fused_computation.129 | convolution fusion | flops 1610612736 | bytes 12582912 | tf_op jit(solution)/shard_map/...ij,...kj->...ki/dot_general | solution.py:29
  99.2 44.4 %all-reduce.2.cloned.1.call-done = f32[32,128,128]{2,1,0:T(8,128)} async-done(((f32[32,128,128]{2,1,0:T(8,128)}), f32[32,128,128]{2,1,0:T(8,128)}) %all-reduce.2.cloned.1.call-update) | async-done | bytes 2097168 | tf_op jit(solution)/shard_map/psum | solution.py:113
  143.6 7.6 %fusion.65 = f32[32,128,128]{2,1,0:T(8,128)} fusion(f32[32,128,128]{2,1,0:T(8,128)} %all-reduce.2.cloned.1.call-done, f32[32,128,128]{2,1,0:T(8,128)S(1)} %copy-done), kind=kOutput, calls=%fused_computation.131 | convolution fusion | flops 805306368 | bytes 6291456 | tf_op jit(solution)/shard_map/...ij,...kj->...ki/dot_general | solution.py:29
  164.9 8.0 %fusion.66 = f32[32,128,128]{2,1,0:T(8,128)} fusion(f32[32,128,128]{2,1,0:T(8,128)} %fusion.65, f32[32,128,128]{2,1,0:T(8,128)} %param.26), kind=kOutput, calls=%fused_computation.132 | convolution fusion | flops 805306368 | bytes 6291456 | tf_op jit(solution)/shard_map/...ij,...kj->...ki/dot_general | solution.py:29
  172.9 70.3 %collective-permute-done.8 = f32[32,128,128]{2,1,0:T(8,128)} collective-permute-done((f32[32,128,128]{2,1,0:T(8,128)}, f32[32,128,128]{2,1,0:T(8,128)}, u32[]{:S(2)}, u32[]{:S(2)}) %collective-permute-start.8) | collective-permute-done | bytes 2097184 | tf_op jit(solution)/shard_map/ppermute | solution.py:14
  246.2 6.2 %pad_maximum_fusion = f32[96,128,128]{2,1,0:T(8,128)} fusion(f32[32,128,128]{2,1,0:T(8,128)} %collective-permute-done.9, f32[32,128,128]{2,1,0:T(8,128)} %fusion.65, f32[32,128,128]{2,1,0:T(8,128)} %collective-permute-done.8), kind=kLoop, calls=%fused_computation.15 | loop fusion | flops 3145728 | bytes 12582912 | tf_op jit(solution)/shard_map/concatenate | solution.py:18
  252.4 13.7 %gather_fusion = f32[192,128,128]{2,1,0:T(8,128)} fusion(f32[96,128,128]{2,1,0:T(8,128)} %pad_maximum_fusion, s32[1024]{0:T(1024)S(1)} %pad_clamp_fusion.3), kind=kCustom, calls=%fused_computation.6 | custom fusion | bytes 25166592 | tf_op jit(solution)/shard_map/jit(_take)/gather | solution.py:48
  266.1 6.7 %multiply_reduce_fusion = f32[32,128,128]{2,1,0:T(8,128)S(1)} fusion(f32[32,6,128,128]{3,2,1,0:T(8,128)} %bitcast.46, f32[32,6,128]{2,1,0:T(8,128)S(1)} %copy.33, pred[32,6]{1,0:T(8,128)(4,1)S(1)} %copy.34), kind=kLoop, calls=%fused_computation.8 | loop fusion | flops 8912896 | bytes 14778560 | tf_op jit(solution)/shard_map/reduce_sum | solution.py:50
  272.8 6.1 %fusion.42 = f32[32,128,128]{2,1,0:T(8,128)S(1)} fusion(f32[32,128,128]{2,1,0:T(8,128)} %fusion.65, f32[32,128,128]{2,1,0:T(8,128)S(1)} %copy-done, f32[32,128,128]{2,1,0:T(8,128)S(1)} %copy-done.5, f32[32,128,128]{2,1,0:T(8,128)S(1)} %copy-done.6, f32[32,128,128]{2,1,0:T(8,128)S(1)} %multiply_reduce_fusion), kind=kOutput, calls=%fused_computation.70 | convolution fusion | flops 806879232 | bytes 12582912 | tf_op jit(solution)/shard_map/...ij,...kj->...ki/dot_general | solution.py:29
  288.4 14.4 %fusion.64 = f32[8,8,128,128]{3,2,1,0:T(8,128)} fusion(f32[8,8,128,128]{3,2,1,0:T(8,128)} %fusion.63, f32[8,8,128,128]{3,2,1,0:T(8,128)} %param.19), kind=kOutput, calls=%fused_computation.130 | convolution fusion | flops 1610612736 | bytes 12582912 | tf_op jit(solution)/shard_map/...ij,...kj->...ki/dot_general | solution.py:29
  303.9 4.9 %collective-permute-start.2 = (f32[10,1,128,128]{3,2,1,0:T(8,128)S(1)}, f32[10,1,128,128]{3,2,1,0:T(8,128)}, u32[]{:S(2)}, u32[]{:S(2)}) collective-permute-start(f32[10,1,128,128]{3,2,1,0:T(8,128)S(1)} %get-tuple-element.20), channel_id=1, source_target_pairs={{0,1},{1,2},{2,3},{3,4},{4,5},{5,6},{6,7},{7,8},{8,9},{9,10},{10,1... | collective-permute-start | bytes 1966088 | tf_op jit(solution)/shard_map/ppermute | solution.py:14
  310.2 31.6 %collective-permute-done.10 = f32[16,16384]{1,0:T(8,128)} collective-permute-done((f32[16,16384]{1,0:T(8,128)}, f32[16,16384]{1,0:T(8,128)}, u32[]{:S(2)}, u32[]{:S(2)}) %collective-permute-start.10) | collective-permute-done | bytes 1048608 | tf_op jit(solution)/shard_map/ppermute | solution.py:25
  345.3 7.6 %gather_fusion.1 = f32[64,16384]{1,0:T(8,128)} fusion(f32[64,16384]{1,0:T(8,128)} %pad_maximum_fusion.21, s32[1024]{0:T(1024)S(1)} %pad_clamp_fusion), kind=kCustom, calls=%fused_computation.7 | custom fusion | bytes 8388864 | tf_op jit(solution)/shard_map/jit(_take)/gather | solution.py:126
  358.7 25.5 %fusion.7 = f32[8,8,128,128]{3,2,1,0:T(8,128)} fusion(f32[8,8,128,128]{3,1,2,0:T(8,128)} %bitcast.49, f32[8,8,128,128]{3,2,1,0:T(8,128)} %fusion.63, f32[8,8,128]{2,1,0:T(8,128)S(1)} %copy-done.14, pred[8,8]{1,0:T(8,128)(4,1)S(1)} %compare_and_fusion.1, f32[8,8,128,128]{3,2,1,0:T(8,128)} %param.20, f32[8,8,128,128]{3,2,1,0:T(8,128)} %param.18, ...), kind=kOutput, calls=%fused_computation.18 | convolution fusion | flops 1632632832 | bytes 27689024 | tf_op jit(solution)/shard_map/...ij,...kj->...ki/dot_general | solution.py:29
  385.7 5.0 %collective-permute-start.12 = (f32[1,8,128,128]{3,2,1,0:T(8,128)S(1)}, f32[1,8,128,128]{3,2,1,0:T(8,128)S(1)}, u32[]{:S(2)}, u32[]{:S(2)}) collective-permute-start(f32[1,8,128,128]{3,2,1,0:T(8,128)S(1)} %get-tuple-element.22), channel_id=1, source_target_pairs={{0,32},{32,64},{64,96},{1,33},{33,65},{65,97},{2,34},{34,66},{66,9... | collective-permute-start | bytes 1572872 | tf_op jit(solution)/shard_map/ppermute | solution.py:14
  396.8 8.1 %collective-permute-done.13 = f32[1,8,128,128]{3,2,1,0:T(8,128)S(1)} collective-permute-done((f32[1,8,128,128]{3,2,1,0:T(8,128)S(1)}, f32[1,8,128,128]{3,2,1,0:T(8,128)S(1)}, u32[]{:S(2)}, u32[]{:S(2)}) %collective-permute-start.13) | collective-permute-done | bytes 524320 | tf_op jit(solution)/shard_map/ppermute | solution.py:17
  406.5 4.6 %collective-permute-start.14 = (f32[10,1,128,128]{3,2,1,0:T(8,128)S(1)}, f32[10,1,128,128]{3,2,1,0:T(8,128)S(1)}, u32[]{:S(2)}, u32[]{:S(2)}) collective-permute-start(f32[10,1,128,128]{3,2,1,0:T(8,128)S(1)} %get-tuple-element.18), channel_id=1, source_target_pairs={{0,1},{1,2},{2,3},{3,4},{4,5},{5,6},{6,7},{7,8},{8,9},{9,10},{10,1... | collective-permute-start | bytes 1966088 | tf_op jit(solution)/shard_map/ppermute | solution.py:14
  412.6 15.6 %collective-permute-done.14 = f32[10,1,128,128]{3,2,1,0:T(8,128)S(1)} collective-permute-done((f32[10,1,128,128]{3,2,1,0:T(8,128)S(1)}, f32[10,1,128,128]{3,2,1,0:T(8,128)S(1)}, u32[]{:S(2)}, u32[]{:S(2)}) %collective-permute-start.14) | collective-permute-done | bytes 655392 | tf_op jit(solution)/shard_map/ppermute | solution.py:14
  429.7 20.3 %fusion.10 = f32[8,8,128,128]{3,2,1,0:T(8,128)} fusion(f32[8,8,128,128]{3,2,1,0:T(8,128)S(1)} %copy-done.4, f32[10,1,128,128]{3,2,1,0:T(8,128)} %collective-permute-done.15, f32[1,8,128,128]{3,2,1,0:T(8,128)} %copy-done.8, f32[8,8,128,128]{3,2,1,0:T(8,128)} %fusion.7, f32[1,8,128,128]{3,2,1,0:T(8,128)} %copy-done.7, f32[10,1,128,128]{3,2,1,0:T(8,128)} %copy-done.13, ...), kind=kOutput, calls=%fused_computation.23 | convolution fusion | flops 1628438528 | bytes 19267584 | tf_op jit(solution)/shard_map/...ij,...kj->...ki/dot_general | solution.py:29
  (118 shorter events, 81.5 us)
Async XLA Ops:
  7.2 136.4 %copy-start = (f32[32,128,128]{2,1,0:T(8,128)S(1)}, f32[32,128,128]{2,1,0:T(8,128)}, u32[]{:S(2)}) copy-start(f32[32,128,128]{2,1,0:T(8,128)} %param.27) | copy-start | bytes 6291460
  7.2 136.4 %all-reduce.2.cloned.1.call-start = ((), (), s32[]{:S(2)}) async-start(), calls=%async_computation | async-start | bytes 4194304 | tf_op jit(solution)/shard_map/psum | solution.py:113
  25.1 54.1 %collective-permute-start.6 = (f32[16,16384]{1,0:T(8,128)}, f32[16,16384]{1,0:T(8,128)}, u32[]{:S(2)}, u32[]{:S(2)}) collective-permute-start(f32[16,16384]{1,0:T(8,128)} %select_multiply_fusion.1), channel_id=1, source_target_pairs={{1,0},{2,1},{3,2},{4,3},{5,4},{6,5},{7,6},{8,7},{9,8},{10,9},{11,1... | collective-permute-start | bytes 3145736 | tf_op jit(solution)/shard_map/ppermute | solution.py:25
  32.0 47.3 %collective-permute-start.7 = (f32[16,16384]{1,0:T(8,128)}, f32[16,16384]{1,0:T(8,128)S(1)}, u32[]{:S(2)}, u32[]{:S(2)}) collective-permute-start(f32[16,16384]{1,0:T(8,128)} %select_multiply_fusion), channel_id=1, source_target_pairs={{0,1},{1,2},{2,3},{3,4},{4,5},{5,6},{6,7},{7,8},{8,9},{9,10},{10,1... | collective-permute-start | bytes 3145736 | tf_op jit(solution)/shard_map/ppermute | solution.py:25
  36.7 37.3 %collective-permute-start.4 = (s32[16]{0:T(128)S(1)}, s32[16]{0:T(128)S(1)}, u32[]{:S(2)}, u32[]{:S(2)}) collective-permute-start(s32[16]{0:T(128)S(1)} %get-tuple-element.10), channel_id=1, source_target_pairs={{1,0},{2,1},{3,2},{4,3},{5,4},{6,5},{7,6},{8,7},{9,8},{10,9},{11,1... | collective-permute-start | bytes 200 | tf_op jit(solution)/shard_map/ppermute | solution.py:25
  38.0 41.2 %collective-permute-start.5 = (s32[16]{0:T(128)S(1)}, s32[16]{0:T(128)S(1)}, u32[]{:S(2)}, u32[]{:S(2)}) collective-permute-start(s32[16]{0:T(128)S(1)} %get-tuple-element.12), channel_id=1, source_target_pairs={{0,1},{1,2},{2,3},{3,4},{4,5},{5,6},{6,7},{7,8},{8,9},{9,10},{10,1... | collective-permute-start | bytes 200 | tf_op jit(solution)/shard_map/ppermute | solution.py:25
  99.1 65.3 %copy-start.12 = (s32[32,6]{0,1:T(8,128)S(1)}, s32[32,6]{0,1:T(8,128)}, u32[]{:S(2)}) copy-start(s32[32,6]{0,1:T(8,128)} %param.28) | copy-start | bytes 2308
  99.1 65.6 %copy-start.10 = (f32[32,6,128]{2,0,1:T(8,128)S(1)}, f32[32,6,128]{2,0,1:T(8,128)}, u32[]{:S(2)}) copy-start(f32[32,6,128]{2,0,1:T(8,128)} %param.29) | copy-start | bytes 294916
  151.1 92.1 %collective-permute-start.8 = (f32[32,128,128]{2,1,0:T(8,128)}, f32[32,128,128]{2,1,0:T(8,128)}, u32[]{:S(2)}, u32[]{:S(2)}) collective-permute-start(f32[32,128,128]{2,1,0:T(8,128)} %fusion.65), channel_id=1, source_target_pairs={{0,1},{1,2},{2,3},{3,4},{4,5},{5,6},{6,7},{7,8},{8,9},{9,10},{10,1... | collective-permute-start | bytes 6291464 | tf_op jit(solution)/shard_map/ppermute | solution.py:14
  154.6 91.5 %collective-permute-start.9 = (f32[32,128,128]{2,1,0:T(8,128)}, f32[32,128,128]{2,1,0:T(8,128)}, u32[]{:S(2)}, u32[]{:S(2)}) collective-permute-start(f32[32,128,128]{2,1,0:T(8,128)} %fusion.65), channel_id=1, source_target_pairs={{1,0},{2,1},{3,2},{4,3},{5,4},{6,5},{7,6},{8,7},{9,8},{10,9},{11,1... | collective-permute-start | bytes 6291464 | tf_op jit(solution)/shard_map/ppermute | solution.py:17
  158.2 144.7 %collective-permute-start = (f32[1,8,128,128]{3,2,1,0:T(8,128)}, f32[1,8,128,128]{3,2,1,0:T(8,128)}, u32[]{:S(2)}, u32[]{:S(2)}) collective-permute-start(f32[1,8,128,128]{3,2,1,0:T(8,128)} %get-tuple-element.24), channel_id=1, source_target_pairs={{0,32},{32,64},{64,96},{1,33},{33,65},{65,97},{2,34},{34,66},{66,9... | collective-permute-start | bytes 1572872 | tf_op jit(solution)/shard_map/ppermute | solution.py:14
  162.3 140.5 %collective-permute-start.1 = (f32[1,8,128,128]{3,2,1,0:T(8,128)}, f32[1,8,128,128]{3,2,1,0:T(8,128)}, u32[]{:S(2)}, u32[]{:S(2)}) collective-permute-start(f32[1,8,128,128]{3,2,1,0:T(8,128)} %get-tuple-element.25), channel_id=1, source_target_pairs={{32,0},{64,32},{96,64},{33,1},{65,33},{97,65},{34,2},{66,34},{98,6... | collective-permute-start | bytes 1572872 | tf_op jit(solution)/shard_map/ppermute | solution.py:17
  282.2 59.6 %collective-permute-start.10 = (f32[16,16384]{1,0:T(8,128)}, f32[16,16384]{1,0:T(8,128)}, u32[]{:S(2)}, u32[]{:S(2)}) collective-permute-start(f32[16,16384]{1,0:T(8,128)} %broadcast_select_fusion.1), channel_id=1, source_target_pairs={{0,1},{1,2},{2,3},{3,4},{4,5},{5,6},{6,7},{7,8},{8,9},{9,10},{10,1... | collective-permute-start | bytes 3145736 | tf_op jit(solution)/shard_map/ppermute | solution.py:25
  286.5 55.3 %collective-permute-start.11 = (f32[16,16384]{1,0:T(8,128)S(1)}, f32[16,16384]{1,0:T(8,128)S(1)}, u32[]{:S(2)}, u32[]{:S(2)}) collective-permute-start(f32[16,16384]{1,0:T(8,128)S(1)} %broadcast_select_fusion), channel_id=1, source_target_pairs={{1,0},{2,1},{3,2},{4,3},{5,4},{6,5},{7,6},{8,7},{9,8},{10,9},{11,1... | collective-permute-start | bytes 3145736 | tf_op jit(solution)/shard_map/ppermute | solution.py:25
  303.9 51.9 %collective-permute-start.2 = (f32[10,1,128,128]{3,2,1,0:T(8,128)S(1)}, f32[10,1,128,128]{3,2,1,0:T(8,128)}, u32[]{:S(2)}, u32[]{:S(2)}) collective-permute-start(f32[10,1,128,128]{3,2,1,0:T(8,128)S(1)} %get-tuple-element.20), channel_id=1, source_target_pairs={{0,1},{1,2},{2,3},{3,4},{4,5},{5,6},{6,7},{7,8},{8,9},{9,10},{10,1... | collective-permute-start | bytes 1966088 | tf_op jit(solution)/shard_map/ppermute | solution.py:14
  308.7 50.0 %collective-permute-start.3 = (f32[10,1,128,128]{3,2,1,0:T(8,128)S(1)}, f32[10,1,128,128]{3,2,1,0:T(8,128)}, u32[]{:S(2)}, u32[]{:S(2)}) collective-permute-start(f32[10,1,128,128]{3,2,1,0:T(8,128)S(1)} %get-tuple-element.21), channel_id=1, source_target_pairs={{1,0},{2,1},{3,2},{4,3},{5,4},{6,5},{7,6},{8,7},{9,8},{10,9},{11,1... | collective-permute-start | bytes 1966088 | tf_op jit(solution)/shard_map/ppermute | solution.py:17
  384.2 45.5 %copy-start.4 = (f32[8,8,128,128]{3,2,1,0:T(8,128)S(1)}, f32[8,8,128,128]{3,2,1,0:T(8,128)}, u32[]{:S(2)}) copy-start(f32[8,8,128,128]{3,2,1,0:T(8,128)} %param.18) | copy-start | bytes 12582916
  385.7 11.1 %collective-permute-start.12 = (f32[1,8,128,128]{3,2,1,0:T(8,128)S(1)}, f32[1,8,128,128]{3,2,1,0:T(8,128)S(1)}, u32[]{:S(2)}, u32[]{:S(2)}) collective-permute-start(f32[1,8,128,128]{3,2,1,0:T(8,128)S(1)} %get-tuple-element.22), channel_id=1, source_target_pairs={{0,32},{32,64},{64,96},{1,33},{33,65},{65,97},{2,34},{34,66},{66,9... | collective-permute-start | bytes 1572872 | tf_op jit(solution)/shard_map/ppermute | solution.py:14
  390.7 14.2 %collective-permute-start.13 = (f32[1,8,128,128]{3,2,1,0:T(8,128)S(1)}, f32[1,8,128,128]{3,2,1,0:T(8,128)S(1)}, u32[]{:S(2)}, u32[]{:S(2)}) collective-permute-start(f32[1,8,128,128]{3,2,1,0:T(8,128)S(1)} %get-tuple-element.23), channel_id=1, source_target_pairs={{32,0},{64,32},{96,64},{33,1},{65,33},{97,65},{34,2},{66,34},{98,6... | collective-permute-start | bytes 1572872 | tf_op jit(solution)/shard_map/ppermute | solution.py:17
  396.8 31.4 %copy-start.7 = (f32[1,8,128,128]{3,2,1,0:T(8,128)}, f32[1,8,128,128]{3,2,1,0:T(8,128)S(1)}, u32[]{:S(2)}) copy-start(f32[1,8,128,128]{3,2,1,0:T(8,128)S(1)} %collective-permute-done.12) | copy-start | bytes 1572868
  404.9 23.3 %copy-start.8 = (f32[1,8,128,128]{3,2,1,0:T(8,128)}, f32[1,8,128,128]{3,2,1,0:T(8,128)S(1)}, u32[]{:S(2)}) copy-start(f32[1,8,128,128]{3,2,1,0:T(8,128)S(1)} %collective-permute-done.13) | copy-start | bytes 1572868
  406.5 21.8 %collective-permute-start.14 = (f32[10,1,128,128]{3,2,1,0:T(8,128)S(1)}, f32[10,1,128,128]{3,2,1,0:T(8,128)S(1)}, u32[]{:S(2)}, u32[]{:S(2)}) collective-permute-start(f32[10,1,128,128]{3,2,1,0:T(8,128)S(1)} %get-tuple-element.18), channel_id=1, source_target_pairs={{0,1},{1,2},{2,3},{3,4},{4,5},{5,6},{6,7},{7,8},{8,9},{9,10},{10,1... | collective-permute-start | bytes 1966088 | tf_op jit(solution)/shard_map/ppermute | solution.py:14
  411.1 18.7 %collective-permute-start.15 = (f32[10,1,128,128]{3,2,1,0:T(8,128)S(1)}, f32[10,1,128,128]{3,2,1,0:T(8,128)}, u32[]{:S(2)}, u32[]{:S(2)}) collective-permute-start(f32[10,1,128,128]{3,2,1,0:T(8,128)S(1)} %get-tuple-element.19), channel_id=1, source_target_pairs={{1,0},{2,1},{3,2},{4,3},{5,4},{6,5},{7,6},{8,7},{9,8},{10,9},{11,1... | collective-permute-start | bytes 1966088 | tf_op jit(solution)/shard_map/ppermute | solution.py:17
  429.7 20.3 %copy-start.1 = (f32[32,128,128]{2,1,0:T(8,128)S(1)}, f32[32,128,128]{2,1,0:T(8,128)}, u32[]{:S(2)}) copy-start(f32[32,128,128]{2,1,0:T(8,128)} %param.27) | copy-start | bytes 6291460
  (8 other events, 56.3 us)
Sparse Core Ops, SparseCore 0:
  84.9 58.6 all-reduce.1
where the time goes:
time: 463 us; the launch traced here: 457 us
  waiting for transfers between devices  215 us (46%)
  matrix products  100 us (22%)
  local copies, waits for them, and re-layouts  48.1 us (10%)
  starting transfers between devices  47.6 us (10%)
  other arithmetic  31.9 us (7%)
  between operations  14.7 us (3%)
    dot_general x7, matrix products, apply_blocks(): return jnp.einsum('...ij,...kj->...ki', matrices, vector, precision=HIGHEST)  96.3 us
    ppermute x5, waiting for transfers between devices, extended(): lax.ppermute(lax.slice_in_dim(block, block.shape[dim] - width, None, axis...  92.9 us
    ppermute x6, waiting for transfers between devices, passed_along(): return lax.ppermute(array, axis, pairs)  62.9 us
    psum x1, waiting for transfers between devices, body(): coarse_rhs = lax.psum(partial_value, 'gx')  44.4 us
    ppermute x5, starting transfers between devices, extended(): lax.ppermute(lax.slice_in_dim(block, block.shape[dim] - width, None, axis...  22.1 us
    ppermute x6, starting transfers between devices, passed_along(): return lax.ppermute(array, axis, pairs)  17.3 us
    ppermute x5, waiting for transfers between devices, extended(): lax.ppermute(lax.slice_in_dim(block, 0, width, axis=dim), axis, backward)  14.7 us
    gather x1, local copies, waits for them, and re-layouts, coarse_cycle(): gathered = jnp.take(window, offsets.reshape(-1), axis=0)  13.7 us
  transfers between devices with their start and end apart: 17, of which 12 were waited for; matrix products, arithmetic and copies ran while one was open for 22% of the time, Pallas kernels for 0%

commit v1 on v0

v1 whole, which is shorter than its diff:
```python
import functools

import jax
import jax.numpy as jnp
from jax import lax
from jax.experimental import pallas as pl
from jax.experimental.pallas import tpu as pltpu
from jax.sharding import PartitionSpec as P

F32 = jnp.float32
BF16 = jnp.bfloat16
VMEM_LIMIT = 40 * 1024 * 1024


def shifted(array, axis, by):
    size = lax.axis_size(axis)
    pairs = [(i, i + by) for i in range(size) if 0 <= i + by < size]
    return lax.ppermute(array, axis, pairs)


def halves(x):
    high = x.astype(BF16)
    low = (x - high.astype(F32)).astype(BF16)
    return high, low


def product(vector, matrix):
    vector_high, vector_low = halves(vector)
    matrix_high, matrix_low = halves(matrix)
    left = jnp.concatenate([vector_high, vector_low], axis=1)
    right = jnp.concatenate(
        [
            jnp.concatenate([matrix_high, matrix_high], axis=1),
            jnp.concatenate([matrix_low, matrix_low], axis=1),
        ],
        axis=0,
    )
    both = lax.dot_general(left, right, (((1,), (1,)), ((), ())), preferred_element_type=F32)
    width = matrix.shape[0]
    return both[:, :width] + both[:, width:]


def call(kernel, grid, in_specs, out_specs, out_shape, scalars=0, scratch=(), flops=0, moved=0):
    return pl.pallas_call(
        kernel,
        grid_spec=pltpu.PrefetchScalarGridSpec(
            num_scalar_prefetch=scalars,
            grid=(grid,),
            in_specs=in_specs,
            out_specs=out_specs,
            scratch_shapes=list(scratch),
        ),
        out_shape=out_shape,
        compiler_params=pltpu.CompilerParams(vmem_limit_bytes=VMEM_LIMIT),
        cost_estimate=pl.CostEstimate(flops=flops, bytes_accessed=moved, transcendentals=0),
    )


def step_block(shape):
    return pl.BlockSpec((1,) + tuple(shape[1:]), lambda s, *_: (s,) + (0,) * (len(shape) - 1))


def part_block(shape, count):
    return pl.BlockSpec((count,) + tuple(shape[1:]), lambda s, *_: (s,) + (0,) * (len(shape) - 1))


def whole(shape):
    return pl.BlockSpec(tuple(shape), lambda s, *_: (0,) * len(shape))


def like(shape):
    return jax.ShapeDtypeStruct(tuple(shape), F32)


def restrict_kernel(parts, pos, owner, agg, r_ref, w_ref, low_ref, own_ref, up_ref, acc):
    s = pl.program_id(0)
    last = pl.num_programs(0) - 1
    blocks_y = r_ref.shape[1]

    @pl.when(s == 0)
    def _():
        acc[...] = jnp.zeros_like(acc)

    for b in range(blocks_y):
        side = owner[s, b] - pos[1] + 1
        slot = agg[s, b] - pos[0] + 1
        acc[side, slot] += w_ref[0, b][None, :] * r_ref[0, b]

    @pl.when(s == last)
    def _():
        rows = acc.shape[2] // parts
        for side, ref in ((0, low_ref), (1, own_ref), (2, up_ref)):
            for part in range(parts):
                ref[part] = acc[side, :, part * rows : (part + 1) * rows]


def put_faces(s, last, row_ref, x_first, x_last, y_first, y_last):
    y_first[0] = row_ref[0, 0]
    y_last[0] = row_ref[0, row_ref.shape[1] - 1]

    @pl.when(s == 0)
    def _():
        x_first[...] = row_ref[0]

    @pl.when(s == last)
    def _():
        x_last[...] = row_ref[0]


def sweep_kernel(r_ref, s_ref, f_ref, x_first, x_last, y_first, y_last):
    s = pl.program_id(0)
    for b in range(r_ref.shape[1]):
        f_ref[0, b] = product(r_ref[0, b], s_ref[0, b])
    put_faces(s, pl.num_programs(0) - 1, f_ref, x_first, x_last, y_first, y_last)


def operator_row(s, v_ref, diag_ref, face_ref, x_low, x_high, y_low, y_high, before, after):
    last = pl.num_programs(0) - 1
    blocks_y = v_ref.shape[1]

    @pl.when(s == 0)
    def _():
        before[...] = x_low[...]

    @pl.when(s > 0)
    def _():
        before[...] = v_ref[jnp.maximum(s - 1, 0)]

    @pl.when(s == last)
    def _():
        after[...] = x_high[...]

    @pl.when(s < last)
    def _():
        after[...] = v_ref[jnp.minimum(s + 1, last)]

    for b in range(blocks_y):
        here = v_ref[s, b]
        left = y_low[0] if b == 0 else v_ref[s, b - 1]
        right = y_high[0] if b == blocks_y - 1 else v_ref[s, b + 1]
        result = product(here, diag_ref[0, b])
        result = result - face_ref[0, b, 0][None, :] * before[b]
        result = result - face_ref[0, b, 1][None, :] * after[b]
        result = result - face_ref[0, b, 2][None, :] * left
        result = result - face_ref[0, b, 3][None, :] * right
        yield b, here, result


def fine_kernel(
    r_ref, s_ref, diag_ref, face_ref, v_ref, x_low, x_high, y_low, y_high, out_ref, before, after
):
    s = pl.program_id(0)
    rows = operator_row(
        s, v_ref, diag_ref, face_ref, x_low, x_high, y_low, y_high, before, after
    )
    for b, here, image in rows:
        out_ref[0, b] = here + product(r_ref[0, b] - image, s_ref[0, b])


def residual_kernel(
    r_ref, diag_ref, face_ref, v_ref, x_low, x_high, y_low, y_high, out_ref, before, after
):
    s = pl.program_id(0)
    rows = operator_row(
        s, v_ref, diag_ref, face_ref, x_low, x_high, y_low, y_high, before, after
    )
    for b, _, image in rows:
        out_ref[0, b] = r_ref[0, b] - image


def coarse_first_kernel(got_ref, smooth_ref, rhs_ref, first_ref):
    s = pl.program_id(0)
    last = pl.num_programs(0) - 1
    count = smooth_ref.shape[0]
    for i in range(count):
        value = got_ref[s, i + 1]
        if i == 0:
            value = value + jnp.where(s > 0, got_ref[jnp.maximum(s - 1, 0), count + 1], 0.0)
        if i == count - 1:
            value = value + jnp.where(s < last, got_ref[jnp.minimum(s + 1, last), 0], 0.0)
        rhs_ref[i] = value
        first_ref[i] = product(value, smooth_ref[i])


def coarse_own_kernel(pos, nbr, rhs_ref, first_ref, diag_ref, weight_ref, out_ref):
    s = pl.program_id(0)
    count = rhs_ref.shape[0]
    total = first_ref.shape[0]
    for i in range(count):
        a = s * count + i
        value = rhs_ref[i] - product(first_ref[a], diag_ref[i])
        for n in range(weight_ref.shape[1]):
            at = nbr[a, n] - pos[1] * total
            mine = (at >= 0) & (at < total)
            at = jnp.clip(at, 0, total - 1)
            value = value + jnp.where(mine, weight_ref[i, n], 0.0)[None, :] * first_ref[at]
        out_ref[i] = value


def coarse_last_kernel(
    pos, nbr, own_ref, first_ref, below_ref, above_ref, smooth_ref, weight_ref, out_ref
):
    s = pl.program_id(0)
    last = pl.num_programs(0) - 1
    count = own_ref.shape[0]
    total = below_ref.shape[0]

    @pl.when(s == 0)
    def _():
        out_ref[0, 0] = jnp.zeros_like(own_ref[0])
        out_ref[last, count + 1] = jnp.zeros_like(own_ref[0])

    for i in range(count):
        a = s * count + i
        value = own_ref[i]
        for n in range(weight_ref.shape[1]):
            at = nbr[a, n] - pos[1] * total
            lower = at < 0
            upper = at >= total
            at_lower = jnp.clip(at + total, 0, total - 1)
            at_upper = jnp.clip(at - total, 0, total - 1)
            weight = weight_ref[i, n]
            value = value + jnp.where(lower, weight, 0.0)[None, :] * below_ref[at_lower]
            value = value + jnp.where(upper, weight, 0.0)[None, :] * above_ref[at_upper]
        value = first_ref[i] + product(value, smooth_ref[i])
        out_ref[s, i + 1] = value
        if i == 0:

            @pl.when(s > 0)
            def _():
                out_ref[jnp.maximum(s - 1, 0), count + 1] = value

        if i == count - 1:

            @pl.when(s < last)
            def _():
                out_ref[jnp.minimum(s + 1, last), 0] = value


def prolong_kernel(
    pos,
    owner,
    agg,
    fine_ref,
    w_ref,
    low_ref,
    own_ref,
    up_ref,
    out_ref,
    x_first,
    x_last,
    y_first,
    y_last,
    table,
):
    s = pl.program_id(0)
    parts, _, rows, _ = own_ref.shape

    @pl.when(s == 0)
    def _():
        for side, ref in ((0, low_ref), (1, own_ref), (2, up_ref)):
            for part in range(parts):
                table[side, :, part * rows : (part + 1) * rows] = ref[part]

    for b in range(fine_ref.shape[1]):
        side = owner[s, b] - pos[1] + 1
        slot = agg[s, b] - pos[0] + 1
        out_ref[0, b] = fine_ref[0, b] + w_ref[0, b][None, :] * table[side, slot]
    put_faces(s, pl.num_programs(0) - 1, out_ref, x_first, x_last, y_first, y_last)


def halo(faces):
    x_first, x_last, y_first, y_last = faces
    y_low = shifted(y_last, "gy", 1)
    y_high = shifted(y_first, "gy", -1)
    x_low = shifted(x_last, "gx", 1)
    x_high = shifted(x_first, "gx", -1)
    return x_low, x_high, y_low, y_high


def body(
    right_side,
    diag_blocks,
    smoother,
    face_weight,
    restrict_weight,
    prolong_weight,
    block_owner,
    block_aggregate,
    coarse_diag,
    coarse_smooth,
    neighbors,
    neighbor_weight,
):
    blocks_x, blocks_y, rows, size = right_side.shape
    total = coarse_diag.shape[0]
    parts = lax.axis_size("gx")
    share = total // parts
    fine_shape = right_side.shape
    mat_shape = diag_blocks.shape
    slab = (parts, share + 2, rows // parts, size)
    coarse_shape = (total, rows // parts, size)
    cmat_shape = coarse_diag.shape
    nw_shape = neighbor_weight.shape
    x_face = (blocks_y, rows, size)
    y_face = (blocks_x, rows, size)
    block_flops = 2 * 4 * rows * size * size
    fine_count = blocks_x * blocks_y
    fine_bytes = fine_count * rows * size * 4
    coarse_flops = total * block_flops // parts
    coarse_bytes = total * size * size * 4

    pos = jnp.stack([lax.axis_index("gx") * share, lax.axis_index("gy")]).astype(jnp.int32)

    low, own, up = call(
        functools.partial(restrict_kernel, parts),
        blocks_x,
        [step_block(fine_shape), step_block(restrict_weight.shape)],
        [whole(slab)] * 3,
        [like(slab)] * 3,
        scalars=3,
        scratch=[pltpu.VMEM((3, share + 2, rows, size), F32)],
        moved=2 * fine_bytes,
    )(pos, block_owner, block_aggregate, right_side, restrict_weight)

    from_above = shifted(low, "gy", -1)
    from_below = shifted(up, "gy", 1)

    face_specs = [whole(x_face), whole(x_face), step_block(y_face), step_block(y_face)]
    face_shapes = [like(x_face), like(x_face), like(y_face), like(y_face)]

    sweep, *faces = call(
        sweep_kernel,
        blocks_x,
        [step_block(fine_shape), step_block(mat_shape)],
        [step_block(fine_shape)] + face_specs,
        [like(fine_shape)] + face_shapes,
        flops=fine_count * block_flops,
        moved=3 * fine_bytes,
    )(right_side, smoother)

    got = lax.all_to_all(own + from_above + from_below, "gx", 0, 0, tiled=True)

    rhs, first = call(
        coarse_first_kernel,
        parts,
        [whole(slab), part_block(cmat_shape, share)],
        [part_block(coarse_shape, share)] * 2,
        [like(coarse_shape)] * 2,
        flops=coarse_flops,
        moved=coarse_bytes,
    )(got, coarse_smooth)

    below = shifted(first, "gy", 1)
    above = shifted(first, "gy", -1)

    inner = call(
        coarse_own_kernel,
        parts,
        [
            part_block(coarse_shape, share),
            whole(coarse_shape),
            part_block(cmat_shape, share),
            part_block(nw_shape, share),
        ],
        part_block(coarse_shape, share),
        like(coarse_shape),
        scalars=2,
        flops=coarse_flops,
        moved=coarse_bytes,
    )(pos, neighbors, rhs, first, coarse_diag, neighbor_weight)

    sweep_halo = halo(faces)
    fine_part = call(
        fine_kernel,
        blocks_x,
        [
            step_block(fine_shape),
            step_block(mat_shape),
            step_block(mat_shape),
            step_block(face_weight.shape),
            whole(fine_shape),
            whole(x_face),
            whole(x_face),
            step_block(y_face),
            step_block(y_face),
        ],
        step_block(fine_shape),
        like(fine_shape),
        scratch=[pltpu.VMEM(x_face, F32)] * 2,
        flops=2 * fine_count * block_flops,
        moved=5 * fine_bytes,
    )(right_side, smoother, diag_blocks, face_weight, sweep, *sweep_halo)

    corr = call(
        coarse_last_kernel,
        parts,
        [
            part_block(coarse_shape, share),
            part_block(coarse_shape, share),
            whole(coarse_shape),
            whole(coarse_shape),
            part_block(cmat_shape, share),
            part_block(nw_shape, share),
        ],
        whole(slab),
        like(slab),
        scalars=2,
        flops=coarse_flops,
        moved=coarse_bytes,
    )(pos, neighbors, inner, first, below, above, coarse_smooth, neighbor_weight)

    mine = lax.all_to_all(corr, "gx", 0, 0, tiled=True)
    lower = shifted(mine, "gy", 1)
    upper = shifted(mine, "gy", -1)

    solved, *faces = call(
        prolong_kernel,
        blocks_x,
        [step_block(fine_shape), step_block(prolong_weight.shape)] + [whole(slab)] * 3,
        [step_block(fine_shape)] + face_specs,
        [like(fine_shape)] + face_shapes,
        scalars=3,
        scratch=[pltpu.VMEM((3, share + 2, rows, size), F32)],
        moved=3 * fine_bytes,
    )(pos, block_owner, block_aggregate, fine_part, prolong_weight, lower, mine, upper)

    solved_halo = halo(faces)
    residual = call(
        residual_kernel,
        blocks_x,
        [
            step_block(fine_shape),
            step_block(mat_shape),
            step_block(face_weight.shape),
            whole(fine_shape),
            whole(x_face),
            whole(x_face),
            step_block(y_face),
            step_block(y_face),
        ],
        step_block(fine_shape),
        like(fine_shape),
        scratch=[pltpu.VMEM(x_face, F32)] * 2,
        flops=fine_count * block_flops,
        moved=4 * fine_bytes,
    )(right_side, diag_blocks, face_weight, solved, *solved_halo)
    return (solved, residual)


def solution(mesh):
    return jax.shard_map(
        body,
        mesh=mesh,
        in_specs=(
            P("gx", "gy", None, None),
            P("gx", "gy", None, None),
            P("gx", "gy", None, None),
            P("gx", "gy", None, None),
            P("gx", "gy", None),
            P("gx", "gy", None),
            P("gx", "gy"),
            P("gx", "gy"),
            P("gy", None, None),
            P("gy", None, None),
            P("gy", None),
            P("gy", None, None),
        ),
        out_specs=(P("gx", "gy", None, None), P("gx", "gy", None, None)),
        check_vma=False,
    )
```

time: 463 us -> 222 us (0.48)
  waiting for transfers between devices: 215 us -> 83 us
  matrix products: 100 us -> 0 us
  Pallas kernels: 0 us -> 43.5 us
  other arithmetic: 31.9 us -> 0.28 us
  local copies, waits for them, and re-layouts: 48.1 us -> 20.1 us
  blocking collectives: 0 us -> 17.1 us
  between operations: 14.7 us -> 0.92 us
  starting transfers between devices: 47.6 us -> 53 us
    dot_general x8 -> x0, matrix products: 100 us -> none  [the longest x7 96.3 us: apply_blocks(): return jnp.einsum('...ij,...kj->...ki', matrices, vector, precision=HIGHEST)]
    ppermute x16 -> x14, waiting for transfers between devices: 170 us -> 79.6 us  [shifted(): return lax.ppermute(array, axis, pairs)]
    psum x1 -> x0, waiting for transfers between devices: 44.4 us -> none  [body(): coarse_rhs = lax.psum(partial_value, 'gx')]
    pallas_call x0 -> x8, Pallas kernels: none -> 43.5 us  [the longest x1 11.6 us: body(): call(fine_kernel, blocks_x, [step_block(fine_shape), step_block(mat_shape...]
    gather x8 -> x0, local copies, waits for them, and re-layouts: 31.5 us -> none  [the longest x1 13.7 us: coarse_cycle(): gathered = jnp.take(window, offsets.reshape(-1), axis=0)]
    all_to_all x0 -> x1, blocking collectives: none -> 17.1 us  [body(): got = lax.all_to_all(own + from_above + from_below, 'gx', 0, 0, tiled=True)]
    concatenate x3 -> x0, other arithmetic: 9.86 us -> none  [the longest x1 6.24 us: extended(): block = jnp.concatenate([low, block, high], axis=dim)]
    unnamed x34 -> x58, local copies, waits for them, and re-layouts: 10.3 us -> 20.1 us
  transfers between devices with their start and end apart: 17 -> 15, of which waited for: 12 -> 7; matrix products, arithmetic and copies ran while one was open for 22% -> 0% of each run, Pallas kernels for 0% -> 12%
where the time goes in v1:
time: 222 us; the launch traced here: 218 us
  waiting for transfers between devices  83 us (37%)
  starting transfers between devices  53 us (24%)
  Pallas kernels  43.5 us (20%)
  local copies, waits for them, and re-layouts  20.1 us (9%)
  blocking collectives  17.1 us (8%)
    ppermute x14, waiting for transfers between devices, shifted(): return lax.ppermute(array, axis, pairs)  79.6 us
    ppermute x14, starting transfers between devices, shifted(): return lax.ppermute(array, axis, pairs)  49 us
    unnamed x58, local copies, waits for them, and re-layouts  20.1 us
    all_to_all x1, blocking collectives, body(): got = lax.all_to_all(own + from_above + from_below, 'gx', 0, 0, tiled=True)  17.1 us
    pallas_call x1, Pallas kernels, body(): call(fine_kernel, blocks_x, [step_block(fine_shape), step_block(mat_shape...  11.6 us
    pallas_call x1, Pallas kernels, body(): call(residual_kernel, blocks_x, [step_block(fine_shape), step_block(mat_s...  8.64 us
    pallas_call x1, Pallas kernels, body(): call(sweep_kernel, blocks_x, [step_block(fine_shape), step_block(mat_shap...  7.63 us
    pallas_call x1, Pallas kernels, body(): call(coarse_last_kernel, parts, [part_block(coarse_shape, share), part_bl...  5.33 us
  transfers between devices with their start and end apart: 15, of which 7 were waited for; matrix products, arithmetic and copies ran while one was open for 0% of the time, Pallas kernels for 12%

profile of v1, /device:TPU:1, one launch (start us, length us, event | category | flops | bytes accessed | tf_op | source)
XLA Modules:
  0.0 218.0 jit_solution(12935406560620789059)
XLA Ops:
  0.7 2.2 %copy-done = f32[8,8,128,128]{3,2,1,0:T(8,128)S(1)} copy-done((f32[8,8,128,128]{3,2,1,0:T(8,128)S(1)}, f32[8,8,128,128]{3,2,1,0:T(8,128)}, u32[]{:S(2)}) %copy-start) | copy-done | bytes 4194328
  8.2 4.7 %collective-permute-start.5 = (f32[4,10,32,128]{3,2,1,0:T(8,128)S(1)}, f32[4,10,32,128]{3,2,1,0:T(8,128)S(1)}, u32[]{:S(2)}, u32[]{:S(2)}) collective-permute-start(f32[4,10,32,128]{3,2,1,0:T(8,128)S(1)} %get-tuple-element.24), channel_id=1, source_target_pairs={{0,1},{1,2},{2,3},{3,4},{4,5},{5,6},{6,7},{7,8},{8,9},{9,10},{10,1... | collective-permute-start | bytes 1966088 | tf_op jit(solution)/shard_map/ppermute | solution.py:18
  12.9 12.1 %collective-permute-done.4 = f32[4,10,32,128]{3,2,1,0:T(8,128)S(1)} collective-permute-done((f32[4,10,32,128]{3,2,1,0:T(8,128)S(1)}, f32[4,10,32,128]{3,2,1,0:T(8,128)S(1)}, u32[]{:S(2)}, u32[]{:S(2)}) %collective-permute-start.4) | collective-permute-done | bytes 655392 | tf_op jit(solution)/shard_map/ppermute | solution.py:18
  25.0 14.9 %collective-permute-done.5 = f32[4,10,32,128]{3,2,1,0:T(8,128)S(1)} collective-permute-done((f32[4,10,32,128]{3,2,1,0:T(8,128)S(1)}, f32[4,10,32,128]{3,2,1,0:T(8,128)S(1)}, u32[]{:S(2)}, u32[]{:S(2)}) %collective-permute-start.5) | collective-permute-done | bytes 655392 | tf_op jit(solution)/shard_map/ppermute | solution.py:18
  40.1 17.1 %all_to_all.10.got_ref = f32[4,10,32,128]{3,2,1,0:T(8,128)S(1)} all-to-all(f32[4,10,32,128]{3,2,1,0:T(8,128)S(1)} %add_add_fusion), channel_id=1, replica_groups=mesh['gx'=4,'gy'=32] {'gx'}, dimensions={0} | all-to-all | bytes 1310720 | tf_op jit(solution)/shard_map/all_to_all | solution.py:342
  61.1 5.0 %collective-permute-start.6 = (f32[32,32,128]{2,1,0:T(8,128)S(1)}, f32[32,32,128]{2,1,0:T(8,128)}, u32[]{:S(2)}, u32[]{:S(2)}) collective-permute-start(f32[32,32,128]{2,1,0:T(8,128)S(1)} %get-tuple-element.26.first_ref), channel_id=1, source_target_pairs={{0,1},{1,2},{2,3},{3,4},{4,5},{5,6},{6,7},{7,8},{8,9},{9,10},{10,1... | collective-permute-start | bytes 1572872 | tf_op jit(solution)/shard_map/ppermute | solution.py:18
  66.0 7.6 %shard_map.131 = (f32[8,8,128,128]{3,2,1,0:T(8,128)S(1)}, f32[8,128,128]{2,1,0:T(8,128)S(1)}, f32[8,128,128]{2,1,0:T(8,128)}, f32[8,128,128]{2,1,0:T(8,128)S(1)}, f32[8,128,128]{2,1,0:T(8,128)S(1)}) custom-call(f32[8,8,128,128]{3,2,1,0:T(8,128)S(1)} %copy-done.1, f32[8,8,128,128]{3,2,1,0:T(8,128)} %s_ref.3), custom_call_target="tpu_custom_call" | custom-call | flops 1073741824 | bytes 12582912 | tf_op jit(solution)/shard_map/pallas_call | solution.py:332
  73.7 2.0 copy-done.6
  78.1 3.8 %collective-permute-start = (f32[8,128,128]{2,1,0:T(8,128)}, f32[8,128,128]{2,1,0:T(8,128)S(1)}, u32[]{:S(2)}, u32[]{:S(2)}) collective-permute-start(f32[8,128,128]{2,1,0:T(8,128)} %get-tuple-element.18), channel_id=1, source_target_pairs={{0,32},{32,64},{64,96},{1,33},{33,65},{65,97},{2,34},{34,66},{66,9... | collective-permute-start | bytes 1572872 | tf_op jit(solution)/shard_map/ppermute | solution.py:18
  84.7 2.6 %shard_map.135.own_ref = f32[32,32,128]{2,1,0:T(8,128)S(1)} custom-call(s32[2]{0:T(128)S(1)} %pad_add_fusion.pos, s32[32,6]{1,0:T(8,128)S(1)} %copy.16.nbr, f32[32,32,128]{2,1,0:T(8,128)S(1)} %copy-done.16, f32[32,32,128]{2,1,0:T(8,128)S(1)} %get-tuple-element.26.first_ref, f32[32,128,128]{2,1,0:T(8,128)S(1)} %copy-done.7, f32[32,6,128]{2,1,0:T(8,128)S(1)} %copy.15.weight_ref), custom_call_target="tpu_custom_call" | custom-call | flops 134217728 | bytes 2097152 | tf_op jit(solution)/shard_map/pallas_call | solution.py:357
  88.0 5.3 %shard_map.136 = f32[4,10,32,128]{3,2,1,0:T(8,128)} custom-call(s32[2]{0:T(128)S(1)} %pad_add_fusion.pos, s32[32,6]{1,0:T(8,128)S(1)} %copy.16.nbr, f32[32,32,128]{2,1,0:T(8,128)S(1)} %shard_map.135.own_ref, f32[32,32,128]{2,1,0:T(8,128)S(1)} %get-tuple-element.26.first_ref, f32[32,32,128]{2,1,0:T(8,128)} %collective-permute-done.6.below_ref, ...), custom_call_target="tpu_custom_call" | custom-call | flops 134217728 | bytes 2097152 | tf_op jit(solution)/shard_map/pallas_call | solution.py:395
  93.3 4.0 %all-to-all-start.1 = ((f32[4,10,32,128]{3,2,1,0:T(8,128)}), f32[4,10,32,128]{3,2,1,0:T(8,128)S(1)}, u32[]{:S(2)}, u32[]{:S(2)}) async-start(f32[4,10,32,128]{3,2,1,0:T(8,128)} %shard_map.136), calls=%async_computation.1 | async-start | bytes 1310720 | tf_op jit(solution)/shard_map/all_to_all | solution.py:413
  99.3 4.2 %collective-permute-start.2 = (f32[8,128,128]{2,1,0:T(8,128)}, f32[8,128,128]{2,1,0:T(8,128)S(1)}, u32[]{:S(2)}, u32[]{:S(2)}) collective-permute-start(f32[8,128,128]{2,1,0:T(8,128)} %copy-done.24), channel_id=1, source_target_pairs={{0,1},{1,2},{2,3},{3,4},{4,5},{5,6},{6,7},{7,8},{8,9},{9,10},{10,1... | collective-permute-start | bytes 1572872 | tf_op jit(solution)/shard_map/ppermute | solution.py:18
  104.9 3.4 %all-to-all-done.1.own_ref = f32[4,10,32,128]{3,2,1,0:T(8,128)S(1)} async-done(((f32[4,10,32,128]{3,2,1,0:T(8,128)}), f32[4,10,32,128]{3,2,1,0:T(8,128)S(1)}, u32[]{:S(2)}, u32[]{:S(2)}) %all-to-all-start.1) | async-done | bytes 655392 | tf_op jit(solution)/shard_map/all_to_all | solution.py:413
  109.6 4.9 %collective-permute-start.8 = (f32[4,10,32,128]{3,2,1,0:T(8,128)S(1)}, f32[4,10,32,128]{3,2,1,0:T(8,128)S(1)}, u32[]{:S(2)}, u32[]{:S(2)}) collective-permute-start(f32[4,10,32,128]{3,2,1,0:T(8,128)S(1)} %all-to-all-done.1.own_ref), channel_id=1, source_target_pairs={{0,1},{1,2},{2,3},{3,4},{4,5},{5,6},{6,7},{7,8},{8,9},{9,10},{10,1... | collective-permute-start | bytes 1966088 | tf_op jit(solution)/shard_map/ppermute | solution.py:18
  114.4 30.4 %collective-permute-done.1.x_high = f32[8,128,128]{2,1,0:T(8,128)S(1)} collective-permute-done((f32[8,128,128]{2,1,0:T(8,128)}, f32[8,128,128]{2,1,0:T(8,128)S(1)}, u32[]{:S(2)}, u32[]{:S(2)}) %collective-permute-start.1) | collective-permute-done | bytes 524320 | tf_op jit(solution)/shard_map/ppermute | solution.py:18
  147.2 2.2 %copy-done.2 = f32[8,8,128,128]{3,2,1,0:T(8,128)S(1)} copy-done((f32[8,8,128,128]{3,2,1,0:T(8,128)S(1)}, f32[8,8,128,128]{3,2,1,0:T(8,128)}, u32[]{:S(2)}) %copy-start.2) | copy-done | bytes 4194328
  152.5 11.6 %shard_map.132.fine_ref = f32[8,8,128,128]{3,2,1,0:T(8,128)S(1)} custom-call(f32[8,8,128,128]{3,2,1,0:T(8,128)S(1)} %copy-done.2, f32[8,8,128,128]{3,2,1,0:T(8,128)} %s_ref.3, f32[8,8,128,128]{3,2,1,0:T(8,128)} %diag_ref.5, f32[8,8,4,128]{3,2,1,0:T(4,128)S(1)} %copy-done.8, f32[8,8,128,128]{3,2,1,0:T(8,128)} %copy-done.6, ...), custom_call_target="tpu_custom_call" | custom-call | flops 2147483648 | bytes 20971520 | tf_op jit(solution)/shard_map/pallas_call | solution.py:374
  164.2 4.5 %shard_map.137 = (f32[8,8,128,128]{3,2,1,0:T(8,128)}, f32[8,128,128]{2,1,0:T(8,128)S(1)}, f32[8,128,128]{2,1,0:T(8,128)S(1)}, f32[8,128,128]{2,1,0:T(8,128)S(1)}, f32[8,128,128]{2,1,0:T(8,128)S(1)}) custom-call(s32[2]{0:T(128)S(1)} %pad_add_fusion.pos, s32[8,8]{1,0:T(8,128)S(1)} %copy-done.20, s32[8,8]{1,0:T(8,128)S(1)} %copy-done.22, ...), custom_call_target="tpu_custom_call" | custom-call | bytes 12582912 | tf_op jit(solution)/shard_map/pallas_call | solution.py:417
  168.7 12.3 %collective-permute-start.10 = (f32[8,128,128]{2,1,0:T(8,128)S(1)}, f32[8,128,128]{2,1,0:T(8,128)S(1)}, u32[]{:S(2)}, u32[]{:S(2)}) collective-permute-start(f32[8,128,128]{2,1,0:T(8,128)S(1)} %get-tuple-element.28), channel_id=1, source_target_pairs={{0,32},{32,64},{64,96},{1,33},{33,65},{65,97},{2,34},{34,66},{66,9... | collective-permute-start | bytes 1572872 | tf_op jit(solution)/shard_map/ppermute | solution.py:18
  182.9 3.4 %collective-permute-start.12 = (f32[8,128,128]{2,1,0:T(8,128)S(1)}, f32[8,128,128]{2,1,0:T(8,128)S(1)}, u32[]{:S(2)}, u32[]{:S(2)}) collective-permute-start(f32[8,128,128]{2,1,0:T(8,128)S(1)} %get-tuple-element.30), channel_id=1, source_target_pairs={{0,1},{1,2},{2,3},{3,4},{4,5},{5,6},{6,7},{7,8},{8,9},{9,10},{10,1... | collective-permute-start | bytes 1572872 | tf_op jit(solution)/shard_map/ppermute | solution.py:18
  187.7 3.4 %collective-permute-done.10.x_low = f32[8,128,128]{2,1,0:T(8,128)S(1)} collective-permute-done((f32[8,128,128]{2,1,0:T(8,128)S(1)}, f32[8,128,128]{2,1,0:T(8,128)S(1)}, u32[]{:S(2)}, u32[]{:S(2)}) %collective-permute-start.10) | collective-permute-done | bytes 524320 | tf_op jit(solution)/shard_map/ppermute | solution.py:18
  191.1 18.2 %collective-permute-done.11.x_high = f32[8,128,128]{2,1,0:T(8,128)S(1)} collective-permute-done((f32[8,128,128]{2,1,0:T(8,128)S(1)}, f32[8,128,128]{2,1,0:T(8,128)S(1)}, u32[]{:S(2)}, u32[]{:S(2)}) %collective-permute-start.11) | collective-permute-done | bytes 524320 | tf_op jit(solution)/shard_map/ppermute | solution.py:18
  209.3 8.6 %shard_map.138 = f32[8,8,128,128]{3,2,1,0:T(8,128)} custom-call(f32[8,8,128,128]{3,2,1,0:T(8,128)S(1)} %copy-done.3, f32[8,8,128,128]{3,2,1,0:T(8,128)S(1)} %copy-done.4, f32[8,8,4,128]{3,2,1,0:T(4,128)S(1)} %copy-done.8, f32[8,8,128,128]{3,2,1,0:T(8,128)} %get-tuple-element.15.v_ref, f32[8,128,128]{2,1,0:T(8,128)S(1)} %collective-permute-done.10.x_low, ...), custom_call_target="tpu_custom_call" | custom-call | flops 1073741824 | bytes 16777216 | tf_op jit(solution)/shard_map/pallas_call | solution.py:429
  (75 shorter events, 28.6 us)
Async XLA Ops:
  5.0 52.1 %copy-start.5 = (f32[32,128,128]{2,1,0:T(8,128)S(1)}, f32[32,128,128]{2,1,0:T(8,128)}, u32[]{:S(2)}) copy-start(f32[32,128,128]{2,1,0:T(8,128)} %smooth_ref.3) | copy-start | bytes 6291460
  6.6 59.4 %copy-start.1 = (f32[8,8,128,128]{3,2,1,0:T(8,128)S(1)}, f32[8,8,128,128]{3,2,1,0:T(8,128)}, u32[]{:S(2)}) copy-start(f32[8,8,128,128]{3,2,1,0:T(8,128)} %r_ref.7) | copy-start | bytes 12582916
  6.6 18.3 %collective-permute-start.4 = (f32[4,10,32,128]{3,2,1,0:T(8,128)S(1)}, f32[4,10,32,128]{3,2,1,0:T(8,128)S(1)}, u32[]{:S(2)}, u32[]{:S(2)}) collective-permute-start(f32[4,10,32,128]{3,2,1,0:T(8,128)S(1)} %get-tuple-element.23), channel_id=1, source_target_pairs={{1,0},{2,1},{3,2},{4,3},{5,4},{6,5},{7,6},{8,7},{9,8},{10,9},{11,1... | collective-permute-start | bytes 1966088 | tf_op jit(solution)/shard_map/ppermute | solution.py:18
  8.2 31.7 %collective-permute-start.5 = (f32[4,10,32,128]{3,2,1,0:T(8,128)S(1)}, f32[4,10,32,128]{3,2,1,0:T(8,128)S(1)}, u32[]{:S(2)}, u32[]{:S(2)}) collective-permute-start(f32[4,10,32,128]{3,2,1,0:T(8,128)S(1)} %get-tuple-element.24), channel_id=1, source_target_pairs={{0,1},{1,2},{2,3},{3,4},{4,5},{5,6},{6,7},{7,8},{8,9},{9,10},{10,1... | collective-permute-start | bytes 1966088 | tf_op jit(solution)/shard_map/ppermute | solution.py:18
  59.7 22.2 %copy-start.27 = (s32[32,6]{0,1:T(8,128)S(1)}, s32[32,6]{0,1:T(8,128)}, u32[]{:S(2)}) copy-start(s32[32,6]{0,1:T(8,128)} %param.22) | copy-start | bytes 2308
  59.7 22.3 %copy-start.26 = (f32[32,6,128]{2,0,1:T(8,128)S(1)}, f32[32,6,128]{2,0,1:T(8,128)}, u32[]{:S(2)}) copy-start(f32[32,6,128]{2,0,1:T(8,128)} %param.23) | copy-start | bytes 294916
  59.7 27.7 %collective-permute-start.7 = (f32[32,32,128]{2,1,0:T(8,128)S(1)}, f32[32,32,128]{2,1,0:T(8,128)}, u32[]{:S(2)}, u32[]{:S(2)}) collective-permute-start(f32[32,32,128]{2,1,0:T(8,128)S(1)} %get-tuple-element.26.first_ref), channel_id=1, source_target_pairs={{1,0},{2,1},{3,2},{4,3},{5,4},{6,5},{7,6},{8,7},{9,8},{10,9},{11,1... | collective-permute-start | bytes 1572872 | tf_op jit(solution)/shard_map/ppermute | solution.py:18
  61.1 26.9 %collective-permute-start.6 = (f32[32,32,128]{2,1,0:T(8,128)S(1)}, f32[32,32,128]{2,1,0:T(8,128)}, u32[]{:S(2)}, u32[]{:S(2)}) collective-permute-start(f32[32,32,128]{2,1,0:T(8,128)S(1)} %get-tuple-element.26.first_ref), channel_id=1, source_target_pairs={{0,1},{1,2},{2,3},{3,4},{4,5},{5,6},{6,7},{7,8},{8,9},{9,10},{10,1... | collective-permute-start | bytes 1572872 | tf_op jit(solution)/shard_map/ppermute | solution.py:18
  78.1 31.5 %collective-permute-start = (f32[8,128,128]{2,1,0:T(8,128)}, f32[8,128,128]{2,1,0:T(8,128)S(1)}, u32[]{:S(2)}, u32[]{:S(2)}) collective-permute-start(f32[8,128,128]{2,1,0:T(8,128)} %get-tuple-element.18), channel_id=1, source_target_pairs={{0,32},{32,64},{64,96},{1,33},{33,65},{65,97},{2,34},{34,66},{66,9... | collective-permute-start | bytes 1572872 | tf_op jit(solution)/shard_map/ppermute | solution.py:18
  84.7 62.5 %copy-start.8 = (f32[8,8,4,128]{3,2,1,0:T(4,128)S(1)}, f32[8,8,4,128]{3,2,1,0:T(4,128)}, u32[]{:S(2)}) copy-start(f32[8,8,4,128]{3,2,1,0:T(4,128)} %face_ref.3) | copy-start | bytes 393220
  93.3 14.9 %all-to-all-start.1 = ((f32[4,10,32,128]{3,2,1,0:T(8,128)}), f32[4,10,32,128]{3,2,1,0:T(8,128)S(1)}, u32[]{:S(2)}, u32[]{:S(2)}) async-start(f32[4,10,32,128]{3,2,1,0:T(8,128)} %shard_map.136), calls=%async_computation.1 | async-start | bytes 1310720 | tf_op jit(solution)/shard_map/all_to_all | solution.py:413
  97.4 47.4 %collective-permute-start.1 = (f32[8,128,128]{2,1,0:T(8,128)}, f32[8,128,128]{2,1,0:T(8,128)S(1)}, u32[]{:S(2)}, u32[]{:S(2)}) collective-permute-start(f32[8,128,128]{2,1,0:T(8,128)} %copy-done.25), channel_id=1, source_target_pairs={{32,0},{64,32},{96,64},{33,1},{65,33},{97,65},{34,2},{66,34},{98,6... | collective-permute-start | bytes 1572872 | tf_op jit(solution)/shard_map/ppermute | solution.py:18
  99.3 46.3 %collective-permute-start.2 = (f32[8,128,128]{2,1,0:T(8,128)}, f32[8,128,128]{2,1,0:T(8,128)S(1)}, u32[]{:S(2)}, u32[]{:S(2)}) collective-permute-start(f32[8,128,128]{2,1,0:T(8,128)} %copy-done.24), channel_id=1, source_target_pairs={{0,1},{1,2},{2,3},{3,4},{4,5},{5,6},{6,7},{7,8},{8,9},{9,10},{10,1... | collective-permute-start | bytes 1572872 | tf_op jit(solution)/shard_map/ppermute | solution.py:18
  103.6 42.8 %collective-permute-start.3 = (f32[8,128,128]{2,1,0:T(8,128)}, f32[8,128,128]{2,1,0:T(8,128)S(1)}, u32[]{:S(2)}, u32[]{:S(2)}) collective-permute-start(f32[8,128,128]{2,1,0:T(8,128)} %copy-done.23), channel_id=1, source_target_pairs={{1,0},{2,1},{3,2},{4,3},{5,4},{6,5},{7,6},{8,7},{9,8},{10,9},{11,1... | collective-permute-start | bytes 1572872 | tf_op jit(solution)/shard_map/ppermute | solution.py:18
  108.3 55.9 %collective-permute-start.9 = (f32[4,10,32,128]{3,2,1,0:T(8,128)S(1)}, f32[4,10,32,128]{3,2,1,0:T(8,128)S(1)}, u32[]{:S(2)}, u32[]{:S(2)}) collective-permute-start(f32[4,10,32,128]{3,2,1,0:T(8,128)S(1)} %all-to-all-done.1.own_ref), channel_id=1, source_target_pairs={{1,0},{2,1},{3,2},{4,3},{5,4},{6,5},{7,6},{8,7},{9,8},{10,9},{11,1... | collective-permute-start | bytes 1966088 | tf_op jit(solution)/shard_map/ppermute | solution.py:18
  109.6 54.6 %collective-permute-start.8 = (f32[4,10,32,128]{3,2,1,0:T(8,128)S(1)}, f32[4,10,32,128]{3,2,1,0:T(8,128)S(1)}, u32[]{:S(2)}, u32[]{:S(2)}) collective-permute-start(f32[4,10,32,128]{3,2,1,0:T(8,128)S(1)} %all-to-all-done.1.own_ref), channel_id=1, source_target_pairs={{0,1},{1,2},{2,3},{3,4},{4,5},{5,6},{6,7},{7,8},{8,9},{9,10},{10,1... | collective-permute-start | bytes 1966088 | tf_op jit(solution)/shard_map/ppermute | solution.py:18
  152.5 11.6 %copy-start.20 = (s32[8,8]{1,0:T(8,128)S(1)}, s32[8,8]{1,0:T(8,128)}, u32[]{:S(2)}) copy-start(s32[8,8]{1,0:T(8,128)} %owner.3) | copy-start | bytes 772
  152.5 11.6 %copy-start.22 = (s32[8,8]{1,0:T(8,128)S(1)}, s32[8,8]{1,0:T(8,128)}, u32[]{:S(2)}) copy-start(s32[8,8]{1,0:T(8,128)} %agg.3) | copy-start | bytes 772
  152.5 56.8 %copy-start.4 = (f32[8,8,128,128]{3,2,1,0:T(8,128)S(1)}, f32[8,8,128,128]{3,2,1,0:T(8,128)}, u32[]{:S(2)}) copy-start(f32[8,8,128,128]{3,2,1,0:T(8,128)} %diag_ref.5) | copy-start | bytes 12582916
  164.1 45.2 %copy-start.3 = (f32[8,8,128,128]{3,2,1,0:T(8,128)S(1)}, f32[8,8,128,128]{3,2,1,0:T(8,128)}, u32[]{:S(2)}) copy-start(f32[8,8,128,128]{3,2,1,0:T(8,128)} %r_ref.7) | copy-start | bytes 12582916
  168.7 22.3 %collective-permute-start.10 = (f32[8,128,128]{2,1,0:T(8,128)S(1)}, f32[8,128,128]{2,1,0:T(8,128)S(1)}, u32[]{:S(2)}, u32[]{:S(2)}) collective-permute-start(f32[8,128,128]{2,1,0:T(8,128)S(1)} %get-tuple-element.28), channel_id=1, source_target_pairs={{0,32},{32,64},{64,96},{1,33},{33,65},{65,97},{2,34},{34,66},{66,9... | collective-permute-start | bytes 1572872 | tf_op jit(solution)/shard_map/ppermute | solution.py:18
  181.0 28.3 %collective-permute-start.11 = (f32[8,128,128]{2,1,0:T(8,128)S(1)}, f32[8,128,128]{2,1,0:T(8,128)S(1)}, u32[]{:S(2)}, u32[]{:S(2)}) collective-permute-start(f32[8,128,128]{2,1,0:T(8,128)S(1)} %get-tuple-element.29), channel_id=1, source_target_pairs={{32,0},{64,32},{96,64},{33,1},{65,33},{97,65},{34,2},{66,34},{98,6... | collective-permute-start | bytes 1572872 | tf_op jit(solution)/shard_map/ppermute | solution.py:18
  182.9 26.4 %collective-permute-start.12 = (f32[8,128,128]{2,1,0:T(8,128)S(1)}, f32[8,128,128]{2,1,0:T(8,128)S(1)}, u32[]{:S(2)}, u32[]{:S(2)}) collective-permute-start(f32[8,128,128]{2,1,0:T(8,128)S(1)} %get-tuple-element.30), channel_id=1, source_target_pairs={{0,1},{1,2},{2,3},{3,4},{4,5},{5,6},{6,7},{7,8},{8,9},{9,10},{10,1... | collective-permute-start | bytes 1572872 | tf_op jit(solution)/shard_map/ppermute | solution.py:18
  186.4 22.9 %collective-permute-start.13 = (f32[8,128,128]{2,1,0:T(8,128)S(1)}, f32[8,128,128]{2,1,0:T(8,128)S(1)}, u32[]{:S(2)}, u32[]{:S(2)}) collective-permute-start(f32[8,128,128]{2,1,0:T(8,128)S(1)} %get-tuple-element.31), channel_id=1, source_target_pairs={{1,0},{2,1},{3,2},{4,3},{5,4},{6,5},{7,6},{8,7},{9,8},{10,9},{11,1... | collective-permute-start | bytes 1572872 | tf_op jit(solution)/shard_map/ppermute | solution.py:18
  (19 other events, 31.5 us)

commit v2 on v0

v2 whole, which is shorter than its diff:
```python
import functools

import jax
import jax.numpy as jnp
from jax import lax
from jax.experimental import pallas as pl
from jax.experimental.pallas import tpu as pltpu
from jax.sharding import PartitionSpec as P

F32 = jnp.float32
BF16 = jnp.bfloat16


def moved_to(array, target):
    count_x, count_y = lax.axis_size("gx"), lax.axis_size("gy")
    pairs = []
    for x in range(count_x):
        for y in range(count_y):
            to_x, to_y = target(x, y)
            if 0 <= to_x < count_x and 0 <= to_y < count_y:
                pairs.append((x * count_y + y, to_x * count_y + to_y))
    return lax.ppermute(array, ("gx", "gy"), pairs)


def straight(array, by):
    return moved_to(array, lambda x, y: (x, y + by))


def in_pair(array):
    return moved_to(array, lambda x, y: (x, y ^ 1))


def between_pairs(array):
    return moved_to(array, lambda x, y: (x ^ 2, ((y + 1) ^ 1) - 1))


def quarter(flip, device):
    return jnp.where(flip == 1, device ^ 2, device)


def halves(x):
    high = x.astype(BF16)
    low = (x - high.astype(F32)).astype(BF16)
    return high, low


def product(vector, matrix):
    vector_high, vector_low = halves(vector)
    matrix_high, matrix_low = halves(matrix)
    left = jnp.concatenate([vector_high, vector_low], axis=1)
    right = jnp.concatenate(
        [
            jnp.concatenate([matrix_high, matrix_high], axis=1),
            jnp.concatenate([matrix_low, matrix_low], axis=1),
        ],
        axis=0,
    )
    both = lax.dot_general(left, right, (((1,), (1,)), ((), ())), preferred_element_type=F32)
    width = matrix.shape[0]
    return both[:, :width] + both[:, width:]


def call(kernel, grid, in_specs, out_specs, out_shape, scalars=0, scratch=(), flops=0, moved=0, aliases=None, limit=48):
    return pl.pallas_call(
        kernel,
        grid_spec=pltpu.PrefetchScalarGridSpec(
            num_scalar_prefetch=scalars,
            grid=(grid,),
            in_specs=in_specs,
            out_specs=out_specs,
            scratch_shapes=list(scratch),
        ),
        out_shape=out_shape,
        input_output_aliases=aliases or {},
        compiler_params=pltpu.CompilerParams(vmem_limit_bytes=limit * 1024 * 1024),
        cost_estimate=pl.CostEstimate(flops=40 * flops, bytes_accessed=40 * moved, transcendentals=0),
    )


def part_block(shape, count):
    return pl.BlockSpec((count,) + tuple(shape[1:]), lambda s, *_: (s,) + (0,) * (len(shape) - 1))


def whole(shape):
    return pl.BlockSpec(tuple(shape), lambda s, *_: (0,) * len(shape))


def like(shape):
    return jax.ShapeDtypeStruct(tuple(shape), F32)


def started(ref, buffer, sems, chunks):
    count = buffer.shape[0] // chunks
    copies = []
    for k in range(chunks):
        part = pl.ds(k * count, count)
        copies.append(pltpu.make_async_copy(ref.at[part], buffer.at[part], sems.at[k]))
        copies[-1].start()
    return copies


def restrict_kernel(pos, owner, agg, r_ref, w_ref, pair_ref, own_ref, next_ref, acc, buffer, sems):
    blocks_x, blocks_y = buffer.shape[:2]
    copies = started(r_ref, buffer, sems, blocks_x)
    acc[...] = jnp.zeros_like(acc)
    for p in range(blocks_x):
        copies[p].wait()
        for b in range(blocks_y):
            side = owner[p, b] - pos[1] + 1
            slot = agg[p, b] - pos[0] + 1
            acc[side, slot] += w_ref[p, b][None, :] * buffer[p, b]
    parts, _, rows, _ = own_ref.shape
    for side, flip, ref in (
        (pos[4], pos[3], pair_ref),
        (1, pos[3], own_ref),
        (2 - pos[4], 1 - pos[3], next_ref),
    ):
        for part in range(parts):
            at = pl.multiple_of(quarter(flip, part) * rows, rows)
            ref[part] = acc[side, :, pl.ds(at, rows)]


def put_faces(s, last, core, row_ref, inner, outer, y_first, y_last):
    per, blocks_y = row_ref.shape[:2]
    for t in range(per):
        y_first[t] = row_ref[t, 0]
        y_last[t] = row_ref[t, blocks_y - 1]

    for end, row, lower in ((0, 0, 1), (last, per - 1, 0)):

        @pl.when((s == end) & (core == lower))
        def _():
            inner[...] = row_ref[row]

        @pl.when((s == end) & (core == 1 - lower))
        def _():
            outer[...] = row_ref[row]


def sweep_kernel(pos, r_ref, s_ref, f_ref, inner, outer, y_first, y_last):
    s = pl.program_id(0)
    per, blocks_y = r_ref.shape[:2]
    for t in range(per):
        for b in range(blocks_y):
            f_ref[t, b] = product(r_ref[t, b], s_ref[t, b])
    put_faces(s, pl.num_programs(0) - 1, pos[2], f_ref, inner, outer, y_first, y_last)


def neighbours_off(result, face, before, after, left, right):
    result = result - face[0][None, :] * before
    result = result - face[1][None, :] * after
    result = result - face[2][None, :] * left
    return result - face[3][None, :] * right


def fine_kernel(
    pos,
    r_ref,
    s_ref,
    diag_ref,
    face_ref,
    v_ref,
    x_inner,
    x_outer,
    y_low,
    y_high,
    out_ref,
    before,
    after,
):
    s = pl.program_id(0)
    last = pl.num_programs(0) - 1
    per, blocks_y = r_ref.shape[:2]

    @pl.when((s == 0) & (pos[2] == 0))
    def _():
        before[...] = x_outer[...]

    @pl.when((s == 0) & (pos[2] == 1))
    def _():
        before[...] = x_inner[...]

    @pl.when(s > 0)
    def _():
        before[...] = v_ref[jnp.maximum(s * per - 1, 0)]

    @pl.when((s == last) & (pos[2] == 0))
    def _():
        after[...] = x_inner[...]

    @pl.when((s == last) & (pos[2] == 1))
    def _():
        after[...] = x_outer[...]

    @pl.when(s < last)
    def _():
        after[...] = v_ref[jnp.minimum((s + 1) * per, v_ref.shape[0] - 1)]

    for t in range(per):
        p = s * per + t
        for b in range(blocks_y):
            here = v_ref[p, b]
            image = neighbours_off(
                product(here, diag_ref[t, b]),
                face_ref[t, b],
                before[b] if t == 0 else v_ref[p - 1, b],
                after[b] if t == per - 1 else v_ref[p + 1, b],
                y_low[t] if b == 0 else v_ref[p, b - 1],
                y_high[t] if b == blocks_y - 1 else v_ref[p, b + 1],
            )
            out_ref[t, b] = here + product(r_ref[t, b] - image, s_ref[t, b])


def coarse_first_kernel(got_ref, smooth_ref, rhs_ref, first_ref, sums, buffer, sems):
    parts = sums.shape[0]
    share = sums.shape[1] - 2
    copies = started(smooth_ref, buffer, sems, parts)
    for part in range(parts):
        sums[part] = got_ref[part, 0] + got_ref[part ^ 2, 1]
    for part in range(parts):
        copies[part].wait()
        for i in range(share):
            value = sums[part, i + 1]
            if i == 0 and part > 0:
                value = value + sums[part - 1, share + 1]
            if i == share - 1 and part < parts - 1:
                value = value + sums[part + 1, 0]
            a = part * share + i
            rhs_ref[a] = value
            first_ref[a] = product(value, buffer[a])


def coarse_own_kernel(rhs_ref, first_ref, diag_ref, out_ref, buffer, sems):
    parts = sems.shape[0]
    share = buffer.shape[0] // parts
    copies = started(diag_ref, buffer, sems, parts)
    for part in range(parts):
        copies[part].wait()
        for a in range(part * share, (part + 1) * share):
            out_ref[a] = rhs_ref[a] - product(first_ref[a], buffer[a])


def coarse_last_kernel(
    pos,
    nbr,
    inner_ref,
    pair_ref,
    first_ref,
    next_ref,
    smooth_ref,
    weight_ref,
    out_ref,
    window,
    buffer,
    sems,
    window_sems,
):
    parts, _, slots = out_ref.shape[:3]
    share = slots - 2
    total = window.shape[0] // 3
    copies = started(smooth_ref, buffer, sems, parts)
    moves = []
    for k, (side, ref) in enumerate(((pos[4], pair_ref), (1, first_ref), (2 - pos[4], next_ref))):
        target = window.at[pl.ds(pl.multiple_of(side * total, total), total)]
        moves.append(pltpu.make_async_copy(ref, target, window_sems.at[k]))
        moves[-1].start()
    out_ref[0, 0, 0] = jnp.zeros_like(inner_ref[0])
    out_ref[parts - 1, 0, share + 1] = jnp.zeros_like(inner_ref[0])
    for move in moves:
        move.wait()
    for part in range(parts):
        copies[part].wait()
        for i in range(share):
            a = part * share + i
            value = inner_ref[a]
            for n in range(weight_ref.shape[1]):
                at = nbr[a, n] - (pos[1] - 1) * total
                value = value + weight_ref[a, n][None, :] * window[at]
            value = first_ref[a] + product(value, buffer[a])
            out_ref[part, 0, i + 1] = value
            if i == 0 and part > 0:
                out_ref[part - 1, 0, share + 1] = value
            if i == share - 1 and part < parts - 1:
                out_ref[part + 1, 0, 0] = value
    for part in range(parts):
        out_ref[part ^ 2, 1] = out_ref[part, 0]


def fill_table(pos, pair_ref, own_ref, next_ref, table):
    parts, _, rows, _ = own_ref.shape
    for side, flip, ref in (
        (pos[4], pos[3], pair_ref),
        (1, pos[3], own_ref),
        (2 - pos[4], 1 - pos[3], next_ref),
    ):
        for part in range(parts):
            at = pl.multiple_of(quarter(flip, part) * rows, rows)
            table[side, :, pl.ds(at, rows)] = ref[part]


def corrected(pos, owner, agg, table, fine, weight, p, b):
    side = owner[p, b] - pos[1] + 1
    slot = agg[p, b] - pos[0] + 1
    return fine + weight[None, :] * table[side, slot]


def rim_kernel(
    pos,
    owner,
    agg,
    fine_ref,
    w_ref,
    pair_ref,
    own_ref,
    next_ref,
    inner,
    outer,
    y_first,
    y_last,
    table,
    row_buf,
    col_buf,
    sems,
):
    blocks_x, blocks_y = w_ref.shape[:2]
    ends, sides = (0, blocks_x - 1), (0, blocks_y - 1)
    loads = [(fine_ref.at[:, q], col_buf.at[k]) for k, q in enumerate(sides)]
    loads += [(fine_ref.at[p], row_buf.at[k]) for k, p in enumerate(ends)]
    copies = [pltpu.make_async_copy(a, b, sems.at[k]) for k, (a, b) in enumerate(loads)]
    for copy in copies:
        copy.start()
    fill_table(pos, pair_ref, own_ref, next_ref, table)
    for k, (q, ref) in enumerate(zip(sides, (y_first, y_last))):
        copies[k].wait()
        for p in range(blocks_x):
            ref[p] = corrected(pos, owner, agg, table, col_buf[k, p], w_ref[p, q], p, q)
    for k, p in enumerate(ends):
        copies[2 + k].wait()

        def put(ref):
            for b in range(blocks_y):
                ref[b] = corrected(pos, owner, agg, table, row_buf[k, b], w_ref[p, b], p, b)

        @pl.when(pos[2] == 1 - k)
        def _():
            put(inner)

        @pl.when(pos[2] == k)
        def _():
            put(outer)


def finish_kernel(
    pos,
    owner,
    agg,
    fine_ref,
    w_ref,
    r_ref,
    diag_ref,
    face_ref,
    pair_ref,
    own_ref,
    next_ref,
    out_ref,
    res_ref,
    table,
    solved,
):
    s = pl.program_id(0)
    last = pl.num_programs(0) - 1
    per, blocks_y = fine_ref.shape[:2]
    blocks_x = solved.shape[0] - 2

    @pl.when(s == 0)
    def _():
        fill_table(pos, pair_ref, own_ref, next_ref, table)
        solved[0] = jnp.zeros_like(solved[0])
        solved[blocks_x + 1] = jnp.zeros_like(solved[0])

    @pl.when(s < last)
    def _():
        for t in range(per):
            p = s * per + t
            for b in range(blocks_y):
                value = corrected(pos, owner, agg, table, fine_ref[t, b], w_ref[t, b], p, b)
                solved[p + 1, b] = value
                out_ref[t, b] = value

    @pl.when(s > 0)
    def _():
        for t in range(per):
            p = (s - 1) * per + t
            for b in range(blocks_y):
                face = face_ref[t, b]
                value = r_ref[t, b] - product(solved[p + 1, b], diag_ref[t, b])
                value = value + face[0][None, :] * solved[p, b]
                value = value + face[1][None, :] * solved[p + 2, b]
                if b > 0:
                    value = value + face[2][None, :] * solved[p + 1, b - 1]
                if b < blocks_y - 1:
                    value = value + face[3][None, :] * solved[p + 1, b + 1]
                res_ref[t, b] = value


def border_kernel(
    pos, part_ref, face_ref, x_inner, x_outer, y_low, y_high, out_ref, row_buf, col_buf, sems
):
    blocks_x, blocks_y = face_ref.shape[:2]
    core = pos[2]
    ends = (0, blocks_x - 1)
    sides = (0, blocks_y - 1)
    inside = pl.ds(1, blocks_x - 2)
    pairs = [(out_ref.at[p], row_buf.at[k]) for k, p in enumerate(ends)]
    pairs += [(out_ref.at[inside, q], col_buf.at[k]) for k, q in enumerate(sides)]
    loads = [pltpu.make_async_copy(a, b, sems.at[k]) for k, (a, b) in enumerate(pairs)]
    for load in loads:
        load.start()
    for load in loads:
        load.wait()
    for k, p in enumerate(ends):
        lower = core == k
        for b in range(blocks_y):
            beyond = jnp.where(lower, x_outer[b], x_inner[b])
            row_buf[k, b] += face_ref[p, b, k][None, :] * beyond
    for k, (q, halo_ref) in enumerate(zip(sides, (y_low, y_high))):
        for j, p in enumerate(ends):
            row_buf[j, q] += face_ref[p, q, 2 + k][None, :] * halo_ref[p]
        for p in range(1, blocks_x - 1):
            col_buf[k, p - 1] += face_ref[p, q, 2 + k][None, :] * halo_ref[p]
    stores = [pltpu.make_async_copy(b, a, sems.at[4 + k]) for k, (a, b) in enumerate(pairs)]
    for store in stores:
        store.start()
    for store in stores:
        store.wait()


def to_sibling(array):
    return moved_to(array, lambda x, y: (x ^ 1, y))


def halo(faces):
    inner, outer, y_first, y_last = faces
    y_low = straight(y_last, 1)
    y_high = straight(y_first, -1)
    x_inner = to_sibling(inner)
    x_outer = moved_to(outer, lambda x, y: (((x + 1) ^ 1) - 1, y))
    return x_inner, x_outer, y_low, y_high


def body(
    right_side,
    diag_blocks,
    smoother,
    face_weight,
    restrict_weight,
    prolong_weight,
    block_owner,
    block_aggregate,
    coarse_diag,
    coarse_smooth,
    neighbors,
    neighbor_weight,
):
    blocks_x, blocks_y, rows, size = right_side.shape
    total = coarse_diag.shape[0]
    parts = lax.axis_size("gx")
    share = total // parts
    per = 2
    steps = blocks_x // per
    fine_shape = right_side.shape
    mat_shape = diag_blocks.shape
    slab = (parts, share + 2, rows // parts, size)
    double = (parts, 2) + slab[1:]
    coarse_shape = (total, rows // parts, size)
    x_face = (blocks_y, rows, size)
    y_face = (blocks_x, rows, size)
    block_flops = 2 * 4 * rows * size * size
    fine_count = blocks_x * blocks_y
    fine_bytes = fine_count * rows * size * 4
    coarse_flops = total * block_flops // parts
    coarse_bytes = total * size * size * 4
    hbm = pl.BlockSpec(memory_space=pl.ANY)
    fine_block = part_block(fine_shape, per)
    mat_block = part_block(mat_shape, per)
    weight_block = part_block(face_weight.shape, per)
    vmem = pl.BlockSpec(memory_space=pltpu.VMEM)
    cmat_scratch = [
        pltpu.VMEM(coarse_diag.shape, F32),
        pltpu.SemaphoreType.DMA((parts,)),
    ]
    face_specs = [whole(x_face)] * 2 + [part_block(y_face, per)] * 2
    face_shapes = [like(x_face)] * 2 + [like(y_face)] * 2

    gx, gy = lax.axis_index("gx"), lax.axis_index("gy")
    pos = jnp.stack([gx * share, gy, gx % 2, gy // 2 % 2, 2 * (1 - gy % 2)]).astype(jnp.int32)

    to_pair, own, to_next = call(
        restrict_kernel,
        1,
        [hbm, whole(restrict_weight.shape)],
        [vmem] * 3,
        [like(slab)] * 3,
        scalars=3,
        scratch=[
            pltpu.VMEM((3, share + 2, rows, size), F32),
            pltpu.VMEM(fine_shape, F32),
            pltpu.SemaphoreType.DMA((blocks_x,)),
        ],
        moved=2 * fine_bytes,
    )(pos, block_owner, block_aggregate, right_side, restrict_weight)

    from_pair = in_pair(to_pair)
    from_next = between_pairs(to_next)

    sweep, *faces = call(
        sweep_kernel,
        steps,
        [fine_block, mat_block],
        [fine_block] + face_specs,
        [like(fine_shape)] + face_shapes,
        scalars=1,
        flops=fine_count * block_flops,
        moved=3 * fine_bytes,
    )(pos, right_side, smoother)

    own, from_pair, from_next, sweep = lax.optimization_barrier(
        (own, from_pair, from_next, sweep)
    )
    got = lax.all_to_all(
        jnp.stack([own + from_pair, from_next], axis=1), "gx", 0, 0, tiled=True
    )

    rhs, first = call(
        coarse_first_kernel,
        1,
        [vmem, hbm],
        [vmem] * 2,
        [like(coarse_shape)] * 2,
        scratch=[pltpu.VMEM(slab, F32)] + cmat_scratch,
        flops=coarse_flops,
        moved=coarse_bytes,
    )(got, coarse_smooth)

    first, rhs, faces = lax.optimization_barrier((first, rhs, faces))
    sweep_halo = halo(faces)
    pair_first = in_pair(first)
    next_first = between_pairs(first)

    inner = call(
        coarse_own_kernel,
        1,
        [vmem, vmem, hbm],
        vmem,
        like(coarse_shape),
        scratch=cmat_scratch,
        flops=coarse_flops,
        moved=coarse_bytes,
    )(rhs, first, coarse_diag)

    corr = call(
        coarse_last_kernel,
        1,
        [vmem] * 4 + [hbm, vmem],
        vmem,
        like(double),
        scalars=2,
        scratch=[pltpu.VMEM((3 * total,) + coarse_shape[1:], F32)]
        + cmat_scratch
        + [pltpu.SemaphoreType.DMA((3,))],
        flops=coarse_flops,
        moved=coarse_bytes,
    )(pos, neighbors, inner, pair_first, first, next_first, coarse_smooth, neighbor_weight)

    x_inner, x_outer, y_low, y_high = sweep_halo
    corr, x_outer, y_low = lax.optimization_barrier((corr, x_outer, y_low))
    sweep_halo = (x_inner, x_outer, y_low, y_high)
    mine = lax.all_to_all(corr, "gx", 0, 0, tiled=True)
    tables = (in_pair(mine[:, 0]), mine[:, 0], between_pairs(mine[:, 1]))

    fine_part = call(
        fine_kernel,
        steps,
        [fine_block] + [mat_block] * 2 + [weight_block, whole(fine_shape)]
        + [vmem] * 2
        + [part_block(y_face, per)] * 2,
        fine_block,
        like(fine_shape),
        scalars=1,
        scratch=[pltpu.VMEM(x_face, F32)] * 2,
        flops=2 * fine_count * block_flops,
        moved=5 * fine_bytes,
    )(pos, right_side, smoother, diag_blocks, face_weight, sweep, *sweep_halo)

    rim = call(
        rim_kernel,
        1,
        [hbm] + [vmem] * 4,
        [vmem] * 4,
        face_shapes,
        scalars=3,
        scratch=[
            pltpu.VMEM((3, share + 2, rows, size), F32),
            pltpu.VMEM((2,) + x_face, F32),
            pltpu.VMEM((2,) + y_face, F32),
            pltpu.SemaphoreType.DMA((4,)),
        ],
        moved=fine_bytes,
    )(pos, block_owner, block_aggregate, fine_part, prolong_weight, *tables)
    solved_halo = halo(rim)

    def now(shape):
        return pl.BlockSpec(
            (per,) + tuple(shape[1:]),
            lambda s, *_: (jnp.minimum(s, steps - 1),) + (0,) * (len(shape) - 1),
        )

    def previous(shape):
        return pl.BlockSpec(
            (per,) + tuple(shape[1:]),
            lambda s, *_: (jnp.maximum(s - 1, 0),) + (0,) * (len(shape) - 1),
        )

    solved, residual = call(
        finish_kernel,
        steps + 1,
        [
            now(fine_shape),
            now(prolong_weight.shape),
            previous(fine_shape),
            previous(mat_shape),
            previous(face_weight.shape),
        ]
        + [vmem] * 3,
        [now(fine_shape), previous(fine_shape)],
        [like(fine_shape)] * 2,
        scalars=3,
        scratch=[
            pltpu.VMEM((3, share + 2, rows, size), F32),
            pltpu.VMEM((blocks_x + 2, blocks_y, rows, size), F32),
        ],
        flops=fine_count * block_flops,
        moved=5 * fine_bytes,
    )(
        pos,
        block_owner,
        block_aggregate,
        fine_part,
        prolong_weight,
        right_side,
        diag_blocks,
        face_weight,
        *tables,
    )

    residual = call(
        border_kernel,
        1,
        [hbm, whole(face_weight.shape)] + [vmem] * 4,
        hbm,
        like(fine_shape),
        scalars=1,
        scratch=[
            pltpu.VMEM((2,) + x_face, F32),
            pltpu.VMEM((2, blocks_x - 2, rows, size), F32),
            pltpu.SemaphoreType.DMA((8,)),
        ],
        moved=fine_bytes,
        aliases={1: 0},
    )(pos, residual, face_weight, *solved_halo)
    return (solved, residual)


def solution(mesh):
    return jax.shard_map(
        body,
        mesh=mesh,
        in_specs=(
            P("gx", "gy", None, None),
            P("gx", "gy", None, None),
            P("gx", "gy", None, None),
            P("gx", "gy", None, None),
            P("gx", "gy", None),
            P("gx", "gy", None),
            P("gx", "gy"),
            P("gx", "gy"),
            P("gy", None, None),
            P("gy", None, None),
            P("gy", None),
            P("gy", None, None),
        ),
        out_specs=(P("gx", "gy", None, None), P("gx", "gy", None, None)),
        check_vma=False,
    )
```

time: 463 us -> 188 us (0.41)
  the two profiles are of different devices: /device:TPU:1 before, /device:TPU:11 now
where the time goes in v2:
time: 188 us; the launch traced here: 187 us
  starting transfers between devices  53.3 us (28%)
  Pallas kernels  50.8 us (27%)
  waiting for transfers between devices  49.3 us (26%)
  blocking collectives  23.1 us (12%)
  local copies, waits for them, and re-layouts  9.42 us (5%)
    ppermute x14, starting transfers between devices, moved_to(): return lax.ppermute(array, ('gx', 'gy'), pairs)  48.9 us
    ppermute x14, waiting for transfers between devices, moved_to(): return lax.ppermute(array, ('gx', 'gy'), pairs)  34.3 us
    all_to_all x1, blocking collectives, body(): lax.all_to_all(jnp.stack([own + from_pair, from_next], axis=1), 'gx', 0,...  23.1 us
    all_to_all x1, waiting for transfers between devices, body(): mine = lax.all_to_all(corr, 'gx', 0, 0, tiled=True)  15 us
    pallas_call x1, Pallas kernels, body(): call(fine_kernel, steps, [fine_block] + [mat_block] * 2 + [weight_block,...  12.9 us
    pallas_call x1, Pallas kernels, body(): call(finish_kernel, steps + 1, [now(fine_shape), now(prolong_weight.shape...  11.4 us
    unnamed x44, local copies, waits for them, and re-layouts  7.96 us
    pallas_call x1, Pallas kernels, body(): call(sweep_kernel, steps, [fine_block, mat_block], [fine_block] + face_sp...  7.91 us
  transfers between devices with their start and end apart: 15, of which 8 were waited for; matrix products, arithmetic and copies ran while one was open for 1% of the time, Pallas kernels for 22%

profile of v2, /device:TPU:11, one launch (start us, length us, event | category | flops | bytes accessed | tf_op | source)
XLA Modules:
  0.0 187.1 jit_solution(17065629762129788219)
XLA Ops:
  0.8 2.2 %copy-done = f32[8,8,128,128]{3,2,1,0:T(8,128)S(1)} copy-done((f32[8,8,128,128]{3,2,1,0:T(8,128)S(1)}, f32[8,8,128,128]{3,2,1,0:T(8,128)}, u32[]{:S(2)}) %copy-start) | copy-done | bytes 4194328
  7.2 5.4 %collective-permute-start.1 = (f32[4,10,32,128]{3,2,1,0:T(8,128)S(1)}, f32[4,10,32,128]{3,2,1,0:T(8,128)S(1)}, u32[]{:S(2)}, u32[]{:S(2)}) collective-permute-start(f32[4,10,32,128]{3,2,1,0:T(8,128)S(1)} %get-tuple-element.33), channel_id=1, source_target_pairs={{1,66},{2,65},{3,68},{4,67},{5,70},{6,69},{7,72},{8,71},{9,74},{10... | collective-permute-start | bytes 1966088 | tf_op jit(solution)/shard_map/ppermute | solution.py:22
  12.5 7.9 %shard_map.132 = (f32[8,8,128,128]{3,2,1,0:T(8,128)}, f32[8,128,128]{2,1,0:T(8,128)S(1)}, f32[8,128,128]{2,1,0:T(8,128)S(1)}, f32[8,128,128]{2,1,0:T(8,128)S(1)}, f32[8,128,128]{2,1,0:T(8,128)S(1)}) custom-call(s32[5]{0:T(128)S(1)} %stack.32.pos, f32[8,8,128,128]{3,2,1,0:T(8,128)} %r_ref.7, f32[8,8,128,128]{3,2,1,0:T(8,128)} %s_ref.3), custom_call_target="tpu_custom_call" | custom-call | flops 42949672960 | bytes 503316480 | tf_op jit(solution)/shard_map/pallas_call | solution.py:516
  22.6 4.1 %collective-permute-done.1 = f32[4,10,32,128]{3,2,1,0:T(8,128)S(1)} collective-permute-done((f32[4,10,32,128]{3,2,1,0:T(8,128)S(1)}, f32[4,10,32,128]{3,2,1,0:T(8,128)S(1)}, u32[]{:S(2)}, u32[]{:S(2)}) %collective-permute-start.1) | collective-permute-done | bytes 655392 | tf_op jit(solution)/shard_map/ppermute | solution.py:22
  26.9 23.1 %all_to_all.10.got_ref = f32[4,2,10,32,128]{4,3,2,1,0:T(8,128)S(1)} all-to-all(f32[4,2,10,32,128]{4,3,2,1,0:T(8,128)S(1)} %pad_maximum_fusion), channel_id=1, replica_groups=mesh['gx'=4,'gy'=32] {'gx'}, dimensions={0} | all-to-all | bytes 2621440 | tf_op jit(solution)/shard_map/all_to_all | solution.py:530
  50.1 2.8 %shard_map.133 = (f32[32,32,128]{2,1,0:T(8,128)S(1)}, f32[32,32,128]{2,1,0:T(8,128)}) custom-call(f32[4,2,10,32,128]{4,3,2,1,0:T(8,128)S(1)} %all_to_all.10.got_ref, f32[32,128,128]{2,1,0:T(8,128)S(1)} %copy-done.9), custom_call_target="tpu_custom_call" | custom-call | flops 5368709120 | bytes 83886080 | tf_op jit(solution)/shard_map/pallas_call | solution.py:534
  53.6 2.4 %collective-permute-start.4 = (f32[32,32,128]{2,1,0:T(8,128)}, f32[32,32,128]{2,1,0:T(8,128)}, u32[]{:S(2)}, u32[]{:S(2)}) collective-permute-start(f32[32,32,128]{2,1,0:T(8,128)} %get-tuple-element.47.first_ref), channel_id=1, source_target_pairs={{1,66},{2,65},{3,68},{4,67},{5,70},{6,69},{7,72},{8,71},{9,74},{10... | collective-permute-start | bytes 1572872 | tf_op jit(solution)/shard_map/ppermute | solution.py:22
  56.0 6.6 %collective-permute-start.3 = (f32[32,32,128]{2,1,0:T(8,128)}, f32[32,32,128]{2,1,0:T(8,128)}, u32[]{:S(2)}, u32[]{:S(2)}) collective-permute-start(f32[32,32,128]{2,1,0:T(8,128)} %get-tuple-element.47.first_ref), channel_id=1, source_target_pairs={{0,1},{1,0},{2,3},{3,2},{4,5},{5,4},{6,7},{7,6},{8,9},{9,8},{10,11... | collective-permute-start | bytes 1572872 | tf_op jit(solution)/shard_map/ppermute | solution.py:22
  62.8 4.7 %collective-permute-start.5 = (f32[8,128,128]{2,1,0:T(8,128)}, f32[8,128,128]{2,1,0:T(8,128)S(1)}, u32[]{:S(2)}, u32[]{:S(2)}) collective-permute-start(f32[8,128,128]{2,1,0:T(8,128)} %copy-done.16), channel_id=1, source_target_pairs={{32,64},{33,65},{34,66},{35,67},{36,68},{37,69},{38,70},{39,71},{4... | collective-permute-start | bytes 1572872 | tf_op jit(solution)/shard_map/ppermute | solution.py:22
  70.5 2.9 %shard_map.134.inner_ref = f32[32,32,128]{2,1,0:T(8,128)S(1)} custom-call(f32[32,32,128]{2,1,0:T(8,128)S(1)} %copy-done.18, f32[32,32,128]{2,1,0:T(8,128)} %get-tuple-element.47.first_ref, f32[32,128,128]{2,1,0:T(8,128)S(1)} %copy-done.8), custom_call_target="tpu_custom_call" | custom-call | flops 5368709120 | bytes 83886080 | tf_op jit(solution)/shard_map/pallas_call | solution.py:550
  74.4 5.2 %shard_map.135 = f32[4,2,10,32,128]{4,3,2,1,0:T(8,128)} custom-call(s32[5]{0:T(128)S(1)} %stack.32.pos, s32[32,6]{1,0:T(8,128)S(1)} %copy.18.nbr, f32[32,32,128]{2,1,0:T(8,128)S(1)} %shard_map.134.inner_ref, f32[32,32,128]{2,1,0:T(8,128)} %collective-permute-done.3.pair_ref, f32[32,32,128]{2,1,0:T(8,128)} %get-tuple-element.47.first_ref, ...), custom_call_target="tpu_custom_call" | custom-call | flops 5368709120 | bytes 83886080 | tf_op jit(solution)/shard_map/pallas_call | solution.py:561
  79.6 7.8 %collective-permute-done.5.x_outer = f32[8,128,128]{2,1,0:T(8,128)S(1)} collective-permute-done((f32[8,128,128]{2,1,0:T(8,128)}, f32[8,128,128]{2,1,0:T(8,128)S(1)}, u32[]{:S(2)}, u32[]{:S(2)}) %collective-permute-start.5) | collective-permute-done | bytes 524320 | tf_op jit(solution)/shard_map/ppermute | solution.py:22
  88.3 3.6 %collective-permute-done.6.y_low = f32[8,128,128]{2,1,0:T(8,128)S(1)} collective-permute-done((f32[8,128,128]{2,1,0:T(8,128)}, f32[8,128,128]{2,1,0:T(8,128)S(1)}, u32[]{:S(2)}, u32[]{:S(2)}) %collective-permute-start.6) | collective-permute-done | bytes 524320 | tf_op jit(solution)/shard_map/ppermute | solution.py:22
  92.7 4.4 %all-to-all-start.1 = ((f32[4,2,10,32,128]{4,3,2,1,0:T(8,128)}), f32[4,2,10,32,128]{4,3,2,1,0:T(8,128)}, u32[]{:S(2)}, u32[]{:S(2)}) async-start(f32[4,2,10,32,128]{4,3,2,1,0:T(8,128)} %shard_map.135), calls=%async_computation.1 | async-start | bytes 2621440 | tf_op jit(solution)/shard_map/all_to_all | solution.py:578
  99.3 15.0 %all-to-all-done.1 = f32[4,2,10,32,128]{4,3,2,1,0:T(8,128)} async-done(((f32[4,2,10,32,128]{4,3,2,1,0:T(8,128)}), f32[4,2,10,32,128]{4,3,2,1,0:T(8,128)}, u32[]{:S(2)}, u32[]{:S(2)}) %all-to-all-start.1) | async-done | bytes 1310752 | tf_op jit(solution)/shard_map/all_to_all | solution.py:578
  115.7 3.8 %collective-permute-start.9 = (f32[4,10,32,128]{3,2,1,0:T(8,128)S(1)}, f32[4,10,32,128]{3,2,1,0:T(8,128)S(1)}, u32[]{:S(2)}, u32[]{:S(2)}) collective-permute-start(f32[4,10,32,128]{3,2,1,0:T(8,128)S(1)} %get-tuple-element.60), channel_id=1, source_target_pairs={{1,66},{2,65},{3,68},{4,67},{5,70},{6,69},{7,72},{8,71},{9,74},{10... | collective-permute-start | bytes 1966088 | tf_op jit(solution)/shard_map/ppermute | solution.py:22
  119.5 9.4 %collective-permute-start.8 = (f32[4,10,32,128]{3,2,1,0:T(8,128)S(1)}, f32[4,10,32,128]{3,2,1,0:T(8,128)S(1)}, u32[]{:S(2)}, u32[]{:S(2)}) collective-permute-start(f32[4,10,32,128]{3,2,1,0:T(8,128)S(1)} %get-tuple-element.61.own_ref), channel_id=1, source_target_pairs={{0,1},{1,0},{2,3},{3,2},{4,5},{5,4},{6,7},{7,6},{8,9},{9,8},{10,11... | collective-permute-start | bytes 1966088 | tf_op jit(solution)/shard_map/ppermute | solution.py:22
  130.8 12.9 %shard_map.136.fine_ref = f32[8,8,128,128]{3,2,1,0:T(8,128)} custom-call(s32[5]{0:T(128)S(1)} %stack.32.pos, f32[8,8,128,128]{3,2,1,0:T(8,128)} %r_ref.7, f32[8,8,128,128]{3,2,1,0:T(8,128)} %s_ref.3, f32[8,8,128,128]{3,2,1,0:T(8,128)} %diag_ref.5, f32[8,8,4,128]{3,2,1,0:T(4,128)S(1)} %copy-done.1, f32[8,8,128,128]{3,2,1,0:T(8,128)} %get-tuple-element.35.v_ref, ...), custom_call_target="tpu_custom_call" | custom-call | flops 85899345920 | bytes 838860800 | tf_op jit(solution)/shard_map/pallas_call | solution.py:581
  143.7 2.4 %shard_map.138 = (f32[8,128,128]{2,1,0:T(8,128)S(1)}, f32[8,128,128]{2,1,0:T(8,128)S(1)}, f32[8,128,128]{2,1,0:T(8,128)S(1)}, f32[8,128,128]{2,1,0:T(8,128)S(1)}) custom-call(s32[5]{0:T(128)S(1)} %stack.32.pos, s32[8,8]{1,0:T(8,128)S(1)} %copy-done.5, s32[8,8]{1,0:T(8,128)S(1)} %copy-done.7, f32[8,8,128,128]{3,2,1,0:T(8,128)} %shard_map.136.fine_ref, ...), custom_call_target="tpu_custom_call" | custom-call | bytes 167772160 | tf_op jit(solution)/shard_map/pallas_call | solution.py:595
  147.1 5.5 %collective-permute-start.11 = (f32[8,128,128]{2,1,0:T(8,128)S(1)}, f32[8,128,128]{2,1,0:T(8,128)S(1)}, u32[]{:S(2)}, u32[]{:S(2)}) collective-permute-start(f32[8,128,128]{2,1,0:T(8,128)S(1)} %get-tuple-element.57), channel_id=1, source_target_pairs={{32,64},{33,65},{34,66},{35,67},{36,68},{37,69},{38,70},{39,71},{4... | collective-permute-start | bytes 1572872 | tf_op jit(solution)/shard_map/ppermute | solution.py:22
  154.5 3.9 %collective-permute-start.13 = (f32[8,128,128]{2,1,0:T(8,128)S(1)}, f32[8,128,128]{2,1,0:T(8,128)S(1)}, u32[]{:S(2)}, u32[]{:S(2)}) collective-permute-start(f32[8,128,128]{2,1,0:T(8,128)S(1)} %get-tuple-element.59), channel_id=1, source_target_pairs={{1,0},{2,1},{3,2},{4,3},{5,4},{6,5},{7,6},{8,7},{9,8},{10,9},{11,1... | collective-permute-start | bytes 1572872 | tf_op jit(solution)/shard_map/ppermute | solution.py:22
  158.4 11.4 %shard_map.137 = (f32[8,8,128,128]{3,2,1,0:T(8,128)}, f32[8,8,128,128]{3,2,1,0:T(8,128)}) custom-call(s32[5]{0:T(128)S(1)} %stack.32.pos, s32[8,8]{1,0:T(8,128)S(1)} %copy-done.5, s32[8,8]{1,0:T(8,128)S(1)} %copy-done.7, f32[8,8,128,128]{3,2,1,0:T(8,128)} %shard_map.136.fine_ref, f32[8,8,128]{2,1,0:T(8,128)S(1)} %copy-done.3, f32[8,8,128,128]{3,2,1,0:T(8,128)} %r_ref.7, ...), custom_call_target="tpu_custom_call" | custom-call | flops 42949672960 | bytes 838860800 | tf_op jit(solution)/shard_map/pallas_call | solution.py:624
  169.8 13.8 %collective-permute-done.12.y_low = f32[8,128,128]{2,1,0:T(8,128)S(1)} collective-permute-done((f32[8,128,128]{2,1,0:T(8,128)S(1)}, f32[8,128,128]{2,1,0:T(8,128)S(1)}, u32[]{:S(2)}, u32[]{:S(2)}) %collective-permute-start.12) | collective-permute-done | bytes 524320 | tf_op jit(solution)/shard_map/ppermute | solution.py:22
  183.6 3.5 %shard_map.139 = f32[8,8,128,128]{3,2,1,0:T(8,128)} custom-call(s32[5]{0:T(128)S(1)} %stack.32.pos, f32[8,8,128,128]{3,2,1,0:T(8,128)} %get-tuple-element.55.part_ref, f32[8,8,4,128]{3,2,1,0:T(4,128)S(1)} %copy-done.1, f32[8,128,128]{2,1,0:T(8,128)S(1)} %collective-permute-done.10.x_inner, ...), custom_call_target="tpu_custom_call", output_to_operand_aliasing={{}: (1, {})} | custom-call | bytes 167772160 | tf_op jit(solution)/shard_map/pallas_call | solution.py:656
  (64 shorter events, 21.4 us)
Async XLA Ops:
  6.9 15.7 %collective-permute-start = (f32[4,10,32,128]{3,2,1,0:T(8,128)S(1)}, f32[4,10,32,128]{3,2,1,0:T(8,128)S(1)}, u32[]{:S(2)}, u32[]{:S(2)}) collective-permute-start(f32[4,10,32,128]{3,2,1,0:T(8,128)S(1)} %get-tuple-element.32), channel_id=1, source_target_pairs={{0,1},{1,0},{2,3},{3,2},{4,5},{5,4},{6,7},{7,6},{8,9},{9,8},{10,11... | collective-permute-start | bytes 1966088 | tf_op jit(solution)/shard_map/ppermute | solution.py:22
  7.2 19.5 %collective-permute-start.1 = (f32[4,10,32,128]{3,2,1,0:T(8,128)S(1)}, f32[4,10,32,128]{3,2,1,0:T(8,128)S(1)}, u32[]{:S(2)}, u32[]{:S(2)}) collective-permute-start(f32[4,10,32,128]{3,2,1,0:T(8,128)S(1)} %get-tuple-element.33), channel_id=1, source_target_pairs={{1,66},{2,65},{3,68},{4,67},{5,70},{6,69},{7,72},{8,71},{9,74},{10... | collective-permute-start | bytes 1966088 | tf_op jit(solution)/shard_map/ppermute | solution.py:22
  26.8 23.3 %copy-start.9 = (f32[32,128,128]{2,1,0:T(8,128)S(1)}, f32[32,128,128]{2,1,0:T(8,128)}, u32[]{:S(2)}) copy-start(f32[32,128,128]{2,1,0:T(8,128)} %smooth_ref.3) | copy-start | bytes 6291460
  50.1 12.6 %copy-start.19 = (f32[32,6,128]{2,0,1:T(8,128)S(1)}, f32[32,6,128]{2,0,1:T(8,128)}, u32[]{:S(2)}) copy-start(f32[32,6,128]{2,0,1:T(8,128)} %param.23) | copy-start | bytes 294916
  50.1 19.4 %copy-start.8 = (f32[32,128,128]{2,1,0:T(8,128)S(1)}, f32[32,128,128]{2,1,0:T(8,128)}, u32[]{:S(2)}) copy-start(f32[32,128,128]{2,1,0:T(8,128)} %diag_ref.3) | copy-start | bytes 6291460
  53.6 19.8 %collective-permute-start.4 = (f32[32,32,128]{2,1,0:T(8,128)}, f32[32,32,128]{2,1,0:T(8,128)}, u32[]{:S(2)}, u32[]{:S(2)}) collective-permute-start(f32[32,32,128]{2,1,0:T(8,128)} %get-tuple-element.47.first_ref), channel_id=1, source_target_pairs={{1,66},{2,65},{3,68},{4,67},{5,70},{6,69},{7,72},{8,71},{9,74},{10... | collective-permute-start | bytes 1572872 | tf_op jit(solution)/shard_map/ppermute | solution.py:22
  56.0 18.3 %collective-permute-start.3 = (f32[32,32,128]{2,1,0:T(8,128)}, f32[32,32,128]{2,1,0:T(8,128)}, u32[]{:S(2)}, u32[]{:S(2)}) collective-permute-start(f32[32,32,128]{2,1,0:T(8,128)} %get-tuple-element.47.first_ref), channel_id=1, source_target_pairs={{0,1},{1,0},{2,3},{3,2},{4,5},{5,4},{6,7},{7,6},{8,9},{9,8},{10,11... | collective-permute-start | bytes 1572872 | tf_op jit(solution)/shard_map/ppermute | solution.py:22
  62.8 24.7 %collective-permute-start.5 = (f32[8,128,128]{2,1,0:T(8,128)}, f32[8,128,128]{2,1,0:T(8,128)S(1)}, u32[]{:S(2)}, u32[]{:S(2)}) collective-permute-start(f32[8,128,128]{2,1,0:T(8,128)} %copy-done.16), channel_id=1, source_target_pairs={{32,64},{33,65},{34,66},{35,67},{36,68},{37,69},{38,70},{39,71},{4... | collective-permute-start | bytes 1572872 | tf_op jit(solution)/shard_map/ppermute | solution.py:22
  67.5 24.3 %collective-permute-start.6 = (f32[8,128,128]{2,1,0:T(8,128)}, f32[8,128,128]{2,1,0:T(8,128)S(1)}, u32[]{:S(2)}, u32[]{:S(2)}) collective-permute-start(f32[8,128,128]{2,1,0:T(8,128)} %copy-done.15), channel_id=1, source_target_pairs={{0,1},{1,2},{2,3},{3,4},{4,5},{5,6},{6,7},{7,8},{8,9},{9,10},{10,1... | collective-permute-start | bytes 1572872 | tf_op jit(solution)/shard_map/ppermute | solution.py:22
  79.6 51.2 %copy-start.1 = (f32[8,8,4,128]{3,2,1,0:T(4,128)S(1)}, f32[8,8,4,128]{3,2,1,0:T(4,128)}, u32[]{:S(2)}) copy-start(f32[8,8,4,128]{3,2,1,0:T(4,128)} %face_ref.5) | copy-start | bytes 393220
  92.7 38.2 %copy-start.12 = (f32[8,128,128]{2,1,0:T(8,128)S(1)}, f32[8,128,128]{2,1,0:T(8,128)}, u32[]{:S(2)}) copy-start(f32[8,128,128]{2,1,0:T(8,128)} %copy-done.11) | copy-start | bytes 1572868
  92.7 21.6 %all-to-all-start.1 = ((f32[4,2,10,32,128]{4,3,2,1,0:T(8,128)}), f32[4,2,10,32,128]{4,3,2,1,0:T(8,128)}, u32[]{:S(2)}, u32[]{:S(2)}) async-start(f32[4,2,10,32,128]{4,3,2,1,0:T(8,128)} %shard_map.135), calls=%async_computation.1 | async-start | bytes 2621440 | tf_op jit(solution)/shard_map/all_to_all | solution.py:578
  97.1 33.7 %copy-start.14 = (f32[8,128,128]{2,1,0:T(8,128)S(1)}, f32[8,128,128]{2,1,0:T(8,128)}, u32[]{:S(2)}) copy-start(f32[8,128,128]{2,1,0:T(8,128)} %copy-done.13) | copy-start | bytes 1572868
  97.1 31.8 %collective-permute-start.2 = (f32[8,128,128]{2,1,0:T(8,128)S(1)}, f32[8,128,128]{2,1,0:T(8,128)S(1)}, u32[]{:S(2)}, u32[]{:S(2)}) collective-permute-start(f32[8,128,128]{2,1,0:T(8,128)S(1)} %get-tuple-element.45), channel_id=1, source_target_pairs={{0,32},{1,33},{2,34},{3,35},{4,36},{5,37},{6,38},{7,39},{8,40},{9,... | collective-permute-start | bytes 1572872 | tf_op jit(solution)/shard_map/ppermute | solution.py:22
  97.2 33.6 %collective-permute-start.7 = (f32[8,128,128]{2,1,0:T(8,128)S(1)}, f32[8,128,128]{2,1,0:T(8,128)S(1)}, u32[]{:S(2)}, u32[]{:S(2)}) collective-permute-start(f32[8,128,128]{2,1,0:T(8,128)S(1)} %get-tuple-element.52), channel_id=1, source_target_pairs={{1,0},{2,1},{3,2},{4,3},{5,4},{6,5},{7,6},{8,7},{9,8},{10,9},{11,1... | collective-permute-start | bytes 1572872 | tf_op jit(solution)/shard_map/ppermute | solution.py:22
  115.7 28.0 %collective-permute-start.9 = (f32[4,10,32,128]{3,2,1,0:T(8,128)S(1)}, f32[4,10,32,128]{3,2,1,0:T(8,128)S(1)}, u32[]{:S(2)}, u32[]{:S(2)}) collective-permute-start(f32[4,10,32,128]{3,2,1,0:T(8,128)S(1)} %get-tuple-element.60), channel_id=1, source_target_pairs={{1,66},{2,65},{3,68},{4,67},{5,70},{6,69},{7,72},{8,71},{9,74},{10... | collective-permute-start | bytes 1966088 | tf_op jit(solution)/shard_map/ppermute | solution.py:22
  119.5 24.3 %copy-start.3 = (f32[8,8,128]{2,1,0:T(8,128)S(1)}, f32[8,8,128]{2,1,0:T(8,128)}, u32[]{:S(2)}) copy-start(f32[8,8,128]{2,1,0:T(8,128)} %w_ref.5) | copy-start | bytes 98308
  119.5 24.2 %copy-start.5 = (s32[8,8]{1,0:T(8,128)S(1)}, s32[8,8]{1,0:T(8,128)}, u32[]{:S(2)}) copy-start(s32[8,8]{1,0:T(8,128)} %owner.5) | copy-start | bytes 772
  119.5 24.2 %copy-start.7 = (s32[8,8]{1,0:T(8,128)S(1)}, s32[8,8]{1,0:T(8,128)}, u32[]{:S(2)}) copy-start(s32[8,8]{1,0:T(8,128)} %agg.5) | copy-start | bytes 772
  119.5 24.2 %collective-permute-start.8 = (f32[4,10,32,128]{3,2,1,0:T(8,128)S(1)}, f32[4,10,32,128]{3,2,1,0:T(8,128)S(1)}, u32[]{:S(2)}, u32[]{:S(2)}) collective-permute-start(f32[4,10,32,128]{3,2,1,0:T(8,128)S(1)} %get-tuple-element.61.own_ref), channel_id=1, source_target_pairs={{0,1},{1,0},{2,3},{3,2},{4,5},{5,4},{6,7},{7,6},{8,9},{9,8},{10,11... | collective-permute-start | bytes 1966088 | tf_op jit(solution)/shard_map/ppermute | solution.py:22
  146.1 23.7 %collective-permute-start.10 = (f32[8,128,128]{2,1,0:T(8,128)S(1)}, f32[8,128,128]{2,1,0:T(8,128)S(1)}, u32[]{:S(2)}, u32[]{:S(2)}) collective-permute-start(f32[8,128,128]{2,1,0:T(8,128)S(1)} %get-tuple-element.56), channel_id=1, source_target_pairs={{0,32},{1,33},{2,34},{3,35},{4,36},{5,37},{6,38},{7,39},{8,40},{9,... | collective-permute-start | bytes 1572872 | tf_op jit(solution)/shard_map/ppermute | solution.py:22
  147.1 22.7 %collective-permute-start.11 = (f32[8,128,128]{2,1,0:T(8,128)S(1)}, f32[8,128,128]{2,1,0:T(8,128)S(1)}, u32[]{:S(2)}, u32[]{:S(2)}) collective-permute-start(f32[8,128,128]{2,1,0:T(8,128)S(1)} %get-tuple-element.57), channel_id=1, source_target_pairs={{32,64},{33,65},{34,66},{35,67},{36,68},{37,69},{38,70},{39,71},{4... | collective-permute-start | bytes 1572872 | tf_op jit(solution)/shard_map/ppermute | solution.py:22
  152.5 31.0 %collective-permute-start.12 = (f32[8,128,128]{2,1,0:T(8,128)S(1)}, f32[8,128,128]{2,1,0:T(8,128)S(1)}, u32[]{:S(2)}, u32[]{:S(2)}) collective-permute-start(f32[8,128,128]{2,1,0:T(8,128)S(1)} %get-tuple-element.58), channel_id=1, source_target_pairs={{0,1},{1,2},{2,3},{3,4},{4,5},{5,6},{6,7},{7,8},{8,9},{9,10},{10,1... | collective-permute-start | bytes 1572872 | tf_op jit(solution)/shard_map/ppermute | solution.py:22
  154.5 29.1 %collective-permute-start.13 = (f32[8,128,128]{2,1,0:T(8,128)S(1)}, f32[8,128,128]{2,1,0:T(8,128)S(1)}, u32[]{:S(2)}, u32[]{:S(2)}) collective-permute-start(f32[8,128,128]{2,1,0:T(8,128)S(1)} %get-tuple-element.59), channel_id=1, source_target_pairs={{1,0},{2,1},{3,2},{4,3},{5,4},{6,5},{7,6},{8,7},{9,8},{10,9},{11,1... | collective-permute-start | bytes 1572872 | tf_op jit(solution)/shard_map/ppermute | solution.py:22
  (12 other events, 44.6 us)

commit v3 on v2

--- a/solution.py
+++ b/solution.py
@@ -22,16 +22,16 @@
     return lax.ppermute(array, ("gx", "gy"), pairs)
 
 
-def straight(array, by):
-    return moved_to(array, lambda x, y: (x, y + by))
-
-
 def in_pair(array):
     return moved_to(array, lambda x, y: (x, y ^ 1))
 
 
 def between_pairs(array):
     return moved_to(array, lambda x, y: (x ^ 2, ((y + 1) ^ 1) - 1))
+
+
+def in_pair_crossed(array):
+    return moved_to(array, lambda x, y: (x ^ 2, y ^ 1))
 
 
 def quarter(flip, device):
@@ -60,7 +60,7 @@
     return both[:, :width] + both[:, width:]
 
 
-def call(kernel, grid, in_specs, out_specs, out_shape, scalars=0, scratch=(), flops=0, moved=0, aliases=None, limit=48):
+def call(kernel, grid, in_specs, out_specs, out_shape, scalars=0, scratch=(), flops=0, moved=0, aliases=None, limit=32):
     return pl.pallas_call(
         kernel,
         grid_spec=pltpu.PrefetchScalarGridSpec(
@@ -111,7 +111,7 @@
             acc[side, slot] += w_ref[p, b][None, :] * buffer[p, b]
     parts, _, rows, _ = own_ref.shape
     for side, flip, ref in (
-        (pos[4], pos[3], pair_ref),
+        (pos[4], 1 - pos[3], pair_ref),
         (1, pos[3], own_ref),
         (2 - pos[4], 1 - pos[3], next_ref),
     ):
@@ -120,11 +120,13 @@
             ref[part] = acc[side, :, pl.ds(at, rows)]
 
 
-def put_faces(s, last, core, row_ref, inner, outer, y_first, y_last):
+def put_faces(s, last, pos, row_ref, inner, outer, y_pair, y_next):
     per, blocks_y = row_ref.shape[:2]
+    core = pos[2]
+    pair_side = jnp.where(pos[4] == 2, blocks_y - 1, 0)
     for t in range(per):
-        y_first[t] = row_ref[t, 0]
-        y_last[t] = row_ref[t, blocks_y - 1]
+        y_pair[t] = row_ref[t, pair_side]
+        y_next[t] = row_ref[t, blocks_y - 1 - pair_side]
 
     for end, row, lower in ((0, 0, 1), (last, per - 1, 0)):
 
@@ -137,13 +139,13 @@
             outer[...] = row_ref[row]
 
 
-def sweep_kernel(pos, r_ref, s_ref, f_ref, inner, outer, y_first, y_last):
+def sweep_kernel(pos, r_ref, s_ref, f_ref, inner, outer, y_pair, y_next):
     s = pl.program_id(0)
     per, blocks_y = r_ref.shape[:2]
     for t in range(per):
         for b in range(blocks_y):
             f_ref[t, b] = product(r_ref[t, b], s_ref[t, b])
-    put_faces(s, pl.num_programs(0) - 1, pos[2], f_ref, inner, outer, y_first, y_last)
+    put_faces(s, pl.num_programs(0) - 1, pos, f_ref, inner, outer, y_pair, y_next)
 
 
 def neighbours_off(result, face, before, after, left, right):
@@ -162,8 +164,8 @@
     v_ref,
     x_inner,
     x_outer,
-    y_low,
-    y_high,
+    y_pair,
+    y_next,
     out_ref,
     before,
     after,
@@ -195,6 +197,14 @@
     @pl.when(s < last)
     def _():
         after[...] = v_ref[jnp.minimum((s + 1) * per, v_ref.shape[0] - 1)]
+
+    even = pos[4] == 2
+
+    def low_side(t):
+        return jnp.where(even, y_next[t], y_pair[t])
+
+    def high_side(t):
+        return jnp.where(even, y_pair[t], y_next[t])
 
     for t in range(per):
         p = s * per + t
@@ -205,8 +215,8 @@
                 face_ref[t, b],
                 before[b] if t == 0 else v_ref[p - 1, b],
                 after[b] if t == per - 1 else v_ref[p + 1, b],
-                y_low[t] if b == 0 else v_ref[p, b - 1],
-                y_high[t] if b == blocks_y - 1 else v_ref[p, b + 1],
+                low_side(t) if b == 0 else v_ref[p, b - 1],
+                high_side(t) if b == blocks_y - 1 else v_ref[p, b + 1],
             )
             out_ref[t, b] = here + product(r_ref[t, b] - image, s_ref[t, b])
 
@@ -289,7 +299,7 @@
 def fill_table(pos, pair_ref, own_ref, next_ref, table):
     parts, _, rows, _ = own_ref.shape
     for side, flip, ref in (
-        (pos[4], pos[3], pair_ref),
+        (pos[4], 1 - pos[3], pair_ref),
         (1, pos[3], own_ref),
         (2 - pos[4], 1 - pos[3], next_ref),
     ):
@@ -305,49 +315,22 @@
 
 
 def rim_kernel(
-    pos,
-    owner,
-    agg,
-    fine_ref,
-    w_ref,
-    pair_ref,
-    own_ref,
-    next_ref,
-    inner,
-    outer,
-    y_first,
-    y_last,
-    table,
-    row_buf,
-    col_buf,
-    sems,
+    pos, owner, agg, fine_ref, w_ref, pair_ref, own_ref, next_ref, y_pair, y_next, table, col_buf, sems
 ):
     blocks_x, blocks_y = w_ref.shape[:2]
-    ends, sides = (0, blocks_x - 1), (0, blocks_y - 1)
-    loads = [(fine_ref.at[:, q], col_buf.at[k]) for k, q in enumerate(sides)]
-    loads += [(fine_ref.at[p], row_buf.at[k]) for k, p in enumerate(ends)]
-    copies = [pltpu.make_async_copy(a, b, sems.at[k]) for k, (a, b) in enumerate(loads)]
+    copies = []
+    for k in range(2):
+        source = fine_ref.at[:, k * (blocks_y - 1)]
+        copies.append(pltpu.make_async_copy(source, col_buf.at[k], sems.at[k]))
+        copies[-1].start()
+    fill_table(pos, pair_ref, own_ref, next_ref, table)
     for copy in copies:
-        copy.start()
-    fill_table(pos, pair_ref, own_ref, next_ref, table)
-    for k, (q, ref) in enumerate(zip(sides, (y_first, y_last))):
-        copies[k].wait()
+        copy.wait()
+    pair_at = jnp.where(pos[4] == 2, 1, 0)
+    for at, ref in ((1 - pair_at, y_next), (pair_at, y_pair)):
+        q = at * (blocks_y - 1)
         for p in range(blocks_x):
-            ref[p] = corrected(pos, owner, agg, table, col_buf[k, p], w_ref[p, q], p, q)
-    for k, p in enumerate(ends):
-        copies[2 + k].wait()
-
-        def put(ref):
-            for b in range(blocks_y):
-                ref[b] = corrected(pos, owner, agg, table, row_buf[k, b], w_ref[p, b], p, b)
-
-        @pl.when(pos[2] == 1 - k)
-        def _():
-            put(inner)
-
-        @pl.when(pos[2] == k)
-        def _():
-            put(outer)
+            ref[p] = corrected(pos, owner, agg, table, col_buf[at, p], w_ref[p, q], p, q)
 
 
 def finish_kernel(
@@ -364,6 +347,8 @@
     next_ref,
     out_ref,
     res_ref,
+    inner,
+    outer,
     table,
     solved,
 ):
@@ -386,6 +371,15 @@
                 value = corrected(pos, owner, agg, table, fine_ref[t, b], w_ref[t, b], p, b)
                 solved[p + 1, b] = value
                 out_ref[t, b] = value
+        for end, row, lower in ((0, 0, 1), (last - 1, per - 1, 0)):
+
+            @pl.when((s == end) & (pos[2] == lower))
+            def _():
+                inner[...] = out_ref[row]
+
+            @pl.when((s == end) & (pos[2] == 1 - lower))
+            def _():
+                outer[...] = out_ref[row]
 
     @pl.when(s > 0)
     def _():
@@ -404,7 +398,7 @@
 
 
 def border_kernel(
-    pos, part_ref, face_ref, x_inner, x_outer, y_low, y_high, out_ref, row_buf, col_buf, sems
+    pos, part_ref, face_ref, x_inner, x_outer, y_pair, y_next, out_ref, row_buf, col_buf, sems
 ):
     blocks_x, blocks_y = face_ref.shape[:2]
     core = pos[2]
@@ -423,11 +417,17 @@
         for b in range(blocks_y):
             beyond = jnp.where(lower, x_outer[b], x_inner[b])
             row_buf[k, b] += face_ref[p, b, k][None, :] * beyond
-    for k, (q, halo_ref) in enumerate(zip(sides, (y_low, y_high))):
+    even = pos[4] == 2
+    for k, q in enumerate(sides):
+        from_pair = even if k == 1 else jnp.logical_not(even)
+
+        def beyond_y(p):
+            return jnp.where(from_pair, y_pair[p], y_next[p])
+
         for j, p in enumerate(ends):
-            row_buf[j, q] += face_ref[p, q, 2 + k][None, :] * halo_ref[p]
+            row_buf[j, q] += face_ref[p, q, 2 + k][None, :] * beyond_y(p)
         for p in range(1, blocks_x - 1):
-            col_buf[k, p - 1] += face_ref[p, q, 2 + k][None, :] * halo_ref[p]
+            col_buf[k, p - 1] += face_ref[p, q, 2 + k][None, :] * beyond_y(p)
     stores = [pltpu.make_async_copy(b, a, sems.at[4 + k]) for k, (a, b) in enumerate(pairs)]
     for store in stores:
         store.start()
@@ -439,13 +439,12 @@
     return moved_to(array, lambda x, y: (x ^ 1, y))
 
 
-def halo(faces):
-    inner, outer, y_first, y_last = faces
-    y_low = straight(y_last, 1)
-    y_high = straight(y_first, -1)
-    x_inner = to_sibling(inner)
-    x_outer = moved_to(outer, lambda x, y: (((x + 1) ^ 1) - 1, y))
-    return x_inner, x_outer, y_low, y_high
+def x_halo(inner, outer):
+    return to_sibling(inner), moved_to(outer, lambda x, y: (((x + 1) ^ 1) - 1, y))
+
+
+def y_halo(y_pair, y_next):
+    return in_pair(y_pair), moved_to(y_next, lambda x, y: (x, ((y + 1) ^ 1) - 1))
 
 
 def body(
@@ -493,7 +492,7 @@
     face_shapes = [like(x_face)] * 2 + [like(y_face)] * 2
 
     gx, gy = lax.axis_index("gx"), lax.axis_index("gy")
-    pos = jnp.stack([gx * share, gy, gx % 2, gy // 2 % 2, 2 * (1 - gy % 2)]).astype(jnp.int32)
+    pos = jnp.stack([gx * share, gy, gx % 2, gy % 2, 2 * (1 - gy % 2)]).astype(jnp.int32)
 
     to_pair, own, to_next = call(
         restrict_kernel,
@@ -524,8 +523,8 @@
         moved=3 * fine_bytes,
     )(pos, right_side, smoother)
 
-    own, from_pair, from_next, sweep = lax.optimization_barrier(
-        (own, from_pair, from_next, sweep)
+    own, from_pair, from_next, sweep_x = lax.optimization_barrier(
+        (own, from_pair, from_next, x_halo(*faces[:2]))
     )
     got = lax.all_to_all(
         jnp.stack([own + from_pair, from_next], axis=1), "gx", 0, 0, tiled=True
@@ -542,9 +541,9 @@
         moved=coarse_bytes,
     )(got, coarse_smooth)
 
-    first, rhs, faces = lax.optimization_barrier((first, rhs, faces))
-    sweep_halo = halo(faces)
-    pair_first = in_pair(first)
+    first, rhs, y_faces = lax.optimization_barrier((first, rhs, faces[2:]))
+    sweep_y = y_halo(*y_faces)
+    pair_first = in_pair_crossed(first)
     next_first = between_pairs(first)
 
     inner = call(
@@ -572,9 +571,7 @@
         moved=coarse_bytes,
     )(pos, neighbors, inner, pair_first, first, next_first, coarse_smooth, neighbor_weight)
 
-    x_inner, x_outer, y_low, y_high = sweep_halo
-    corr, x_outer, y_low = lax.optimization_barrier((corr, x_outer, y_low))
-    sweep_halo = (x_inner, x_outer, y_low, y_high)
+    corr, sweep_y = lax.optimization_barrier((corr, sweep_y))
     mine = lax.all_to_all(corr, "gx", 0, 0, tiled=True)
     tables = (in_pair(mine[:, 0]), mine[:, 0], between_pairs(mine[:, 1]))
 
@@ -582,7 +579,7 @@
         fine_kernel,
         steps,
         [fine_block] + [mat_block] * 2 + [weight_block, whole(fine_shape)]
-        + [vmem] * 2
+        + [whole(x_face)] * 2
         + [part_block(y_face, per)] * 2,
         fine_block,
         like(fine_shape),
@@ -590,24 +587,23 @@
         scratch=[pltpu.VMEM(x_face, F32)] * 2,
         flops=2 * fine_count * block_flops,
         moved=5 * fine_bytes,
-    )(pos, right_side, smoother, diag_blocks, face_weight, sweep, *sweep_halo)
+    )(pos, right_side, smoother, diag_blocks, face_weight, sweep, *sweep_x, *sweep_y)
 
     rim = call(
         rim_kernel,
         1,
-        [hbm] + [vmem] * 4,
-        [vmem] * 4,
-        face_shapes,
+        [hbm, whole(prolong_weight.shape)] + [vmem] * 3,
+        [vmem] * 2,
+        [like(y_face)] * 2,
         scalars=3,
         scratch=[
             pltpu.VMEM((3, share + 2, rows, size), F32),
-            pltpu.VMEM((2,) + x_face, F32),
             pltpu.VMEM((2,) + y_face, F32),
-            pltpu.SemaphoreType.DMA((4,)),
+            pltpu.SemaphoreType.DMA((2,)),
         ],
         moved=fine_bytes,
     )(pos, block_owner, block_aggregate, fine_part, prolong_weight, *tables)
-    solved_halo = halo(rim)
+    solved_y = y_halo(*rim)
 
     def now(shape):
         return pl.BlockSpec(
@@ -621,7 +617,7 @@
             lambda s, *_: (jnp.maximum(s - 1, 0),) + (0,) * (len(shape) - 1),
         )
 
-    solved, residual = call(
+    solved, residual, *x_faces = call(
         finish_kernel,
         steps + 1,
         [
@@ -632,8 +628,8 @@
             previous(face_weight.shape),
         ]
         + [vmem] * 3,
-        [now(fine_shape), previous(fine_shape)],
-        [like(fine_shape)] * 2,
+        [now(fine_shape), previous(fine_shape)] + [vmem] * 2,
+        [like(fine_shape)] * 2 + [like(x_face)] * 2,
         scalars=3,
         scratch=[
             pltpu.VMEM((3, share + 2, rows, size), F32),
@@ -667,7 +663,7 @@
         ],
         moved=fine_bytes,
         aliases={1: 0},
-    )(pos, residual, face_weight, *solved_halo)
+    )(pos, residual, face_weight, *x_halo(*x_faces), *solved_y)
     return (solved, residual)
 
 

time: 188 us -> 175 us (0.931)
  the two profiles are of different devices: /device:TPU:11 before, /device:TPU:1 now
where the time goes in v3:
time: 175 us; the launch traced here: 173 us
  waiting for transfers between devices  50.3 us (29%)
  blocking collectives  42.7 us (24%)
  Pallas kernels  37.7 us (22%)
  starting transfers between devices  32.3 us (18%)
  local copies, waits for them, and re-layouts  8.56 us (5%)
    ppermute x14, waiting for transfers between devices, moved_to(): return lax.ppermute(array, ('gx', 'gy'), pairs)  50.3 us
    ppermute x14, starting transfers between devices, moved_to(): return lax.ppermute(array, ('gx', 'gy'), pairs)  32.3 us
    all_to_all x1, blocking collectives, body(): mine = lax.all_to_all(corr, 'gx', 0, 0, tiled=True)  22.4 us
    all_to_all x1, blocking collectives, body(): lax.all_to_all(jnp.stack([own + from_pair, from_next], axis=1), 'gx', 0,...  20.2 us
    pallas_call x1, Pallas kernels, body(): call(fine_kernel, steps, [fine_block] + [mat_block] * 2 + [weight_block,...  9.7 us
    unnamed x46, local copies, waits for them, and re-layouts  8.38 us
    pallas_call x1, Pallas kernels, body(): call(finish_kernel, steps + 1, [now(fine_shape), now(prolong_weight.shape...  7.21 us
    pallas_call x1, Pallas kernels, body(): call(coarse_last_kernel, 1, [vmem] * 4 + [hbm, vmem], vmem, like(double),...  4.64 us
  transfers between devices with their start and end apart: 14, of which 5 were waited for; matrix products, arithmetic and copies ran while one was open for 0% of the time, Pallas kernels for 17%

profile of v3, /device:TPU:1, one launch (start us, length us, event | category | flops | bytes accessed | tf_op | source)
XLA Modules:
  0.0 172.7 jit_solution(14095744198296504807)
XLA Ops:
  0.7 2.2 %copy-done = f32[8,8,128,128]{3,2,1,0:T(8,128)S(1)} copy-done((f32[8,8,128,128]{3,2,1,0:T(8,128)S(1)}, f32[8,8,128,128]{3,2,1,0:T(8,128)}, u32[]{:S(2)}) %copy-start) | copy-done | bytes 4194328
  5.1 1.8 %shard_map.132 = (f32[4,10,32,128]{3,2,1,0:T(8,128)S(1)}, f32[4,10,32,128]{3,2,1,0:T(8,128)S(1)}, f32[4,10,32,128]{3,2,1,0:T(8,128)S(1)}) custom-call(s32[5]{0:T(128)S(1)} %stack.32.pos, s32[8,8]{1,0:T(8,128)S(1)} %copy-done.5, s32[8,8]{1,0:T(8,128)S(1)} %copy-done.7, f32[8,8,128,128]{3,2,1,0:T(8,128)S(1)} %copy-done, f32[8,8,128]{2,1,0:T(8,128)S(1)} %copy-done.3), custom_call_target="tpu_custom_call" | custom-call | bytes 335544320 | tf_op jit(solution)/shard_map/pallas_call | solution.py:497
  6.9 2.2 %collective-permute-start = (f32[4,10,32,128]{3,2,1,0:T(8,128)S(1)}, f32[4,10,32,128]{3,2,1,0:T(8,128)S(1)}, u32[]{:S(2)}, u32[]{:S(2)}) collective-permute-start(f32[4,10,32,128]{3,2,1,0:T(8,128)S(1)} %get-tuple-element.32), channel_id=1, source_target_pairs={{0,1},{1,0},{2,3},{3,2},{4,5},{5,4},{6,7},{7,6},{8,9},{9,8},{10,11... | collective-permute-start | bytes 1966088 | tf_op jit(solution)/shard_map/ppermute | solution.py:22
  9.8 4.1 %shard_map.131 = (f32[8,8,128,128]{3,2,1,0:T(8,128)S(1)}, f32[8,128,128]{2,1,0:T(8,128)S(1)}, f32[8,128,128]{2,1,0:T(8,128)S(1)}, f32[8,128,128]{2,1,0:T(8,128)S(1)}, f32[8,128,128]{2,1,0:T(8,128)S(1)}) custom-call(s32[5]{0:T(128)S(1)} %stack.32.pos, f32[8,8,128,128]{3,2,1,0:T(8,128)S(1)} %copy-done, f32[8,8,128,128]{3,2,1,0:T(8,128)S(1)} %copy-done.9), custom_call_target="tpu_custom_call" | custom-call | flops 42949672960 | bytes 503316480 | tf_op jit(solution)/shard_map/pallas_call | solution.py:515
  13.9 2.0 %copy-done.19 = f32[8,8,128,128]{3,2,1,0:T(8,128)} copy-done((f32[8,8,128,128]{3,2,1,0:T(8,128)}, f32[8,8,128,128]{3,2,1,0:T(8,128)S(1)}, u32[]{:S(2)}) %copy-start.19) | copy-done | bytes 4194328
  16.9 4.4 %collective-permute-start.3 = (f32[8,128,128]{2,1,0:T(8,128)S(1)}, f32[8,128,128]{2,1,0:T(8,128)S(1)}, u32[]{:S(2)}, u32[]{:S(2)}) collective-permute-start(f32[8,128,128]{2,1,0:T(8,128)S(1)} %get-tuple-element.35), channel_id=1, source_target_pairs={{32,64},{33,65},{34,66},{35,67},{36,68},{37,69},{38,70},{39,71},{4... | collective-permute-start | bytes 1572872 | tf_op jit(solution)/shard_map/ppermute | solution.py:22
  21.3 11.1 %collective-permute-done.3.x_outer = f32[8,128,128]{2,1,0:T(8,128)S(1)} collective-permute-done((f32[8,128,128]{2,1,0:T(8,128)S(1)}, f32[8,128,128]{2,1,0:T(8,128)S(1)}, u32[]{:S(2)}, u32[]{:S(2)}) %collective-permute-start.3) | collective-permute-done | bytes 524320 | tf_op jit(solution)/shard_map/ppermute | solution.py:22
  32.7 20.2 %all_to_all.10.got_ref = f32[4,2,10,32,128]{4,3,2,1,0:T(8,128)S(1)} all-to-all(f32[4,2,10,32,128]{4,3,2,1,0:T(8,128)S(1)} %pad_maximum_fusion), channel_id=1, replica_groups=mesh['gx'=4,'gy'=32] {'gx'}, dimensions={0} | all-to-all | bytes 2621440 | tf_op jit(solution)/shard_map/all_to_all | solution.py:529
  52.9 2.8 %shard_map.133 = (f32[32,32,128]{2,1,0:T(8,128)S(1)}, f32[32,32,128]{2,1,0:T(8,128)}) custom-call(f32[4,2,10,32,128]{4,3,2,1,0:T(8,128)S(1)} %all_to_all.10.got_ref, f32[32,128,128]{2,1,0:T(8,128)S(1)} %copy-done.13), custom_call_target="tpu_custom_call" | custom-call | flops 5368709120 | bytes 83886080 | tf_op jit(solution)/shard_map/pallas_call | solution.py:533
  58.0 8.3 %collective-permute-start.4 = (f32[32,32,128]{2,1,0:T(8,128)}, f32[32,32,128]{2,1,0:T(8,128)}, u32[]{:S(2)}, u32[]{:S(2)}) collective-permute-start(f32[32,32,128]{2,1,0:T(8,128)} %get-tuple-element.46.first_ref), channel_id=1, source_target_pairs={{0,65},{1,64},{2,67},{3,66},{4,69},{5,68},{6,71},{7,70},{8,73},{9,... | collective-permute-start | bytes 1572872 | tf_op jit(solution)/shard_map/ppermute | solution.py:22
  68.5 2.9 %shard_map.134.inner_ref = f32[32,32,128]{2,1,0:T(8,128)S(1)} custom-call(f32[32,32,128]{2,1,0:T(8,128)S(1)} %copy-done.18, f32[32,32,128]{2,1,0:T(8,128)} %get-tuple-element.46.first_ref, f32[32,128,128]{2,1,0:T(8,128)S(1)} %copy-done.12), custom_call_target="tpu_custom_call" | custom-call | flops 5368709120 | bytes 83886080 | tf_op jit(solution)/shard_map/pallas_call | solution.py:549
  71.4 17.3 %collective-permute-done.4.pair_ref = f32[32,32,128]{2,1,0:T(8,128)} collective-permute-done((f32[32,32,128]{2,1,0:T(8,128)}, f32[32,32,128]{2,1,0:T(8,128)}, u32[]{:S(2)}, u32[]{:S(2)}) %collective-permute-start.4) | collective-permute-done | bytes 524320 | tf_op jit(solution)/shard_map/ppermute | solution.py:22
  88.7 4.6 %shard_map.135 = f32[4,2,10,32,128]{4,3,2,1,0:T(8,128)S(1)} custom-call(s32[5]{0:T(128)S(1)} %stack.32.pos, s32[32,6]{1,0:T(8,128)S(1)} %copy.18.nbr, f32[32,32,128]{2,1,0:T(8,128)S(1)} %shard_map.134.inner_ref, f32[32,32,128]{2,1,0:T(8,128)} %collective-permute-done.4.pair_ref, f32[32,32,128]{2,1,0:T(8,128)} %get-tuple-element.46.first_ref, ...), custom_call_target="tpu_custom_call" | custom-call | flops 5368709120 | bytes 83886080 | tf_op jit(solution)/shard_map/pallas_call | solution.py:560
  93.4 22.4 %all_to_all.11 = f32[4,2,10,32,128]{4,3,2,1,0:T(8,128)S(1)} all-to-all(f32[4,2,10,32,128]{4,3,2,1,0:T(8,128)S(1)} %shard_map.135), channel_id=1, replica_groups=mesh['gx'=4,'gy'=32] {'gx'}, dimensions={0} | all-to-all | bytes 2621440 | tf_op jit(solution)/shard_map/all_to_all | solution.py:575
  116.6 3.6 %collective-permute-start.8 = (f32[4,10,32,128]{3,2,1,0:T(8,128)S(1)}, f32[4,10,32,128]{3,2,1,0:T(8,128)S(1)}, u32[]{:S(2)}, u32[]{:S(2)}) collective-permute-start(f32[4,10,32,128]{3,2,1,0:T(8,128)S(1)} %get-tuple-element.59.own_ref), channel_id=1, source_target_pairs={{0,1},{1,0},{2,3},{3,2},{4,5},{5,4},{6,7},{7,6},{8,9},{9,8},{10,11... | collective-permute-start | bytes 1966088 | tf_op jit(solution)/shard_map/ppermute | solution.py:22
  120.2 9.7 %shard_map.136.fine_ref = f32[8,8,128,128]{3,2,1,0:T(8,128)S(1)} custom-call(s32[5]{0:T(128)S(1)} %stack.32.pos, f32[8,8,128,128]{3,2,1,0:T(8,128)S(1)} %copy-done.1, f32[8,8,128,128]{3,2,1,0:T(8,128)S(1)} %copy-done.10, f32[8,8,128,128]{3,2,1,0:T(8,128)S(1)} %copy-done.11, f32[8,8,4,128]{3,2,1,0:T(4,128)S(1)} %copy-done.2, f32[8,8,128,128]{3,2,1,0:T(8,128)} %copy-done.19, ...), custom_call_target="tpu_custom_call" | custom-call | flops 85899345920 | bytes 838860800 | tf_op jit(solution)/shard_map/pallas_call | solution.py:578
  129.9 4.3 %collective-permute-done.8.pair_ref = f32[4,10,32,128]{3,2,1,0:T(8,128)S(1)} collective-permute-done((f32[4,10,32,128]{3,2,1,0:T(8,128)S(1)}, f32[4,10,32,128]{3,2,1,0:T(8,128)S(1)}, u32[]{:S(2)}, u32[]{:S(2)}) %collective-permute-start.8) | collective-permute-done | bytes 655392 | tf_op jit(solution)/shard_map/ppermute | solution.py:22
  135.2 2.0 %collective-permute-start.12 = (f32[8,128,128]{2,1,0:T(8,128)S(1)}, f32[8,128,128]{2,1,0:T(8,128)S(1)}, u32[]{:S(2)}, u32[]{:S(2)}) collective-permute-start(f32[8,128,128]{2,1,0:T(8,128)S(1)} %get-tuple-element.56), channel_id=1, source_target_pairs={{0,1},{1,0},{2,3},{3,2},{4,5},{5,4},{6,7},{7,6},{8,9},{9,8},{10,11... | collective-permute-start | bytes 1572872 | tf_op jit(solution)/shard_map/ppermute | solution.py:22
  138.0 7.2 %shard_map.137 = (f32[8,8,128,128]{3,2,1,0:T(8,128)}, f32[8,8,128,128]{3,2,1,0:T(8,128)}, f32[8,128,128]{2,1,0:T(8,128)S(1)}, f32[8,128,128]{2,1,0:T(8,128)S(1)}) custom-call(s32[5]{0:T(128)S(1)} %stack.32.pos, s32[8,8]{1,0:T(8,128)S(1)} %copy-done.6, s32[8,8]{1,0:T(8,128)S(1)} %copy-done.8, f32[8,8,128,128]{3,2,1,0:T(8,128)S(1)} %shard_map.136.fine_ref, ...), custom_call_target="tpu_custom_call" | custom-call | flops 42949672960 | bytes 838860800 | tf_op jit(solution)/shard_map/pallas_call | solution.py:620
  145.2 2.2 %collective-permute-start.10 = (f32[8,128,128]{2,1,0:T(8,128)S(1)}, f32[8,128,128]{2,1,0:T(8,128)S(1)}, u32[]{:S(2)}, u32[]{:S(2)}) collective-permute-start(f32[8,128,128]{2,1,0:T(8,128)S(1)} %get-tuple-element.54), channel_id=1, source_target_pairs={{0,32},{1,33},{2,34},{3,35},{4,36},{5,37},{6,38},{7,39},{8,40},{9,... | collective-permute-start | bytes 1572872 | tf_op jit(solution)/shard_map/ppermute | solution.py:22
  147.4 4.1 %collective-permute-start.11 = (f32[8,128,128]{2,1,0:T(8,128)S(1)}, f32[8,128,128]{2,1,0:T(8,128)S(1)}, u32[]{:S(2)}, u32[]{:S(2)}) collective-permute-start(f32[8,128,128]{2,1,0:T(8,128)S(1)} %get-tuple-element.55), channel_id=1, source_target_pairs={{32,64},{33,65},{34,66},{35,67},{36,68},{37,69},{38,70},{39,71},{4... | collective-permute-start | bytes 1572872 | tf_op jit(solution)/shard_map/ppermute | solution.py:22
  151.5 6.2 %collective-permute-done.12.y_pair = f32[8,128,128]{2,1,0:T(8,128)S(1)} collective-permute-done((f32[8,128,128]{2,1,0:T(8,128)S(1)}, f32[8,128,128]{2,1,0:T(8,128)S(1)}, u32[]{:S(2)}, u32[]{:S(2)}) %collective-permute-start.12) | collective-permute-done | bytes 524320 | tf_op jit(solution)/shard_map/ppermute | solution.py:22
  157.8 11.4 %collective-permute-done.11.x_outer = f32[8,128,128]{2,1,0:T(8,128)S(1)} collective-permute-done((f32[8,128,128]{2,1,0:T(8,128)S(1)}, f32[8,128,128]{2,1,0:T(8,128)S(1)}, u32[]{:S(2)}, u32[]{:S(2)}) %collective-permute-start.11) | collective-permute-done | bytes 524320 | tf_op jit(solution)/shard_map/ppermute | solution.py:22
  169.2 3.5 %shard_map.139 = f32[8,8,128,128]{3,2,1,0:T(8,128)} custom-call(s32[5]{0:T(128)S(1)} %stack.32.pos, f32[8,8,128,128]{3,2,1,0:T(8,128)} %get-tuple-element.53.part_ref, f32[8,8,4,128]{3,2,1,0:T(4,128)S(1)} %copy-done.2, f32[8,128,128]{2,1,0:T(8,128)S(1)} %collective-permute-done.10.x_inner, ...), custom_call_target="tpu_custom_call", output_to_operand_aliasing={{}: (1, {})} | custom-call | bytes 167772160 | tf_op jit(solution)/shard_map/pallas_call | solution.py:652
  (65 shorter events, 11.0 us)
Async XLA Ops:
  6.9 25.5 %collective-permute-start = (f32[4,10,32,128]{3,2,1,0:T(8,128)S(1)}, f32[4,10,32,128]{3,2,1,0:T(8,128)S(1)}, u32[]{:S(2)}, u32[]{:S(2)}) collective-permute-start(f32[4,10,32,128]{3,2,1,0:T(8,128)S(1)} %get-tuple-element.32), channel_id=1, source_target_pairs={{0,1},{1,0},{2,3},{3,2},{4,5},{5,4},{6,7},{7,6},{8,9},{9,8},{10,11... | collective-permute-start | bytes 1966088 | tf_op jit(solution)/shard_map/ppermute | solution.py:22
  9.1 23.3 %collective-permute-start.1 = (f32[4,10,32,128]{3,2,1,0:T(8,128)S(1)}, f32[4,10,32,128]{3,2,1,0:T(8,128)S(1)}, u32[]{:S(2)}, u32[]{:S(2)}) collective-permute-start(f32[4,10,32,128]{3,2,1,0:T(8,128)S(1)} %get-tuple-element.33), channel_id=1, source_target_pairs={{1,66},{2,65},{3,68},{4,67},{5,70},{6,69},{7,72},{8,71},{9,74},{10... | collective-permute-start | bytes 1966088 | tf_op jit(solution)/shard_map/ppermute | solution.py:22
  15.9 16.7 %copy-start.15 = (f32[8,128,128]{2,1,0:T(8,128)}, f32[8,128,128]{2,1,0:T(8,128)S(1)}, u32[]{:S(2)}) copy-start(f32[8,128,128]{2,1,0:T(8,128)S(1)} %get-tuple-element.48) | copy-start | bytes 1572868
  15.9 16.8 %copy-start.16 = (f32[8,128,128]{2,1,0:T(8,128)}, f32[8,128,128]{2,1,0:T(8,128)S(1)}, u32[]{:S(2)}) copy-start(f32[8,128,128]{2,1,0:T(8,128)S(1)} %get-tuple-element.47) | copy-start | bytes 1572868
  15.9 5.4 %collective-permute-start.2 = (f32[8,128,128]{2,1,0:T(8,128)S(1)}, f32[8,128,128]{2,1,0:T(8,128)S(1)}, u32[]{:S(2)}, u32[]{:S(2)}) collective-permute-start(f32[8,128,128]{2,1,0:T(8,128)S(1)} %get-tuple-element.34), channel_id=1, source_target_pairs={{0,32},{1,33},{2,34},{3,35},{4,36},{5,37},{6,38},{7,39},{8,40},{9,... | collective-permute-start | bytes 1572872 | tf_op jit(solution)/shard_map/ppermute | solution.py:22
  16.9 15.5 %collective-permute-start.3 = (f32[8,128,128]{2,1,0:T(8,128)S(1)}, f32[8,128,128]{2,1,0:T(8,128)S(1)}, u32[]{:S(2)}, u32[]{:S(2)}) collective-permute-start(f32[8,128,128]{2,1,0:T(8,128)S(1)} %get-tuple-element.35), channel_id=1, source_target_pairs={{32,64},{33,65},{34,66},{35,67},{36,68},{37,69},{38,70},{39,71},{4... | collective-permute-start | bytes 1572872 | tf_op jit(solution)/shard_map/ppermute | solution.py:22
  32.5 20.4 %copy-start.13 = (f32[32,128,128]{2,1,0:T(8,128)S(1)}, f32[32,128,128]{2,1,0:T(8,128)}, u32[]{:S(2)}) copy-start(f32[32,128,128]{2,1,0:T(8,128)} %smooth_ref.3) | copy-start | bytes 6291460
  52.9 14.5 %copy-start.12 = (f32[32,128,128]{2,1,0:T(8,128)S(1)}, f32[32,128,128]{2,1,0:T(8,128)}, u32[]{:S(2)}) copy-start(f32[32,128,128]{2,1,0:T(8,128)} %diag_ref.3) | copy-start | bytes 6291460
  56.5 14.9 %collective-permute-start.5 = (f32[32,32,128]{2,1,0:T(8,128)}, f32[32,32,128]{2,1,0:T(8,128)}, u32[]{:S(2)}, u32[]{:S(2)}) collective-permute-start(f32[32,32,128]{2,1,0:T(8,128)} %get-tuple-element.46.first_ref), channel_id=1, source_target_pairs={{1,66},{2,65},{3,68},{4,67},{5,70},{6,69},{7,72},{8,71},{9,74},{10... | collective-permute-start | bytes 1572872 | tf_op jit(solution)/shard_map/ppermute | solution.py:22
  58.0 30.7 %collective-permute-start.4 = (f32[32,32,128]{2,1,0:T(8,128)}, f32[32,32,128]{2,1,0:T(8,128)}, u32[]{:S(2)}, u32[]{:S(2)}) collective-permute-start(f32[32,32,128]{2,1,0:T(8,128)} %get-tuple-element.46.first_ref), channel_id=1, source_target_pairs={{0,65},{1,64},{2,67},{3,66},{4,69},{5,68},{6,71},{7,70},{8,73},{9,... | collective-permute-start | bytes 1572872 | tf_op jit(solution)/shard_map/ppermute | solution.py:22
  66.5 22.2 %copy-start.14 = (f32[32,128,128]{2,1,0:T(8,128)S(1)}, f32[32,128,128]{2,1,0:T(8,128)}, u32[]{:S(2)}) copy-start(f32[32,128,128]{2,1,0:T(8,128)} %smooth_ref.3) | copy-start | bytes 6291460
  66.5 26.9 %collective-permute-start.6 = (f32[8,128,128]{2,1,0:T(8,128)}, f32[8,128,128]{2,1,0:T(8,128)S(1)}, u32[]{:S(2)}, u32[]{:S(2)}) collective-permute-start(f32[8,128,128]{2,1,0:T(8,128)} %copy-done.16), channel_id=1, source_target_pairs={{0,1},{1,0},{2,3},{3,2},{4,5},{5,4},{6,7},{7,6},{8,9},{9,8},{10,11... | collective-permute-start | bytes 1572872 | tf_op jit(solution)/shard_map/ppermute | solution.py:22
  66.6 26.8 %collective-permute-start.7 = (f32[8,128,128]{2,1,0:T(8,128)}, f32[8,128,128]{2,1,0:T(8,128)S(1)}, u32[]{:S(2)}, u32[]{:S(2)}) collective-permute-start(f32[8,128,128]{2,1,0:T(8,128)} %copy-done.15), channel_id=1, source_target_pairs={{1,2},{2,1},{3,4},{4,3},{5,6},{6,5},{7,8},{8,7},{9,10},{10,9},{11,... | collective-permute-start | bytes 1572872 | tf_op jit(solution)/shard_map/ppermute | solution.py:22
  88.7 31.5 %copy-start.10 = (f32[8,8,128,128]{3,2,1,0:T(8,128)S(1)}, f32[8,8,128,128]{3,2,1,0:T(8,128)}, u32[]{:S(2)}) copy-start(f32[8,8,128,128]{3,2,1,0:T(8,128)} %s_ref.3) | copy-start | bytes 12582916
  88.7 31.5 %copy-start.11 = (f32[8,8,128,128]{3,2,1,0:T(8,128)S(1)}, f32[8,8,128,128]{3,2,1,0:T(8,128)}, u32[]{:S(2)}) copy-start(f32[8,8,128,128]{3,2,1,0:T(8,128)} %diag_ref.5) | copy-start | bytes 12582916
  93.3 26.8 %copy-start.1 = (f32[8,8,128,128]{3,2,1,0:T(8,128)S(1)}, f32[8,8,128,128]{3,2,1,0:T(8,128)}, u32[]{:S(2)}) copy-start(f32[8,8,128,128]{3,2,1,0:T(8,128)} %r_ref.7) | copy-start | bytes 12582916
  93.4 26.8 %copy-start.2 = (f32[8,8,4,128]{3,2,1,0:T(4,128)S(1)}, f32[8,8,4,128]{3,2,1,0:T(4,128)}, u32[]{:S(2)}) copy-start(f32[8,8,4,128]{3,2,1,0:T(4,128)} %face_ref.5) | copy-start | bytes 393220
  115.9 14.0 %collective-permute-start.9 = (f32[4,10,32,128]{3,2,1,0:T(8,128)S(1)}, f32[4,10,32,128]{3,2,1,0:T(8,128)S(1)}, u32[]{:S(2)}, u32[]{:S(2)}) collective-permute-start(f32[4,10,32,128]{3,2,1,0:T(8,128)S(1)} %get-tuple-element.58), channel_id=1, source_target_pairs={{1,66},{2,65},{3,68},{4,67},{5,70},{6,69},{7,72},{8,71},{9,74},{10... | collective-permute-start | bytes 1966088 | tf_op jit(solution)/shard_map/ppermute | solution.py:22
  116.6 17.6 %collective-permute-start.8 = (f32[4,10,32,128]{3,2,1,0:T(8,128)S(1)}, f32[4,10,32,128]{3,2,1,0:T(8,128)S(1)}, u32[]{:S(2)}, u32[]{:S(2)}) collective-permute-start(f32[4,10,32,128]{3,2,1,0:T(8,128)S(1)} %get-tuple-element.59.own_ref), channel_id=1, source_target_pairs={{0,1},{1,0},{2,3},{3,2},{4,5},{5,4},{6,7},{7,6},{8,9},{9,8},{10,11... | collective-permute-start | bytes 1966088 | tf_op jit(solution)/shard_map/ppermute | solution.py:22
  120.2 14.0 %copy-start.4 = (f32[8,8,128]{2,1,0:T(8,128)S(1)}, f32[8,8,128]{2,1,0:T(8,128)}, u32[]{:S(2)}) copy-start(f32[8,8,128]{2,1,0:T(8,128)} %w_ref.5) | copy-start | bytes 98308
  135.2 22.5 %collective-permute-start.12 = (f32[8,128,128]{2,1,0:T(8,128)S(1)}, f32[8,128,128]{2,1,0:T(8,128)S(1)}, u32[]{:S(2)}, u32[]{:S(2)}) collective-permute-start(f32[8,128,128]{2,1,0:T(8,128)S(1)} %get-tuple-element.56), channel_id=1, source_target_pairs={{0,1},{1,0},{2,3},{3,2},{4,5},{5,4},{6,7},{7,6},{8,9},{9,8},{10,11... | collective-permute-start | bytes 1572872 | tf_op jit(solution)/shard_map/ppermute | solution.py:22
  137.3 20.5 %collective-permute-start.13 = (f32[8,128,128]{2,1,0:T(8,128)S(1)}, f32[8,128,128]{2,1,0:T(8,128)S(1)}, u32[]{:S(2)}, u32[]{:S(2)}) collective-permute-start(f32[8,128,128]{2,1,0:T(8,128)S(1)} %get-tuple-element.57), channel_id=1, source_target_pairs={{1,2},{2,1},{3,4},{4,3},{5,6},{6,5},{7,8},{8,7},{9,10},{10,9},{11,... | collective-permute-start | bytes 1572872 | tf_op jit(solution)/shard_map/ppermute | solution.py:22
  145.2 12.6 %collective-permute-start.10 = (f32[8,128,128]{2,1,0:T(8,128)S(1)}, f32[8,128,128]{2,1,0:T(8,128)S(1)}, u32[]{:S(2)}, u32[]{:S(2)}) collective-permute-start(f32[8,128,128]{2,1,0:T(8,128)S(1)} %get-tuple-element.54), channel_id=1, source_target_pairs={{0,32},{1,33},{2,34},{3,35},{4,36},{5,37},{6,38},{7,39},{8,40},{9,... | collective-permute-start | bytes 1572872 | tf_op jit(solution)/shard_map/ppermute | solution.py:22
  147.4 21.8 %collective-permute-start.11 = (f32[8,128,128]{2,1,0:T(8,128)S(1)}, f32[8,128,128]{2,1,0:T(8,128)S(1)}, u32[]{:S(2)}, u32[]{:S(2)}) collective-permute-start(f32[8,128,128]{2,1,0:T(8,128)S(1)} %get-tuple-element.55), channel_id=1, source_target_pairs={{32,64},{33,65},{34,66},{35,67},{36,68},{37,69},{38,70},{39,71},{4... | collective-permute-start | bytes 1572872 | tf_op jit(solution)/shard_map/ppermute | solution.py:22
  (12 other events, 67.8 us)

commit v4 on v3

--- a/solution.py
+++ b/solution.py
@@ -26,16 +26,24 @@
     return moved_to(array, lambda x, y: (x, y ^ 1))
 
 
-def between_pairs(array):
-    return moved_to(array, lambda x, y: (x ^ 2, ((y + 1) ^ 1) - 1))
-
-
 def in_pair_crossed(array):
     return moved_to(array, lambda x, y: (x ^ 2, y ^ 1))
 
 
-def quarter(flip, device):
-    return jnp.where(flip == 1, device ^ 2, device)
+def between_pairs(array):
+    return moved_to(array, lambda x, y: (x, ((y + 1) ^ 1) - 1))
+
+
+def between_pairs_crossed(array):
+    return moved_to(array, lambda x, y: (x ^ 2, ((y + 1) ^ 1) - 1))
+
+
+def to_partner(array):
+    return moved_to(array, lambda x, y: (x ^ 2, y))
+
+
+def quarter(flip, chip, core):
+    return 2 * jnp.where(flip == 1, 1 - chip, chip) + core
 
 
 def halves(x):
@@ -99,7 +107,8 @@
     return copies
 
 
-def restrict_kernel(pos, owner, agg, r_ref, w_ref, pair_ref, own_ref, next_ref, acc, buffer, sems):
+def restrict_kernel(pos, owner, agg, r_ref, w_ref, *refs):
+    out_refs, (acc, buffer, sems) = refs[:6], refs[6:]
     blocks_x, blocks_y = buffer.shape[:2]
     copies = started(r_ref, buffer, sems, blocks_x)
     acc[...] = jnp.zeros_like(acc)
@@ -109,15 +118,26 @@
             side = owner[p, b] - pos[1] + 1
             slot = agg[p, b] - pos[0] + 1
             acc[side, slot] += w_ref[p, b][None, :] * buffer[p, b]
-    parts, _, rows, _ = own_ref.shape
-    for side, flip, ref in (
-        (pos[4], 1 - pos[3], pair_ref),
-        (1, pos[3], own_ref),
-        (2 - pos[4], 1 - pos[3], next_ref),
+    rows = out_refs[0].shape[2]
+    for k, (side, flip) in enumerate(
+        ((pos[4], 1 - pos[3]), (1, pos[3]), (2 - pos[4], 1 - pos[3]))
     ):
-        for part in range(parts):
-            at = pl.multiple_of(quarter(flip, part) * rows, rows)
-            ref[part] = acc[side, :, pl.ds(at, rows)]
+        for j, chip in enumerate((pos[5], 1 - pos[5])):
+            for core in range(2):
+                at = pl.multiple_of(quarter(flip, chip, core) * rows, rows)
+                out_refs[2 * k + j][core] = acc[side, :, pl.ds(at, rows)]
+
+
+def gather_kernel(pos, pair_s, own_s, next_s, pair_x, own_x, next_x, keep, send):
+    core = pos[2]
+    for k, refs in enumerate(((pair_s, own_s, next_s), (pair_x, own_x, next_x))):
+        for out, c in ((keep, core), (send, 1 - core)):
+            out[k] = refs[0][c] + refs[1][c] + refs[2][c]
+
+
+def device_at(pos, k, sibling):
+    chip = pos[5] if k == 0 else 1 - pos[5]
+    return 2 * chip + (1 - pos[2] if sibling else pos[2])
 
 
 def put_faces(s, last, pos, row_ref, inner, outer, y_pair, y_next):
@@ -221,12 +241,13 @@
             out_ref[t, b] = here + product(r_ref[t, b] - image, s_ref[t, b])
 
 
-def coarse_first_kernel(got_ref, smooth_ref, rhs_ref, first_ref, sums, buffer, sems):
+def coarse_first_kernel(pos, keep, other, smooth_ref, rhs_ref, first_ref, sums, buffer, sems):
     parts = sums.shape[0]
     share = sums.shape[1] - 2
     copies = started(smooth_ref, buffer, sems, parts)
-    for part in range(parts):
-        sums[part] = got_ref[part, 0] + got_ref[part ^ 2, 1]
+    for k in range(2):
+        sums[device_at(pos, k, False)] = keep[k]
+        sums[device_at(pos, k, True)] = other[k]
     for part in range(parts):
         copies[part].wait()
         for i in range(share):
@@ -259,13 +280,15 @@
     next_ref,
     smooth_ref,
     weight_ref,
-    out_ref,
+    keep,
+    send,
+    slab,
     window,
     buffer,
     sems,
     window_sems,
 ):
-    parts, _, slots = out_ref.shape[:3]
+    parts, slots = slab.shape[:2]
     share = slots - 2
     total = window.shape[0] // 3
     copies = started(smooth_ref, buffer, sems, parts)
@@ -274,8 +297,8 @@
         target = window.at[pl.ds(pl.multiple_of(side * total, total), total)]
         moves.append(pltpu.make_async_copy(ref, target, window_sems.at[k]))
         moves[-1].start()
-    out_ref[0, 0, 0] = jnp.zeros_like(inner_ref[0])
-    out_ref[parts - 1, 0, share + 1] = jnp.zeros_like(inner_ref[0])
+    slab[0, 0] = jnp.zeros_like(inner_ref[0])
+    slab[parts - 1, share + 1] = jnp.zeros_like(inner_ref[0])
     for move in moves:
         move.wait()
     for part in range(parts):
@@ -287,25 +310,25 @@
                 at = nbr[a, n] - (pos[1] - 1) * total
                 value = value + weight_ref[a, n][None, :] * window[at]
             value = first_ref[a] + product(value, buffer[a])
-            out_ref[part, 0, i + 1] = value
+            slab[part, i + 1] = value
             if i == 0 and part > 0:
-                out_ref[part - 1, 0, share + 1] = value
+                slab[part - 1, share + 1] = value
             if i == share - 1 and part < parts - 1:
-                out_ref[part + 1, 0, 0] = value
-    for part in range(parts):
-        out_ref[part ^ 2, 1] = out_ref[part, 0]
-
-
-def fill_table(pos, pair_ref, own_ref, next_ref, table):
-    parts, _, rows, _ = own_ref.shape
-    for side, flip, ref in (
-        (pos[4], 1 - pos[3], pair_ref),
-        (1, pos[3], own_ref),
-        (2 - pos[4], 1 - pos[3], next_ref),
+                slab[part + 1, 0] = value
+    for k in range(2):
+        keep[k] = slab[device_at(pos, k, False)]
+        send[k] = slab[device_at(pos, k, True)]
+
+
+def fill_table(pos, refs, table):
+    rows = refs[0].shape[2]
+    for k, (side, flip) in enumerate(
+        ((pos[4], 1 - pos[3]), (1, pos[3]), (2 - pos[4], 1 - pos[3]))
     ):
-        for part in range(parts):
-            at = pl.multiple_of(quarter(flip, part) * rows, rows)
-            table[side, :, pl.ds(at, rows)] = ref[part]
+        for j, chip in enumerate((pos[5], 1 - pos[5])):
+            for c, core in enumerate((pos[2], 1 - pos[2])):
+                at = pl.multiple_of(quarter(flip, chip, core) * rows, rows)
+                table[side, :, pl.ds(at, rows)] = refs[2 * k + j][c]
 
 
 def corrected(pos, owner, agg, table, fine, weight, p, b):
@@ -315,15 +338,16 @@
 
 
 def rim_kernel(
-    pos, owner, agg, fine_ref, w_ref, pair_ref, own_ref, next_ref, y_pair, y_next, table, col_buf, sems
+    pos, owner, agg, fine_ref, w_ref, *refs
 ):
+    messages, (y_pair, y_next, table, col_buf, sems) = refs[:6], refs[6:]
     blocks_x, blocks_y = w_ref.shape[:2]
     copies = []
     for k in range(2):
         source = fine_ref.at[:, k * (blocks_y - 1)]
         copies.append(pltpu.make_async_copy(source, col_buf.at[k], sems.at[k]))
         copies[-1].start()
-    fill_table(pos, pair_ref, own_ref, next_ref, table)
+    fill_table(pos, messages, table)
     for copy in copies:
         copy.wait()
     pair_at = jnp.where(pos[4] == 2, 1, 0)
@@ -342,16 +366,9 @@
     r_ref,
     diag_ref,
     face_ref,
-    pair_ref,
-    own_ref,
-    next_ref,
-    out_ref,
-    res_ref,
-    inner,
-    outer,
-    table,
-    solved,
+    *refs,
 ):
+    messages, (out_ref, res_ref, inner, outer, table, solved) = refs[:6], refs[6:]
     s = pl.program_id(0)
     last = pl.num_programs(0) - 1
     per, blocks_y = fine_ref.shape[:2]
@@ -359,7 +376,7 @@
 
     @pl.when(s == 0)
     def _():
-        fill_table(pos, pair_ref, own_ref, next_ref, table)
+        fill_table(pos, messages, table)
         solved[0] = jnp.zeros_like(solved[0])
         solved[blocks_x + 1] = jnp.zeros_like(solved[0])
 
@@ -444,7 +461,7 @@
 
 
 def y_halo(y_pair, y_next):
-    return in_pair(y_pair), moved_to(y_next, lambda x, y: (x, ((y + 1) ^ 1) - 1))
+    return in_pair(y_pair), between_pairs(y_next)
 
 
 def body(
@@ -470,7 +487,7 @@
     fine_shape = right_side.shape
     mat_shape = diag_blocks.shape
     slab = (parts, share + 2, rows // parts, size)
-    double = (parts, 2) + slab[1:]
+    message = (2,) + slab[1:]
     coarse_shape = (total, rows // parts, size)
     x_face = (blocks_y, rows, size)
     y_face = (blocks_x, rows, size)
@@ -492,14 +509,14 @@
     face_shapes = [like(x_face)] * 2 + [like(y_face)] * 2
 
     gx, gy = lax.axis_index("gx"), lax.axis_index("gy")
-    pos = jnp.stack([gx * share, gy, gx % 2, gy % 2, 2 * (1 - gy % 2)]).astype(jnp.int32)
-
-    to_pair, own, to_next = call(
+    pos = jnp.stack([gx * share, gy, gx % 2, gy % 2, 2 * (1 - gy % 2), gx // 2]).astype(jnp.int32)
+
+    pair_s, pair_x, own_s, own_x, next_s, next_x = call(
         restrict_kernel,
         1,
         [hbm, whole(restrict_weight.shape)],
-        [vmem] * 3,
-        [like(slab)] * 3,
+        [vmem] * 6,
+        [like(message)] * 6,
         scalars=3,
         scratch=[
             pltpu.VMEM((3, share + 2, rows, size), F32),
@@ -509,8 +526,14 @@
         moved=2 * fine_bytes,
     )(pos, block_owner, block_aggregate, right_side, restrict_weight)
 
-    from_pair = in_pair(to_pair)
-    from_next = between_pairs(to_next)
+    sums = (
+        in_pair(pair_s),
+        own_s,
+        between_pairs(next_s),
+        in_pair_crossed(pair_x),
+        to_partner(own_x),
+        between_pairs_crossed(next_x),
+    )
 
     sweep, *faces = call(
         sweep_kernel,
@@ -523,28 +546,34 @@
         moved=3 * fine_bytes,
     )(pos, right_side, smoother)
 
-    own, from_pair, from_next, sweep_x = lax.optimization_barrier(
-        (own, from_pair, from_next, x_halo(*faces[:2]))
-    )
-    got = lax.all_to_all(
-        jnp.stack([own + from_pair, from_next], axis=1), "gx", 0, 0, tiled=True
-    )
+    sums, sweep = lax.optimization_barrier((sums, sweep))
+    keep, send = call(
+        gather_kernel,
+        1,
+        [vmem] * 6,
+        [vmem] * 2,
+        [like(message)] * 2,
+        scalars=1,
+        moved=coarse_bytes,
+    )(pos, *sums)
+    other, sweep_x = lax.optimization_barrier((to_sibling(send), x_halo(*faces[:2])))
 
     rhs, first = call(
         coarse_first_kernel,
         1,
-        [vmem, hbm],
+        [vmem, vmem, hbm],
         [vmem] * 2,
         [like(coarse_shape)] * 2,
+        scalars=1,
         scratch=[pltpu.VMEM(slab, F32)] + cmat_scratch,
         flops=coarse_flops,
         moved=coarse_bytes,
-    )(got, coarse_smooth)
+    )(pos, keep, other, coarse_smooth)
 
     first, rhs, y_faces = lax.optimization_barrier((first, rhs, faces[2:]))
     sweep_y = y_halo(*y_faces)
     pair_first = in_pair_crossed(first)
-    next_first = between_pairs(first)
+    next_first = between_pairs_crossed(first)
 
     inner = call(
         coarse_own_kernel,
@@ -557,23 +586,32 @@
         moved=coarse_bytes,
     )(rhs, first, coarse_diag)
 
-    corr = call(
+    keep, send = call(
         coarse_last_kernel,
         1,
         [vmem] * 4 + [hbm, vmem],
-        vmem,
-        like(double),
+        [vmem] * 2,
+        [like(message)] * 2,
         scalars=2,
-        scratch=[pltpu.VMEM((3 * total,) + coarse_shape[1:], F32)]
+        scratch=[pltpu.VMEM(slab, F32), pltpu.VMEM((3 * total,) + coarse_shape[1:], F32)]
         + cmat_scratch
         + [pltpu.SemaphoreType.DMA((3,))],
         flops=coarse_flops,
         moved=coarse_bytes,
     )(pos, neighbors, inner, pair_first, first, next_first, coarse_smooth, neighbor_weight)
 
-    corr, sweep_y = lax.optimization_barrier((corr, sweep_y))
-    mine = lax.all_to_all(corr, "gx", 0, 0, tiled=True)
-    tables = (in_pair(mine[:, 0]), mine[:, 0], between_pairs(mine[:, 1]))
+    send, sweep_y = lax.optimization_barrier((send, sweep_y))
+    other = to_sibling(send)
+    mine = jnp.stack([keep[0], other[0]])
+    partners = jnp.stack([keep[1], other[1]])
+    tables = (
+        in_pair(mine),
+        in_pair_crossed(partners),
+        mine,
+        to_partner(partners),
+        between_pairs(mine),
+        between_pairs_crossed(partners),
+    )
 
     fine_part = call(
         fine_kernel,
@@ -592,7 +630,7 @@
     rim = call(
         rim_kernel,
         1,
-        [hbm, whole(prolong_weight.shape)] + [vmem] * 3,
+        [hbm, whole(prolong_weight.shape)] + [vmem] * 6,
         [vmem] * 2,
         [like(y_face)] * 2,
         scalars=3,
@@ -627,7 +665,7 @@
             previous(mat_shape),
             previous(face_weight.shape),
         ]
-        + [vmem] * 3,
+        + [vmem] * 6,
         [now(fine_shape), previous(fine_shape)] + [vmem] * 2,
         [like(fine_shape)] * 2 + [like(x_face)] * 2,
         scalars=3,

time: 175 us -> 157 us (0.90)
  blocking collectives: 42.7 us -> 0 us
  starting transfers between devices: 32.3 us -> 53.5 us
  waiting for transfers between devices: 50.3 us -> 56.3 us
  local copies, waits for them, and re-layouts: 8.56 us -> 6.51 us
    all_to_all x2 -> x0, blocking collectives: 42.7 us -> none  [the longest x1 22.4 us: body(): mine = lax.all_to_all(corr, 'gx', 0, 0, tiled=True)]
    ppermute x14 -> x22, starting transfers between devices: 32.3 us -> 53.5 us  [moved_to(): return lax.ppermute(array, ('gx', 'gy'), pairs)]
    ppermute x14 -> x22, waiting for transfers between devices: 50.3 us -> 56.3 us  [moved_to(): return lax.ppermute(array, ('gx', 'gy'), pairs)]
    unnamed x46, local copies, waits for them, and re-layouts: 8.38 us -> 6.38 us
    pallas_call x4 -> x5, Pallas kernels: 10.3 us -> 11 us  [the longest x1 4.27 us: body(): call(coarse_last_kernel, 1, [vmem] * 4 + [hbm, vmem], [vmem] * 2, [like(m...]
  transfers between devices with their start and end apart: 14 -> 22, of which waited for: 5 -> 8; matrix products, arithmetic and copies ran while one was open for 0% -> 0% of each run, Pallas kernels for 17% -> 19%
where the time goes in v4:
time: 157 us; the launch traced here: 156 us
  waiting for transfers between devices  56.3 us (36%)
  starting transfers between devices  53.5 us (34%)
  Pallas kernels  38.5 us (25%)
  local copies, waits for them, and re-layouts  6.51 us (4%)
    ppermute x22, waiting for transfers between devices, moved_to(): return lax.ppermute(array, ('gx', 'gy'), pairs)  56.3 us
    ppermute x22, starting transfers between devices, moved_to(): return lax.ppermute(array, ('gx', 'gy'), pairs)  53.5 us
    pallas_call x1, Pallas kernels, body(): call(fine_kernel, steps, [fine_block] + [mat_block] * 2 + [weight_block,...  9.71 us
    pallas_call x1, Pallas kernels, body(): call(finish_kernel, steps + 1, [now(fine_shape), now(prolong_weight.shape...  7.24 us
    unnamed x46, local copies, waits for them, and re-layouts  6.38 us
    pallas_call x1, Pallas kernels, body(): call(coarse_last_kernel, 1, [vmem] * 4 + [hbm, vmem], [vmem] * 2, [like(m...  4.27 us
    pallas_call x1, Pallas kernels, body(): call(sweep_kernel, steps, [fine_block, mat_block], [fine_block] + face_sp...  4.1 us
    pallas_call x1, Pallas kernels, body(): call(border_kernel, 1, [hbm, whole(face_weight.shape)] + [vmem] * 4, hbm,...  3.52 us
  transfers between devices with their start and end apart: 22, of which 8 were waited for; matrix products, arithmetic and copies ran while one was open for 0% of the time, Pallas kernels for 19%

profile of v4, /device:TPU:1, one launch (start us, length us, event | category | flops | bytes accessed | tf_op | source)
XLA Modules:
  0.0 155.9 jit_solution(10412438289430417943)
XLA Ops:
  0.7 2.2 %copy-done = f32[8,8,128,128]{3,2,1,0:T(8,128)S(1)} copy-done((f32[8,8,128,128]{3,2,1,0:T(8,128)S(1)}, f32[8,8,128,128]{3,2,1,0:T(8,128)}, u32[]{:S(2)}) %copy-start) | copy-done | bytes 4194328
  6.9 2.2 %collective-permute-start = (f32[2,10,32,128]{3,2,1,0:T(8,128)S(1)}, f32[2,10,32,128]{3,2,1,0:T(8,128)S(1)}, u32[]{:S(2)}, u32[]{:S(2)}) collective-permute-start(f32[2,10,32,128]{3,2,1,0:T(8,128)S(1)} %get-tuple-element.42), channel_id=1, source_target_pairs={{0,1},{1,0},{2,3},{3,2},{4,5},{5,4},{6,7},{7,6},{8,9},{9,8},{10,11... | collective-permute-start | bytes 983048 | tf_op jit(solution)/shard_map/ppermute | solution.py:22
  9.8 5.6 %collective-permute-start.2 = (f32[2,10,32,128]{3,2,1,0:T(8,128)S(1)}, f32[2,10,32,128]{3,2,1,0:T(8,128)S(1)}, u32[]{:S(2)}, u32[]{:S(2)}) collective-permute-start(f32[2,10,32,128]{3,2,1,0:T(8,128)S(1)} %get-tuple-element.45), channel_id=1, source_target_pairs={{0,65},{1,64},{2,67},{3,66},{4,69},{5,68},{6,71},{7,70},{8,73},{9,... | collective-permute-start | bytes 983048 | tf_op jit(solution)/shard_map/ppermute | solution.py:22
  16.5 4.1 %shard_map.132 = (f32[8,8,128,128]{3,2,1,0:T(8,128)S(1)}, f32[8,128,128]{2,1,0:T(8,128)S(1)}, f32[8,128,128]{2,1,0:T(8,128)S(1)}, f32[8,128,128]{2,1,0:T(8,128)S(1)}, f32[8,128,128]{2,1,0:T(8,128)S(1)}) custom-call(s32[6]{0:T(128)S(1)} %stack.33.pos, f32[8,8,128,128]{3,2,1,0:T(8,128)S(1)} %copy-done, f32[8,8,128,128]{3,2,1,0:T(8,128)S(1)} %copy-done.9), custom_call_target="tpu_custom_call" | custom-call | flops 42949672960 | bytes 503316480 | tf_op jit(solution)/shard_map/pallas_call | solution.py:538
  20.7 3.8 %collective-permute-start.6 = (f32[8,128,128]{2,1,0:T(8,128)S(1)}, f32[8,128,128]{2,1,0:T(8,128)S(1)}, u32[]{:S(2)}, u32[]{:S(2)}) collective-permute-start(f32[8,128,128]{2,1,0:T(8,128)S(1)} %get-tuple-element.57), channel_id=1, source_target_pairs={{0,32},{1,33},{2,34},{3,35},{4,36},{5,37},{6,38},{7,39},{8,40},{9,... | collective-permute-start | bytes 1572872 | tf_op jit(solution)/shard_map/ppermute | solution.py:22
  24.5 3.0 %collective-permute-start.7 = (f32[8,128,128]{2,1,0:T(8,128)S(1)}, f32[8,128,128]{2,1,0:T(8,128)S(1)}, u32[]{:S(2)}, u32[]{:S(2)}) collective-permute-start(f32[8,128,128]{2,1,0:T(8,128)S(1)} %get-tuple-element.58), channel_id=1, source_target_pairs={{32,64},{33,65},{34,66},{35,67},{36,68},{37,69},{38,70},{39,71},{4... | collective-permute-start | bytes 1572872 | tf_op jit(solution)/shard_map/ppermute | solution.py:22
  27.6 6.2 %collective-permute-done.3.own_x = f32[2,10,32,128]{3,2,1,0:T(8,128)S(1)} collective-permute-done((f32[2,10,32,128]{3,2,1,0:T(8,128)S(1)}, f32[2,10,32,128]{3,2,1,0:T(8,128)S(1)}, u32[]{:S(2)}, u32[]{:S(2)}) %collective-permute-start.3) | collective-permute-done | bytes 327712 | tf_op jit(solution)/shard_map/ppermute | solution.py:22
  34.4 9.3 %collective-permute-start.5 = (f32[2,10,32,128]{3,2,1,0:T(8,128)S(1)}, f32[2,10,32,128]{3,2,1,0:T(8,128)S(1)}, u32[]{:S(2)}, u32[]{:S(2)}) collective-permute-start(f32[2,10,32,128]{3,2,1,0:T(8,128)S(1)} %get-tuple-element.56), channel_id=1, source_target_pairs={{0,32},{1,33},{2,34},{3,35},{4,36},{5,37},{6,38},{7,39},{8,40},{9,... | collective-permute-start | bytes 983048 | tf_op jit(solution)/shard_map/ppermute | solution.py:22
  45.0 3.3 %shard_map.134 = (f32[32,32,128]{2,1,0:T(8,128)S(1)}, f32[32,32,128]{2,1,0:T(8,128)}) custom-call(s32[6]{0:T(128)S(1)} %stack.33.pos, f32[2,10,32,128]{3,2,1,0:T(8,128)S(1)} %get-tuple-element.61.keep, f32[2,10,32,128]{3,2,1,0:T(8,128)S(1)} %collective-permute-done.5.other, f32[32,128,128]{2,1,0:T(8,128)S(1)} %copy-done.13), custom_call_target="tpu_custom_call" | custom-call | flops 5368709120 | bytes 83886080 | tf_op jit(solution)/shard_map/pallas_call | solution.py:561
  50.5 5.3 %collective-permute-start.8 = (f32[32,32,128]{2,1,0:T(8,128)}, f32[32,32,128]{2,1,0:T(8,128)}, u32[]{:S(2)}, u32[]{:S(2)}) collective-permute-start(f32[32,32,128]{2,1,0:T(8,128)} %get-tuple-element.68.first_ref), channel_id=1, source_target_pairs={{0,65},{1,64},{2,67},{3,66},{4,69},{5,68},{6,71},{7,70},{8,73},{9,... | collective-permute-start | bytes 1572872 | tf_op jit(solution)/shard_map/ppermute | solution.py:22
  58.0 2.9 %shard_map.135.inner_ref = f32[32,32,128]{2,1,0:T(8,128)S(1)} custom-call(f32[32,32,128]{2,1,0:T(8,128)S(1)} %copy-done.18, f32[32,32,128]{2,1,0:T(8,128)} %get-tuple-element.68.first_ref, f32[32,128,128]{2,1,0:T(8,128)S(1)} %copy-done.12), custom_call_target="tpu_custom_call" | custom-call | flops 5368709120 | bytes 83886080 | tf_op jit(solution)/shard_map/pallas_call | solution.py:578
  60.9 18.3 %collective-permute-done.8.pair_ref = f32[32,32,128]{2,1,0:T(8,128)} collective-permute-done((f32[32,32,128]{2,1,0:T(8,128)}, f32[32,32,128]{2,1,0:T(8,128)}, u32[]{:S(2)}, u32[]{:S(2)}) %collective-permute-start.8) | collective-permute-done | bytes 524320 | tf_op jit(solution)/shard_map/ppermute | solution.py:22
  79.3 4.3 %shard_map.136 = (f32[2,10,32,128]{3,2,1,0:T(8,128)S(1)}, f32[2,10,32,128]{3,2,1,0:T(8,128)S(1)}) custom-call(s32[6]{0:T(128)S(1)} %stack.33.pos, s32[32,6]{1,0:T(8,128)S(1)} %copy.15.nbr, f32[32,32,128]{2,1,0:T(8,128)S(1)} %shard_map.135.inner_ref, f32[32,32,128]{2,1,0:T(8,128)} %collective-permute-done.8.pair_ref, ...), custom_call_target="tpu_custom_call" | custom-call | flops 5368709120 | bytes 83886080 | tf_op jit(solution)/shard_map/pallas_call | solution.py:589
  86.5 3.8 %collective-permute-start.13 = (f32[2,10,32,128]{3,2,1,0:T(8,128)S(1)}, f32[2,10,32,128]{3,2,1,0:T(8,128)S(1)}, u32[]{:S(2)}, u32[]{:S(2)}) collective-permute-start(f32[2,10,32,128]{3,2,1,0:T(8,128)S(1)} %pad_maximum_fusion.refs_2_), channel_id=1, source_target_pairs={{0,1},{1,0},{2,3},{3,2},{4,5},{5,4},{6,7},{7,6},{8,9},{9,8},{10,11... | collective-permute-start | bytes 983048 | tf_op jit(solution)/shard_map/ppermute | solution.py:22
  91.8 5.0 %collective-permute-start.14 = (f32[2,10,32,128]{3,2,1,0:T(8,128)S(1)}, f32[2,10,32,128]{3,2,1,0:T(8,128)S(1)}, u32[]{:S(2)}, u32[]{:S(2)}) collective-permute-start(f32[2,10,32,128]{3,2,1,0:T(8,128)S(1)} %pad_maximum_fusion.1), channel_id=1, source_target_pairs={{0,65},{1,64},{2,67},{3,66},{4,69},{5,68},{6,71},{7,70},{8,73},{9,... | collective-permute-start | bytes 983048 | tf_op jit(solution)/shard_map/ppermute | solution.py:22
  96.9 9.7 %shard_map.137.fine_ref = f32[8,8,128,128]{3,2,1,0:T(8,128)S(1)} custom-call(s32[6]{0:T(128)S(1)} %stack.33.pos, f32[8,8,128,128]{3,2,1,0:T(8,128)S(1)} %copy-done.1, f32[8,8,128,128]{3,2,1,0:T(8,128)S(1)} %copy-done.10, f32[8,8,128,128]{3,2,1,0:T(8,128)S(1)} %copy-done.11, f32[8,8,4,128]{3,2,1,0:T(4,128)S(1)} %copy-done.2, f32[8,8,128,128]{3,2,1,0:T(8,128)} %copy-done.19, ...), custom_call_target="tpu_custom_call" | custom-call | flops 85899345920 | bytes 838860800 | tf_op jit(solution)/shard_map/pallas_call | solution.py:616
  106.6 5.5 %collective-permute-done.15.refs_3_ = f32[2,10,32,128]{3,2,1,0:T(8,128)S(1)} collective-permute-done((f32[2,10,32,128]{3,2,1,0:T(8,128)S(1)}, f32[2,10,32,128]{3,2,1,0:T(8,128)S(1)}, u32[]{:S(2)}, u32[]{:S(2)}) %collective-permute-start.15) | collective-permute-done | bytes 327712 | tf_op jit(solution)/shard_map/ppermute | solution.py:22
  112.1 6.0 %collective-permute-done.14.refs_1_ = f32[2,10,32,128]{3,2,1,0:T(8,128)S(1)} collective-permute-done((f32[2,10,32,128]{3,2,1,0:T(8,128)S(1)}, f32[2,10,32,128]{3,2,1,0:T(8,128)S(1)}, u32[]{:S(2)}, u32[]{:S(2)}) %collective-permute-start.14) | collective-permute-done | bytes 327712 | tf_op jit(solution)/shard_map/ppermute | solution.py:22
  120.5 7.2 %shard_map.138 = (f32[8,8,128,128]{3,2,1,0:T(8,128)}, f32[8,8,128,128]{3,2,1,0:T(8,128)}, f32[8,128,128]{2,1,0:T(8,128)S(1)}, f32[8,128,128]{2,1,0:T(8,128)S(1)}) custom-call(s32[6]{0:T(128)S(1)} %stack.33.pos, s32[8,8]{1,0:T(8,128)S(1)} %copy-done.6, s32[8,8]{1,0:T(8,128)S(1)} %copy-done.8, f32[8,8,128,128]{3,2,1,0:T(8,128)S(1)} %shard_map.137.fine_ref, ...), custom_call_target="tpu_custom_call" | custom-call | flops 42949672960 | bytes 838860800 | tf_op jit(solution)/shard_map/pallas_call | solution.py:658
  127.7 2.5 %collective-permute-start.18 = (f32[8,128,128]{2,1,0:T(8,128)S(1)}, f32[8,128,128]{2,1,0:T(8,128)S(1)}, u32[]{:S(2)}, u32[]{:S(2)}) collective-permute-start(f32[8,128,128]{2,1,0:T(8,128)S(1)} %get-tuple-element.78), channel_id=1, source_target_pairs={{0,32},{1,33},{2,34},{3,35},{4,36},{5,37},{6,38},{7,39},{8,40},{9,... | collective-permute-start | bytes 1572872 | tf_op jit(solution)/shard_map/ppermute | solution.py:22
  130.2 4.3 %collective-permute-start.19 = (f32[8,128,128]{2,1,0:T(8,128)S(1)}, f32[8,128,128]{2,1,0:T(8,128)S(1)}, u32[]{:S(2)}, u32[]{:S(2)}) collective-permute-start(f32[8,128,128]{2,1,0:T(8,128)S(1)} %get-tuple-element.79), channel_id=1, source_target_pairs={{32,64},{33,65},{34,66},{35,67},{36,68},{37,69},{38,70},{39,71},{4... | collective-permute-start | bytes 1572872 | tf_op jit(solution)/shard_map/ppermute | solution.py:22
  134.5 5.5 %collective-permute-done.20.y_pair = f32[8,128,128]{2,1,0:T(8,128)S(1)} collective-permute-done((f32[8,128,128]{2,1,0:T(8,128)S(1)}, f32[8,128,128]{2,1,0:T(8,128)S(1)}, u32[]{:S(2)}, u32[]{:S(2)}) %collective-permute-start.20) | collective-permute-done | bytes 524320 | tf_op jit(solution)/shard_map/ppermute | solution.py:22
  140.1 12.3 %collective-permute-done.19.x_outer = f32[8,128,128]{2,1,0:T(8,128)S(1)} collective-permute-done((f32[8,128,128]{2,1,0:T(8,128)S(1)}, f32[8,128,128]{2,1,0:T(8,128)S(1)}, u32[]{:S(2)}, u32[]{:S(2)}) %collective-permute-start.19) | collective-permute-done | bytes 524320 | tf_op jit(solution)/shard_map/ppermute | solution.py:22
  152.3 3.5 %shard_map.140 = f32[8,8,128,128]{3,2,1,0:T(8,128)} custom-call(s32[6]{0:T(128)S(1)} %stack.33.pos, f32[8,8,128,128]{3,2,1,0:T(8,128)} %get-tuple-element.77.part_ref, f32[8,8,4,128]{3,2,1,0:T(4,128)S(1)} %copy-done.2, f32[8,128,128]{2,1,0:T(8,128)S(1)} %collective-permute-done.18.x_inner, ...), custom_call_target="tpu_custom_call", output_to_operand_aliasing={{}: (1, {})} | custom-call | bytes 167772160 | tf_op jit(solution)/shard_map/pallas_call | solution.py:690
  (81 shorter events, 19.0 us)
Async XLA Ops:
  6.9 13.8 %collective-permute-start = (f32[2,10,32,128]{3,2,1,0:T(8,128)S(1)}, f32[2,10,32,128]{3,2,1,0:T(8,128)S(1)}, u32[]{:S(2)}, u32[]{:S(2)}) collective-permute-start(f32[2,10,32,128]{3,2,1,0:T(8,128)S(1)} %get-tuple-element.42), channel_id=1, source_target_pairs={{0,1},{1,0},{2,3},{3,2},{4,5},{5,4},{6,7},{7,6},{8,9},{9,8},{10,11... | collective-permute-start | bytes 983048 | tf_op jit(solution)/shard_map/ppermute | solution.py:22
  9.1 15.4 %collective-permute-start.1 = (f32[2,10,32,128]{3,2,1,0:T(8,128)S(1)}, f32[2,10,32,128]{3,2,1,0:T(8,128)S(1)}, u32[]{:S(2)}, u32[]{:S(2)}) collective-permute-start(f32[2,10,32,128]{3,2,1,0:T(8,128)S(1)} %get-tuple-element.44), channel_id=1, source_target_pairs={{1,2},{2,1},{3,4},{4,3},{5,6},{6,5},{7,8},{8,7},{9,10},{10,9},{11,... | collective-permute-start | bytes 983048 | tf_op jit(solution)/shard_map/ppermute | solution.py:22
  9.8 17.8 %collective-permute-start.2 = (f32[2,10,32,128]{3,2,1,0:T(8,128)S(1)}, f32[2,10,32,128]{3,2,1,0:T(8,128)S(1)}, u32[]{:S(2)}, u32[]{:S(2)}) collective-permute-start(f32[2,10,32,128]{3,2,1,0:T(8,128)S(1)} %get-tuple-element.45), channel_id=1, source_target_pairs={{0,65},{1,64},{2,67},{3,66},{4,69},{5,68},{6,71},{7,70},{8,73},{9,... | collective-permute-start | bytes 983048 | tf_op jit(solution)/shard_map/ppermute | solution.py:22
  15.4 18.4 %collective-permute-start.3 = (f32[2,10,32,128]{3,2,1,0:T(8,128)S(1)}, f32[2,10,32,128]{3,2,1,0:T(8,128)S(1)}, u32[]{:S(2)}, u32[]{:S(2)}) collective-permute-start(f32[2,10,32,128]{3,2,1,0:T(8,128)S(1)} %get-tuple-element.46), channel_id=1, source_target_pairs={{0,64},{1,65},{2,66},{3,67},{4,68},{5,69},{6,70},{7,71},{8,72},{9,... | collective-permute-start | bytes 983048 | tf_op jit(solution)/shard_map/ppermute | solution.py:22
  15.7 18.0 %collective-permute-start.4 = (f32[2,10,32,128]{3,2,1,0:T(8,128)S(1)}, f32[2,10,32,128]{3,2,1,0:T(8,128)S(1)}, u32[]{:S(2)}, u32[]{:S(2)}) collective-permute-start(f32[2,10,32,128]{3,2,1,0:T(8,128)S(1)} %get-tuple-element.47), channel_id=1, source_target_pairs={{1,66},{2,65},{3,68},{4,67},{5,70},{6,69},{7,72},{8,71},{9,74},{10... | collective-permute-start | bytes 983048 | tf_op jit(solution)/shard_map/ppermute | solution.py:22
  20.7 23.0 %collective-permute-start.6 = (f32[8,128,128]{2,1,0:T(8,128)S(1)}, f32[8,128,128]{2,1,0:T(8,128)S(1)}, u32[]{:S(2)}, u32[]{:S(2)}) collective-permute-start(f32[8,128,128]{2,1,0:T(8,128)S(1)} %get-tuple-element.57), channel_id=1, source_target_pairs={{0,32},{1,33},{2,34},{3,35},{4,36},{5,37},{6,38},{7,39},{8,40},{9,... | collective-permute-start | bytes 1572872 | tf_op jit(solution)/shard_map/ppermute | solution.py:22
  24.5 19.2 %collective-permute-start.7 = (f32[8,128,128]{2,1,0:T(8,128)S(1)}, f32[8,128,128]{2,1,0:T(8,128)S(1)}, u32[]{:S(2)}, u32[]{:S(2)}) collective-permute-start(f32[8,128,128]{2,1,0:T(8,128)S(1)} %get-tuple-element.58), channel_id=1, source_target_pairs={{32,64},{33,65},{34,66},{35,67},{36,68},{37,69},{38,70},{39,71},{4... | collective-permute-start | bytes 1572872 | tf_op jit(solution)/shard_map/ppermute | solution.py:22
  34.4 10.6 %collective-permute-start.5 = (f32[2,10,32,128]{3,2,1,0:T(8,128)S(1)}, f32[2,10,32,128]{3,2,1,0:T(8,128)S(1)}, u32[]{:S(2)}, u32[]{:S(2)}) collective-permute-start(f32[2,10,32,128]{3,2,1,0:T(8,128)S(1)} %get-tuple-element.56), channel_id=1, source_target_pairs={{0,32},{1,33},{2,34},{3,35},{4,36},{5,37},{6,38},{7,39},{8,40},{9,... | collective-permute-start | bytes 983048 | tf_op jit(solution)/shard_map/ppermute | solution.py:22
  49.1 11.8 %collective-permute-start.9 = (f32[32,32,128]{2,1,0:T(8,128)}, f32[32,32,128]{2,1,0:T(8,128)}, u32[]{:S(2)}, u32[]{:S(2)}) collective-permute-start(f32[32,32,128]{2,1,0:T(8,128)} %get-tuple-element.68.first_ref), channel_id=1, source_target_pairs={{1,66},{2,65},{3,68},{4,67},{5,70},{6,69},{7,72},{8,71},{9,74},{10... | collective-permute-start | bytes 1572872 | tf_op jit(solution)/shard_map/ppermute | solution.py:22
  50.5 28.7 %collective-permute-start.8 = (f32[32,32,128]{2,1,0:T(8,128)}, f32[32,32,128]{2,1,0:T(8,128)}, u32[]{:S(2)}, u32[]{:S(2)}) collective-permute-start(f32[32,32,128]{2,1,0:T(8,128)} %get-tuple-element.68.first_ref), channel_id=1, source_target_pairs={{0,65},{1,64},{2,67},{3,66},{4,69},{5,68},{6,71},{7,70},{8,73},{9,... | collective-permute-start | bytes 1572872 | tf_op jit(solution)/shard_map/ppermute | solution.py:22
  56.0 27.5 %collective-permute-start.10 = (f32[8,128,128]{2,1,0:T(8,128)}, f32[8,128,128]{2,1,0:T(8,128)S(1)}, u32[]{:S(2)}, u32[]{:S(2)}) collective-permute-start(f32[8,128,128]{2,1,0:T(8,128)} %copy-done.16), channel_id=1, source_target_pairs={{0,1},{1,0},{2,3},{3,2},{4,5},{5,4},{6,7},{7,6},{8,9},{9,8},{10,11... | collective-permute-start | bytes 1572872 | tf_op jit(solution)/shard_map/ppermute | solution.py:22
  56.1 27.5 %collective-permute-start.11 = (f32[8,128,128]{2,1,0:T(8,128)}, f32[8,128,128]{2,1,0:T(8,128)S(1)}, u32[]{:S(2)}, u32[]{:S(2)}) collective-permute-start(f32[8,128,128]{2,1,0:T(8,128)} %copy-done.15), channel_id=1, source_target_pairs={{1,2},{2,1},{3,4},{4,3},{5,6},{6,5},{7,8},{8,7},{9,10},{10,9},{11,... | collective-permute-start | bytes 1572872 | tf_op jit(solution)/shard_map/ppermute | solution.py:22
  60.9 36.0 %copy-start.1 = (f32[8,8,128,128]{3,2,1,0:T(8,128)S(1)}, f32[8,8,128,128]{3,2,1,0:T(8,128)}, u32[]{:S(2)}) copy-start(f32[8,8,128,128]{3,2,1,0:T(8,128)} %r_ref.7) | copy-start | bytes 12582916
  60.9 36.0 %copy-start.2 = (f32[8,8,4,128]{3,2,1,0:T(4,128)S(1)}, f32[8,8,4,128]{3,2,1,0:T(4,128)}, u32[]{:S(2)}) copy-start(f32[8,8,4,128]{3,2,1,0:T(4,128)} %face_ref.5) | copy-start | bytes 393220
  83.6 2.2 %collective-permute-start.12 = (f32[2,10,32,128]{3,2,1,0:T(8,128)S(1)}, f32[2,10,32,128]{3,2,1,0:T(8,128)S(1)}, u32[]{:S(2)}, u32[]{:S(2)}) collective-permute-start(f32[2,10,32,128]{3,2,1,0:T(8,128)S(1)} %get-tuple-element.75), channel_id=1, source_target_pairs={{0,32},{1,33},{2,34},{3,35},{4,36},{5,37},{6,38},{7,39},{8,40},{9,... | collective-permute-start | bytes 983048 | tf_op jit(solution)/shard_map/ppermute | solution.py:22
  85.8 20.7 %collective-permute-start.16 = (f32[2,10,32,128]{3,2,1,0:T(8,128)S(1)}, f32[2,10,32,128]{3,2,1,0:T(8,128)S(1)}, u32[]{:S(2)}, u32[]{:S(2)}) collective-permute-start(f32[2,10,32,128]{3,2,1,0:T(8,128)S(1)} %pad_maximum_fusion.refs_2_), channel_id=1, source_target_pairs={{1,2},{2,1},{3,4},{4,3},{5,6},{6,5},{7,8},{8,7},{9,10},{10,9},{11,... | collective-permute-start | bytes 983048 | tf_op jit(solution)/shard_map/ppermute | solution.py:22
  86.5 20.1 %collective-permute-start.13 = (f32[2,10,32,128]{3,2,1,0:T(8,128)S(1)}, f32[2,10,32,128]{3,2,1,0:T(8,128)S(1)}, u32[]{:S(2)}, u32[]{:S(2)}) collective-permute-start(f32[2,10,32,128]{3,2,1,0:T(8,128)S(1)} %pad_maximum_fusion.refs_2_), channel_id=1, source_target_pairs={{0,1},{1,0},{2,3},{3,2},{4,5},{5,4},{6,7},{7,6},{8,9},{9,8},{10,11... | collective-permute-start | bytes 983048 | tf_op jit(solution)/shard_map/ppermute | solution.py:22
  90.4 16.2 %collective-permute-start.17 = (f32[2,10,32,128]{3,2,1,0:T(8,128)S(1)}, f32[2,10,32,128]{3,2,1,0:T(8,128)S(1)}, u32[]{:S(2)}, u32[]{:S(2)}) collective-permute-start(f32[2,10,32,128]{3,2,1,0:T(8,128)S(1)} %pad_maximum_fusion.1), channel_id=1, source_target_pairs={{1,66},{2,65},{3,68},{4,67},{5,70},{6,69},{7,72},{8,71},{9,74},{10... | collective-permute-start | bytes 983048 | tf_op jit(solution)/shard_map/ppermute | solution.py:22
  91.2 20.9 %collective-permute-start.15 = (f32[2,10,32,128]{3,2,1,0:T(8,128)S(1)}, f32[2,10,32,128]{3,2,1,0:T(8,128)S(1)}, u32[]{:S(2)}, u32[]{:S(2)}) collective-permute-start(f32[2,10,32,128]{3,2,1,0:T(8,128)S(1)} %pad_maximum_fusion.1), channel_id=1, source_target_pairs={{0,64},{1,65},{2,66},{3,67},{4,68},{5,69},{6,70},{7,71},{8,72},{9,... | collective-permute-start | bytes 983048 | tf_op jit(solution)/shard_map/ppermute | solution.py:22
  91.8 26.2 %collective-permute-start.14 = (f32[2,10,32,128]{3,2,1,0:T(8,128)S(1)}, f32[2,10,32,128]{3,2,1,0:T(8,128)S(1)}, u32[]{:S(2)}, u32[]{:S(2)}) collective-permute-start(f32[2,10,32,128]{3,2,1,0:T(8,128)S(1)} %pad_maximum_fusion.1), channel_id=1, source_target_pairs={{0,65},{1,64},{2,67},{3,66},{4,69},{5,68},{6,71},{7,70},{8,73},{9,... | collective-permute-start | bytes 983048 | tf_op jit(solution)/shard_map/ppermute | solution.py:22
  119.1 21.0 %collective-permute-start.20 = (f32[8,128,128]{2,1,0:T(8,128)S(1)}, f32[8,128,128]{2,1,0:T(8,128)S(1)}, u32[]{:S(2)}, u32[]{:S(2)}) collective-permute-start(f32[8,128,128]{2,1,0:T(8,128)S(1)} %get-tuple-element.80), channel_id=1, source_target_pairs={{0,1},{1,0},{2,3},{3,2},{4,5},{5,4},{6,7},{7,6},{8,9},{9,8},{10,11... | collective-permute-start | bytes 1572872 | tf_op jit(solution)/shard_map/ppermute | solution.py:22
  119.8 20.3 %collective-permute-start.21 = (f32[8,128,128]{2,1,0:T(8,128)S(1)}, f32[8,128,128]{2,1,0:T(8,128)S(1)}, u32[]{:S(2)}, u32[]{:S(2)}) collective-permute-start(f32[8,128,128]{2,1,0:T(8,128)S(1)} %get-tuple-element.81), channel_id=1, source_target_pairs={{1,2},{2,1},{3,4},{4,3},{5,6},{6,5},{7,8},{8,7},{9,10},{10,9},{11,... | collective-permute-start | bytes 1572872 | tf_op jit(solution)/shard_map/ppermute | solution.py:22
  127.7 12.3 %collective-permute-start.18 = (f32[8,128,128]{2,1,0:T(8,128)S(1)}, f32[8,128,128]{2,1,0:T(8,128)S(1)}, u32[]{:S(2)}, u32[]{:S(2)}) collective-permute-start(f32[8,128,128]{2,1,0:T(8,128)S(1)} %get-tuple-element.78), channel_id=1, source_target_pairs={{0,32},{1,33},{2,34},{3,35},{4,36},{5,37},{6,38},{7,39},{8,40},{9,... | collective-permute-start | bytes 1572872 | tf_op jit(solution)/shard_map/ppermute | solution.py:22
  130.2 22.1 %collective-permute-start.19 = (f32[8,128,128]{2,1,0:T(8,128)S(1)}, f32[8,128,128]{2,1,0:T(8,128)S(1)}, u32[]{:S(2)}, u32[]{:S(2)}) collective-permute-start(f32[8,128,128]{2,1,0:T(8,128)S(1)} %get-tuple-element.79), channel_id=1, source_target_pairs={{32,64},{33,65},{34,66},{35,67},{36,68},{37,69},{38,70},{39,71},{4... | collective-permute-start | bytes 1572872 | tf_op jit(solution)/shard_map/ppermute | solution.py:22
  (20 other events, 341.7 us)

commit v5 on v4

--- a/solution.py
+++ b/solution.py
@@ -128,7 +128,7 @@
                 out_refs[2 * k + j][core] = acc[side, :, pl.ds(at, rows)]
 
 
-def gather_kernel(pos, pair_s, own_s, next_s, pair_x, own_x, next_x, keep, send):
+def gather_kernel(pos, pair_s, next_x, pair_x, next_s, own_x, own_s, keep, send):
     core = pos[2]
     for k, refs in enumerate(((pair_s, own_s, next_s), (pair_x, own_x, next_x))):
         for out, c in ((keep, core), (send, 1 - core)):
@@ -321,7 +321,9 @@
 
 
 def fill_table(pos, refs, table):
-    rows = refs[0].shape[2]
+    pair_s, next_x, pair_x, next_s, own_x, own_s = refs
+    refs = (pair_s, pair_x, own_s, own_x, next_s, next_x)
+    rows = own_s.shape[2]
     for k, (side, flip) in enumerate(
         ((pos[4], 1 - pos[3]), (1, pos[3]), (2 - pos[4], 1 - pos[3]))
     ):
@@ -414,42 +416,43 @@
                 res_ref[t, b] = value
 
 
-def border_kernel(
-    pos, part_ref, face_ref, x_inner, x_outer, y_pair, y_next, out_ref, row_buf, col_buf, sems
-):
-    blocks_x, blocks_y = face_ref.shape[:2]
-    core = pos[2]
-    ends = (0, blocks_x - 1)
-    sides = (0, blocks_y - 1)
-    inside = pl.ds(1, blocks_x - 2)
-    pairs = [(out_ref.at[p], row_buf.at[k]) for k, p in enumerate(ends)]
-    pairs += [(out_ref.at[inside, q], col_buf.at[k]) for k, q in enumerate(sides)]
-    loads = [pltpu.make_async_copy(a, b, sems.at[k]) for k, (a, b) in enumerate(pairs)]
+def updated(out_ref, views, buffer, sems, change):
+    loads = [pltpu.make_async_copy(v, buffer.at[k], sems.at[k]) for k, v in enumerate(views)]
     for load in loads:
         load.start()
-    for load in loads:
-        load.wait()
-    for k, p in enumerate(ends):
-        lower = core == k
-        for b in range(blocks_y):
-            beyond = jnp.where(lower, x_outer[b], x_inner[b])
-            row_buf[k, b] += face_ref[p, b, k][None, :] * beyond
-    even = pos[4] == 2
-    for k, q in enumerate(sides):
-        from_pair = even if k == 1 else jnp.logical_not(even)
-
-        def beyond_y(p):
-            return jnp.where(from_pair, y_pair[p], y_next[p])
-
-        for j, p in enumerate(ends):
-            row_buf[j, q] += face_ref[p, q, 2 + k][None, :] * beyond_y(p)
-        for p in range(1, blocks_x - 1):
-            col_buf[k, p - 1] += face_ref[p, q, 2 + k][None, :] * beyond_y(p)
-    stores = [pltpu.make_async_copy(b, a, sems.at[4 + k]) for k, (a, b) in enumerate(pairs)]
-    for store in stores:
-        store.start()
+    stores = []
+    for k, view in enumerate(views):
+        loads[k].wait()
+        for j in range(buffer.shape[1]):
+            buffer[k, j] += change(k, j)
+        stores.append(pltpu.make_async_copy(buffer.at[k], view, sems.at[2 + k]))
+        stores[-1].start()
     for store in stores:
         store.wait()
+
+
+def y_border_kernel(pos, part_ref, face_ref, y_pair, y_next, out_ref, buffer, sems):
+    blocks_y = face_ref.shape[1]
+    even = pos[4] == 2
+
+    def change(k, p):
+        from_pair = even if k == 1 else jnp.logical_not(even)
+        beyond = jnp.where(from_pair, y_pair[p], y_next[p])
+        return face_ref[p, k * (blocks_y - 1), 2 + k][None, :] * beyond
+
+    views = [out_ref.at[:, k * (blocks_y - 1)] for k in range(2)]
+    updated(out_ref, views, buffer, sems, change)
+
+
+def x_border_kernel(pos, part_ref, face_ref, x_inner, x_outer, out_ref, buffer, sems):
+    blocks_x = face_ref.shape[0]
+
+    def change(k, b):
+        beyond = jnp.where(pos[2] == k, x_outer[b], x_inner[b])
+        return face_ref[k * (blocks_x - 1), b, k][None, :] * beyond
+
+    views = [out_ref.at[k * (blocks_x - 1)] for k in range(2)]
+    updated(out_ref, views, buffer, sems, change)
 
 
 def to_sibling(array):
@@ -528,11 +531,11 @@
 
     sums = (
         in_pair(pair_s),
+        between_pairs_crossed(next_x),
+        in_pair_crossed(pair_x),
+        between_pairs(next_s),
+        to_partner(own_x),
         own_s,
-        between_pairs(next_s),
-        in_pair_crossed(pair_x),
-        to_partner(own_x),
-        between_pairs_crossed(next_x),
     )
 
     sweep, *faces = call(
@@ -606,11 +609,11 @@
     partners = jnp.stack([keep[1], other[1]])
     tables = (
         in_pair(mine),
+        between_pairs_crossed(partners),
         in_pair_crossed(partners),
+        between_pairs(mine),
+        to_partner(partners),
         mine,
-        to_partner(partners),
-        between_pairs(mine),
-        between_pairs_crossed(partners),
     )
 
     fine_part = call(
@@ -687,21 +690,21 @@
         *tables,
     )
 
-    residual = call(
-        border_kernel,
-        1,
-        [hbm, whole(face_weight.shape)] + [vmem] * 4,
-        hbm,
-        like(fine_shape),
-        scalars=1,
-        scratch=[
-            pltpu.VMEM((2,) + x_face, F32),
-            pltpu.VMEM((2, blocks_x - 2, rows, size), F32),
-            pltpu.SemaphoreType.DMA((8,)),
-        ],
-        moved=fine_bytes,
-        aliases={1: 0},
-    )(pos, residual, face_weight, *x_halo(*x_faces), *solved_y)
+    for kernel, face, beyond in (
+        (y_border_kernel, y_face, solved_y),
+        (x_border_kernel, x_face, x_halo(*x_faces)),
+    ):
+        residual = call(
+            kernel,
+            1,
+            [hbm, whole(face_weight.shape)] + [vmem] * 2,
+            hbm,
+            like(fine_shape),
+            scalars=1,
+            scratch=[pltpu.VMEM((2,) + face, F32), pltpu.SemaphoreType.DMA((4,))],
+            moved=fine_bytes,
+            aliases={1: 0},
+        )(pos, residual, face_weight, *beyond)
     return (solved, residual)
 
 

time: 157 us -> 151 us (0.962)
  starting transfers between devices: 53.5 us -> 43.1 us
  waiting for transfers between devices: 56.3 us -> 59.4 us
  Pallas kernels: 38.5 us -> 40.4 us
    ppermute x22, starting transfers between devices: 53.5 us -> 43.1 us  [moved_to(): return lax.ppermute(array, ('gx', 'gy'), pairs)]
    ppermute x22, waiting for transfers between devices: 56.3 us -> 59.4 us  [moved_to(): return lax.ppermute(array, ('gx', 'gy'), pairs)]
    pallas_call x1 -> x2, Pallas kernels: 3.52 us -> 5.39 us  [body(): call(kernel, 1, [hbm, whole(face_weight.shape)] + [vmem] * 2, hbm, like(f...]
  transfers between devices with their start and end apart: 22 -> 22, of which waited for: 8 -> 8; matrix products, arithmetic and copies ran while one was open for 0% -> 0% of each run, Pallas kernels for 19% -> 21%
where the time goes in v5:
time: 151 us; the launch traced here: 150 us
  waiting for transfers between devices  59.4 us (39%)
  starting transfers between devices  43.1 us (29%)
  Pallas kernels  40.4 us (27%)
  local copies, waits for them, and re-layouts  6.51 us (4%)
    ppermute x22, waiting for transfers between devices, moved_to(): return lax.ppermute(array, ('gx', 'gy'), pairs)  59.4 us
    ppermute x22, starting transfers between devices, moved_to(): return lax.ppermute(array, ('gx', 'gy'), pairs)  43.1 us
    pallas_call x1, Pallas kernels, body(): call(fine_kernel, steps, [fine_block] + [mat_block] * 2 + [weight_block,...  9.71 us
    pallas_call x1, Pallas kernels, body(): call(finish_kernel, steps + 1, [now(fine_shape), now(prolong_weight.shape...  7.23 us
    unnamed x46, local copies, waits for them, and re-layouts  6.38 us
    pallas_call x2, Pallas kernels, body(): call(kernel, 1, [hbm, whole(face_weight.shape)] + [vmem] * 2, hbm, like(f...  5.39 us
    pallas_call x1, Pallas kernels, body(): call(coarse_last_kernel, 1, [vmem] * 4 + [hbm, vmem], [vmem] * 2, [like(m...  4.27 us
    pallas_call x1, Pallas kernels, body(): call(sweep_kernel, steps, [fine_block, mat_block], [fine_block] + face_sp...  4.1 us
  transfers between devices with their start and end apart: 22, of which 8 were waited for; matrix products, arithmetic and copies ran while one was open for 0% of the time, Pallas kernels for 21%

profile of v5, /device:TPU:1, one launch (start us, length us, event | category | flops | bytes accessed | tf_op | source)
XLA Modules:
  0.0 150.5 jit_solution(14298410454628626685)
XLA Ops:
  0.7 2.2 %copy-done = f32[8,8,128,128]{3,2,1,0:T(8,128)S(1)} copy-done((f32[8,8,128,128]{3,2,1,0:T(8,128)S(1)}, f32[8,8,128,128]{3,2,1,0:T(8,128)}, u32[]{:S(2)}) %copy-start) | copy-done | bytes 4194328
  6.9 2.2 %collective-permute-start = (f32[2,10,32,128]{3,2,1,0:T(8,128)S(1)}, f32[2,10,32,128]{3,2,1,0:T(8,128)S(1)}, u32[]{:S(2)}, u32[]{:S(2)}) collective-permute-start(f32[2,10,32,128]{3,2,1,0:T(8,128)S(1)} %get-tuple-element.42), channel_id=1, source_target_pairs={{0,1},{1,0},{2,3},{3,2},{4,5},{5,4},{6,7},{7,6},{8,9},{9,8},{10,11... | collective-permute-start | bytes 983048 | tf_op jit(solution)/shard_map/ppermute | solution.py:22
  9.8 5.3 %collective-permute-start.2 = (f32[2,10,32,128]{3,2,1,0:T(8,128)S(1)}, f32[2,10,32,128]{3,2,1,0:T(8,128)S(1)}, u32[]{:S(2)}, u32[]{:S(2)}) collective-permute-start(f32[2,10,32,128]{3,2,1,0:T(8,128)S(1)} %get-tuple-element.44), channel_id=1, source_target_pairs={{0,65},{1,64},{2,67},{3,66},{4,69},{5,68},{6,71},{7,70},{8,73},{9,... | collective-permute-start | bytes 983048 | tf_op jit(solution)/shard_map/ppermute | solution.py:22
  17.3 4.1 %shard_map.132 = (f32[8,8,128,128]{3,2,1,0:T(8,128)S(1)}, f32[8,128,128]{2,1,0:T(8,128)S(1)}, f32[8,128,128]{2,1,0:T(8,128)S(1)}, f32[8,128,128]{2,1,0:T(8,128)S(1)}, f32[8,128,128]{2,1,0:T(8,128)S(1)}) custom-call(s32[6]{0:T(128)S(1)} %stack.33.pos, f32[8,8,128,128]{3,2,1,0:T(8,128)S(1)} %copy-done, f32[8,8,128,128]{3,2,1,0:T(8,128)S(1)} %copy-done.9), custom_call_target="tpu_custom_call" | custom-call | flops 42949672960 | bytes 503316480 | tf_op jit(solution)/shard_map/pallas_call | solution.py:541
  21.5 1.9 %collective-permute-start.6 = (f32[8,128,128]{2,1,0:T(8,128)S(1)}, f32[8,128,128]{2,1,0:T(8,128)S(1)}, u32[]{:S(2)}, u32[]{:S(2)}) collective-permute-start(f32[8,128,128]{2,1,0:T(8,128)S(1)} %get-tuple-element.57), channel_id=1, source_target_pairs={{0,32},{1,33},{2,34},{3,35},{4,36},{5,37},{6,38},{7,39},{8,40},{9,... | collective-permute-start | bytes 1572872 | tf_op jit(solution)/shard_map/ppermute | solution.py:22
  23.4 3.4 %collective-permute-start.7 = (f32[8,128,128]{2,1,0:T(8,128)S(1)}, f32[8,128,128]{2,1,0:T(8,128)S(1)}, u32[]{:S(2)}, u32[]{:S(2)}) collective-permute-start(f32[8,128,128]{2,1,0:T(8,128)S(1)} %get-tuple-element.58), channel_id=1, source_target_pairs={{32,64},{33,65},{34,66},{35,67},{36,68},{37,69},{38,70},{39,71},{4... | collective-permute-start | bytes 1572872 | tf_op jit(solution)/shard_map/ppermute | solution.py:22
  26.7 14.8 %collective-permute-done.2.pair_x = f32[2,10,32,128]{3,2,1,0:T(8,128)S(1)} collective-permute-done((f32[2,10,32,128]{3,2,1,0:T(8,128)S(1)}, f32[2,10,32,128]{3,2,1,0:T(8,128)S(1)}, u32[]{:S(2)}, u32[]{:S(2)}) %collective-permute-start.2) | collective-permute-done | bytes 327712 | tf_op jit(solution)/shard_map/ppermute | solution.py:22
  42.1 1.9 %collective-permute-start.5 = (f32[2,10,32,128]{3,2,1,0:T(8,128)S(1)}, f32[2,10,32,128]{3,2,1,0:T(8,128)S(1)}, u32[]{:S(2)}, u32[]{:S(2)}) collective-permute-start(f32[2,10,32,128]{3,2,1,0:T(8,128)S(1)} %get-tuple-element.56), channel_id=1, source_target_pairs={{0,32},{1,33},{2,34},{3,35},{4,36},{5,37},{6,38},{7,39},{8,40},{9,... | collective-permute-start | bytes 983048 | tf_op jit(solution)/shard_map/ppermute | solution.py:22
  45.4 3.3 %shard_map.134 = (f32[32,32,128]{2,1,0:T(8,128)S(1)}, f32[32,32,128]{2,1,0:T(8,128)}) custom-call(s32[6]{0:T(128)S(1)} %stack.33.pos, f32[2,10,32,128]{3,2,1,0:T(8,128)S(1)} %get-tuple-element.61.keep, f32[2,10,32,128]{3,2,1,0:T(8,128)S(1)} %collective-permute-done.5.other, f32[32,128,128]{2,1,0:T(8,128)S(1)} %copy-done.13), custom_call_target="tpu_custom_call" | custom-call | flops 5368709120 | bytes 83886080 | tf_op jit(solution)/shard_map/pallas_call | solution.py:564
  50.9 4.6 %collective-permute-start.8 = (f32[32,32,128]{2,1,0:T(8,128)}, f32[32,32,128]{2,1,0:T(8,128)}, u32[]{:S(2)}, u32[]{:S(2)}) collective-permute-start(f32[32,32,128]{2,1,0:T(8,128)} %get-tuple-element.68.first_ref), channel_id=1, source_target_pairs={{0,65},{1,64},{2,67},{3,66},{4,69},{5,68},{6,71},{7,70},{8,73},{9,... | collective-permute-start | bytes 1572872 | tf_op jit(solution)/shard_map/ppermute | solution.py:22
  57.6 2.9 %shard_map.135.inner_ref = f32[32,32,128]{2,1,0:T(8,128)S(1)} custom-call(f32[32,32,128]{2,1,0:T(8,128)S(1)} %copy-done.18, f32[32,32,128]{2,1,0:T(8,128)} %get-tuple-element.68.first_ref, f32[32,128,128]{2,1,0:T(8,128)S(1)} %copy-done.12), custom_call_target="tpu_custom_call" | custom-call | flops 5368709120 | bytes 83886080 | tf_op jit(solution)/shard_map/pallas_call | solution.py:581
  60.6 18.0 %collective-permute-done.8.pair_ref = f32[32,32,128]{2,1,0:T(8,128)} collective-permute-done((f32[32,32,128]{2,1,0:T(8,128)}, f32[32,32,128]{2,1,0:T(8,128)}, u32[]{:S(2)}, u32[]{:S(2)}) %collective-permute-start.8) | collective-permute-done | bytes 524320 | tf_op jit(solution)/shard_map/ppermute | solution.py:22
  78.6 4.3 %shard_map.136 = (f32[2,10,32,128]{3,2,1,0:T(8,128)S(1)}, f32[2,10,32,128]{3,2,1,0:T(8,128)S(1)}) custom-call(s32[6]{0:T(128)S(1)} %stack.33.pos, s32[32,6]{1,0:T(8,128)S(1)} %copy.16.nbr, f32[32,32,128]{2,1,0:T(8,128)S(1)} %shard_map.135.inner_ref, f32[32,32,128]{2,1,0:T(8,128)} %collective-permute-done.8.pair_ref, ...), custom_call_target="tpu_custom_call" | custom-call | flops 5368709120 | bytes 83886080 | tf_op jit(solution)/shard_map/pallas_call | solution.py:592
  86.2 4.1 %collective-permute-start.13 = (f32[2,10,32,128]{3,2,1,0:T(8,128)S(1)}, f32[2,10,32,128]{3,2,1,0:T(8,128)S(1)}, u32[]{:S(2)}, u32[]{:S(2)}) collective-permute-start(f32[2,10,32,128]{3,2,1,0:T(8,128)S(1)} %pad_maximum_fusion.refs_5_), channel_id=1, source_target_pairs={{0,1},{1,0},{2,3},{3,2},{4,5},{5,4},{6,7},{7,6},{8,9},{9,8},{10,11... | collective-permute-start | bytes 983048 | tf_op jit(solution)/shard_map/ppermute | solution.py:22
  93.6 9.7 %shard_map.137.fine_ref = f32[8,8,128,128]{3,2,1,0:T(8,128)S(1)} custom-call(s32[6]{0:T(128)S(1)} %stack.33.pos, f32[8,8,128,128]{3,2,1,0:T(8,128)S(1)} %copy-done.1, f32[8,8,128,128]{3,2,1,0:T(8,128)S(1)} %copy-done.10, f32[8,8,128,128]{3,2,1,0:T(8,128)S(1)} %copy-done.11, f32[8,8,4,128]{3,2,1,0:T(4,128)S(1)} %copy-done.2, f32[8,8,128,128]{3,2,1,0:T(8,128)} %copy-done.19, ...), custom_call_target="tpu_custom_call" | custom-call | flops 85899345920 | bytes 838860800 | tf_op jit(solution)/shard_map/pallas_call | solution.py:619
  104.7 8.3 %collective-permute-done.17.refs_4_ = f32[2,10,32,128]{3,2,1,0:T(8,128)S(1)} collective-permute-done((f32[2,10,32,128]{3,2,1,0:T(8,128)S(1)}, f32[2,10,32,128]{3,2,1,0:T(8,128)S(1)}, u32[]{:S(2)}, u32[]{:S(2)}) %collective-permute-start.17) | collective-permute-done | bytes 327712 | tf_op jit(solution)/shard_map/ppermute | solution.py:22
  114.0 2.5 %collective-permute-start.18 = (f32[8,128,128]{2,1,0:T(8,128)S(1)}, f32[8,128,128]{2,1,0:T(8,128)S(1)}, u32[]{:S(2)}, u32[]{:S(2)}) collective-permute-start(f32[8,128,128]{2,1,0:T(8,128)S(1)} %get-tuple-element.78), channel_id=1, source_target_pairs={{0,1},{1,0},{2,3},{3,2},{4,5},{5,4},{6,7},{7,6},{8,9},{9,8},{10,11... | collective-permute-start | bytes 1572872 | tf_op jit(solution)/shard_map/ppermute | solution.py:22
  117.2 7.2 %shard_map.138 = (f32[8,8,128,128]{3,2,1,0:T(8,128)}, f32[8,8,128,128]{3,2,1,0:T(8,128)}, f32[8,128,128]{2,1,0:T(8,128)S(1)}, f32[8,128,128]{2,1,0:T(8,128)S(1)}) custom-call(s32[6]{0:T(128)S(1)} %stack.33.pos, s32[8,8]{1,0:T(8,128)S(1)} %copy-done.6, s32[8,8]{1,0:T(8,128)S(1)} %copy-done.8, f32[8,8,128,128]{3,2,1,0:T(8,128)S(1)} %shard_map.137.fine_ref, ...), custom_call_target="tpu_custom_call" | custom-call | flops 42949672960 | bytes 838860800 | tf_op jit(solution)/shard_map/pallas_call | solution.py:661
  124.4 2.4 %collective-permute-start.20 = (f32[8,128,128]{2,1,0:T(8,128)S(1)}, f32[8,128,128]{2,1,0:T(8,128)S(1)}, u32[]{:S(2)}, u32[]{:S(2)}) collective-permute-start(f32[8,128,128]{2,1,0:T(8,128)S(1)} %get-tuple-element.80), channel_id=1, source_target_pairs={{0,32},{1,33},{2,34},{3,35},{4,36},{5,37},{6,38},{7,39},{8,40},{9,... | collective-permute-start | bytes 1572872 | tf_op jit(solution)/shard_map/ppermute | solution.py:22
  126.9 3.7 %collective-permute-start.21 = (f32[8,128,128]{2,1,0:T(8,128)S(1)}, f32[8,128,128]{2,1,0:T(8,128)S(1)}, u32[]{:S(2)}, u32[]{:S(2)}) collective-permute-start(f32[8,128,128]{2,1,0:T(8,128)S(1)} %get-tuple-element.81), channel_id=1, source_target_pairs={{32,64},{33,65},{34,66},{35,67},{36,68},{37,69},{38,70},{39,71},{4... | collective-permute-start | bytes 1572872 | tf_op jit(solution)/shard_map/ppermute | solution.py:22
  130.6 6.2 %collective-permute-done.18.y_pair = f32[8,128,128]{2,1,0:T(8,128)S(1)} collective-permute-done((f32[8,128,128]{2,1,0:T(8,128)S(1)}, f32[8,128,128]{2,1,0:T(8,128)S(1)}, u32[]{:S(2)}, u32[]{:S(2)}) %collective-permute-start.18) | collective-permute-done | bytes 524320 | tf_op jit(solution)/shard_map/ppermute | solution.py:22
  136.8 2.7 %shard_map.140.part_ref = f32[8,8,128,128]{3,2,1,0:T(8,128)} custom-call(s32[6]{0:T(128)S(1)} %stack.33.pos, f32[8,8,128,128]{3,2,1,0:T(8,128)} %get-tuple-element.77.part_ref, f32[8,8,4,128]{3,2,1,0:T(4,128)S(1)} %copy-done.2, f32[8,128,128]{2,1,0:T(8,128)S(1)} %collective-permute-done.18.y_pair, ...), custom_call_target="tpu_custom_call", output_to_operand_aliasing={{}: (1, {})} | custom-call | bytes 167772160 | tf_op jit(solution)/shard_map/pallas_call | solution.py:697
  139.5 8.2 %collective-permute-done.21.x_outer = f32[8,128,128]{2,1,0:T(8,128)S(1)} collective-permute-done((f32[8,128,128]{2,1,0:T(8,128)S(1)}, f32[8,128,128]{2,1,0:T(8,128)S(1)}, u32[]{:S(2)}, u32[]{:S(2)}) %collective-permute-start.21) | collective-permute-done | bytes 524320 | tf_op jit(solution)/shard_map/ppermute | solution.py:22
  147.8 2.7 %shard_map.141 = f32[8,8,128,128]{3,2,1,0:T(8,128)} custom-call(s32[6]{0:T(128)S(1)} %stack.33.pos, f32[8,8,128,128]{3,2,1,0:T(8,128)} %shard_map.140.part_ref, f32[8,8,4,128]{3,2,1,0:T(4,128)S(1)} %copy-done.2, f32[8,128,128]{2,1,0:T(8,128)S(1)} %collective-permute-done.20.x_inner, ...), custom_call_target="tpu_custom_call", output_to_operand_aliasing={{}: (1, {})} | custom-call | bytes 167772160 | tf_op jit(solution)/shard_map/pallas_call | solution.py:697
  (82 shorter events, 22.8 us)
Async XLA Ops:
  6.9 14.5 %collective-permute-start = (f32[2,10,32,128]{3,2,1,0:T(8,128)S(1)}, f32[2,10,32,128]{3,2,1,0:T(8,128)S(1)}, u32[]{:S(2)}, u32[]{:S(2)}) collective-permute-start(f32[2,10,32,128]{3,2,1,0:T(8,128)S(1)} %get-tuple-element.42), channel_id=1, source_target_pairs={{0,1},{1,0},{2,3},{3,2},{4,5},{5,4},{6,7},{7,6},{8,9},{9,8},{10,11... | collective-permute-start | bytes 983048 | tf_op jit(solution)/shard_map/ppermute | solution.py:22
  9.1 14.2 %collective-permute-start.1 = (f32[2,10,32,128]{3,2,1,0:T(8,128)S(1)}, f32[2,10,32,128]{3,2,1,0:T(8,128)S(1)}, u32[]{:S(2)}, u32[]{:S(2)}) collective-permute-start(f32[2,10,32,128]{3,2,1,0:T(8,128)S(1)} %get-tuple-element.43), channel_id=1, source_target_pairs={{1,66},{2,65},{3,68},{4,67},{5,70},{6,69},{7,72},{8,71},{9,74},{10... | collective-permute-start | bytes 983048 | tf_op jit(solution)/shard_map/ppermute | solution.py:22
  9.8 31.7 %collective-permute-start.2 = (f32[2,10,32,128]{3,2,1,0:T(8,128)S(1)}, f32[2,10,32,128]{3,2,1,0:T(8,128)S(1)}, u32[]{:S(2)}, u32[]{:S(2)}) collective-permute-start(f32[2,10,32,128]{3,2,1,0:T(8,128)S(1)} %get-tuple-element.44), channel_id=1, source_target_pairs={{0,65},{1,64},{2,67},{3,66},{4,69},{5,68},{6,71},{7,70},{8,73},{9,... | collective-permute-start | bytes 983048 | tf_op jit(solution)/shard_map/ppermute | solution.py:22
  15.1 26.4 %collective-permute-start.3 = (f32[2,10,32,128]{3,2,1,0:T(8,128)S(1)}, f32[2,10,32,128]{3,2,1,0:T(8,128)S(1)}, u32[]{:S(2)}, u32[]{:S(2)}) collective-permute-start(f32[2,10,32,128]{3,2,1,0:T(8,128)S(1)} %get-tuple-element.45), channel_id=1, source_target_pairs={{1,2},{2,1},{3,4},{4,3},{5,6},{6,5},{7,8},{8,7},{9,10},{10,9},{11,... | collective-permute-start | bytes 983048 | tf_op jit(solution)/shard_map/ppermute | solution.py:22
  15.8 25.7 %collective-permute-start.4 = (f32[2,10,32,128]{3,2,1,0:T(8,128)S(1)}, f32[2,10,32,128]{3,2,1,0:T(8,128)S(1)}, u32[]{:S(2)}, u32[]{:S(2)}) collective-permute-start(f32[2,10,32,128]{3,2,1,0:T(8,128)S(1)} %get-tuple-element.46), channel_id=1, source_target_pairs={{0,64},{1,65},{2,66},{3,67},{4,68},{5,69},{6,70},{7,71},{8,72},{9,... | collective-permute-start | bytes 983048 | tf_op jit(solution)/shard_map/ppermute | solution.py:22
  21.5 22.6 %collective-permute-start.6 = (f32[8,128,128]{2,1,0:T(8,128)S(1)}, f32[8,128,128]{2,1,0:T(8,128)S(1)}, u32[]{:S(2)}, u32[]{:S(2)}) collective-permute-start(f32[8,128,128]{2,1,0:T(8,128)S(1)} %get-tuple-element.57), channel_id=1, source_target_pairs={{0,32},{1,33},{2,34},{3,35},{4,36},{5,37},{6,38},{7,39},{8,40},{9,... | collective-permute-start | bytes 1572872 | tf_op jit(solution)/shard_map/ppermute | solution.py:22
  23.4 20.8 %collective-permute-start.7 = (f32[8,128,128]{2,1,0:T(8,128)S(1)}, f32[8,128,128]{2,1,0:T(8,128)S(1)}, u32[]{:S(2)}, u32[]{:S(2)}) collective-permute-start(f32[8,128,128]{2,1,0:T(8,128)S(1)} %get-tuple-element.58), channel_id=1, source_target_pairs={{32,64},{33,65},{34,66},{35,67},{36,68},{37,69},{38,70},{39,71},{4... | collective-permute-start | bytes 1572872 | tf_op jit(solution)/shard_map/ppermute | solution.py:22
  42.1 3.2 %collective-permute-start.5 = (f32[2,10,32,128]{3,2,1,0:T(8,128)S(1)}, f32[2,10,32,128]{3,2,1,0:T(8,128)S(1)}, u32[]{:S(2)}, u32[]{:S(2)}) collective-permute-start(f32[2,10,32,128]{3,2,1,0:T(8,128)S(1)} %get-tuple-element.56), channel_id=1, source_target_pairs={{0,32},{1,33},{2,34},{3,35},{4,36},{5,37},{6,38},{7,39},{8,40},{9,... | collective-permute-start | bytes 983048 | tf_op jit(solution)/shard_map/ppermute | solution.py:22
  49.5 11.1 %collective-permute-start.9 = (f32[32,32,128]{2,1,0:T(8,128)}, f32[32,32,128]{2,1,0:T(8,128)}, u32[]{:S(2)}, u32[]{:S(2)}) collective-permute-start(f32[32,32,128]{2,1,0:T(8,128)} %get-tuple-element.68.first_ref), channel_id=1, source_target_pairs={{1,66},{2,65},{3,68},{4,67},{5,70},{6,69},{7,72},{8,71},{9,74},{10... | collective-permute-start | bytes 1572872 | tf_op jit(solution)/shard_map/ppermute | solution.py:22
  50.9 27.7 %collective-permute-start.8 = (f32[32,32,128]{2,1,0:T(8,128)}, f32[32,32,128]{2,1,0:T(8,128)}, u32[]{:S(2)}, u32[]{:S(2)}) collective-permute-start(f32[32,32,128]{2,1,0:T(8,128)} %get-tuple-element.68.first_ref), channel_id=1, source_target_pairs={{0,65},{1,64},{2,67},{3,66},{4,69},{5,68},{6,71},{7,70},{8,73},{9,... | collective-permute-start | bytes 1572872 | tf_op jit(solution)/shard_map/ppermute | solution.py:22
  55.7 27.2 %collective-permute-start.10 = (f32[8,128,128]{2,1,0:T(8,128)}, f32[8,128,128]{2,1,0:T(8,128)S(1)}, u32[]{:S(2)}, u32[]{:S(2)}) collective-permute-start(f32[8,128,128]{2,1,0:T(8,128)} %copy-done.16), channel_id=1, source_target_pairs={{0,1},{1,0},{2,3},{3,2},{4,5},{5,4},{6,7},{7,6},{8,9},{9,8},{10,11... | collective-permute-start | bytes 1572872 | tf_op jit(solution)/shard_map/ppermute | solution.py:22
  55.8 27.1 %collective-permute-start.11 = (f32[8,128,128]{2,1,0:T(8,128)}, f32[8,128,128]{2,1,0:T(8,128)S(1)}, u32[]{:S(2)}, u32[]{:S(2)}) collective-permute-start(f32[8,128,128]{2,1,0:T(8,128)} %copy-done.15), channel_id=1, source_target_pairs={{1,2},{2,1},{3,4},{4,3},{5,6},{6,5},{7,8},{8,7},{9,10},{10,9},{11,... | collective-permute-start | bytes 1572872 | tf_op jit(solution)/shard_map/ppermute | solution.py:22
  60.6 33.0 %copy-start.1 = (f32[8,8,128,128]{3,2,1,0:T(8,128)S(1)}, f32[8,8,128,128]{3,2,1,0:T(8,128)}, u32[]{:S(2)}) copy-start(f32[8,8,128,128]{3,2,1,0:T(8,128)} %r_ref.7) | copy-start | bytes 12582916
  60.6 33.0 %copy-start.2 = (f32[8,8,4,128]{3,2,1,0:T(4,128)S(1)}, f32[8,8,4,128]{3,2,1,0:T(4,128)}, u32[]{:S(2)}) copy-start(f32[8,8,4,128]{3,2,1,0:T(4,128)} %face_ref.7) | copy-start | bytes 393220
  82.9 2.5 %collective-permute-start.12 = (f32[2,10,32,128]{3,2,1,0:T(8,128)S(1)}, f32[2,10,32,128]{3,2,1,0:T(8,128)S(1)}, u32[]{:S(2)}, u32[]{:S(2)}) collective-permute-start(f32[2,10,32,128]{3,2,1,0:T(8,128)S(1)} %get-tuple-element.75), channel_id=1, source_target_pairs={{0,32},{1,33},{2,34},{3,35},{4,36},{5,37},{6,38},{7,39},{8,40},{9,... | collective-permute-start | bytes 983048 | tf_op jit(solution)/shard_map/ppermute | solution.py:22
  85.5 17.8 %collective-permute-start.16 = (f32[2,10,32,128]{3,2,1,0:T(8,128)S(1)}, f32[2,10,32,128]{3,2,1,0:T(8,128)S(1)}, u32[]{:S(2)}, u32[]{:S(2)}) collective-permute-start(f32[2,10,32,128]{3,2,1,0:T(8,128)S(1)} %pad_maximum_fusion.refs_5_), channel_id=1, source_target_pairs={{1,2},{2,1},{3,4},{4,3},{5,6},{6,5},{7,8},{8,7},{9,10},{10,9},{11,... | collective-permute-start | bytes 983048 | tf_op jit(solution)/shard_map/ppermute | solution.py:22
  86.2 18.5 %collective-permute-start.13 = (f32[2,10,32,128]{3,2,1,0:T(8,128)S(1)}, f32[2,10,32,128]{3,2,1,0:T(8,128)S(1)}, u32[]{:S(2)}, u32[]{:S(2)}) collective-permute-start(f32[2,10,32,128]{3,2,1,0:T(8,128)S(1)} %pad_maximum_fusion.refs_5_), channel_id=1, source_target_pairs={{0,1},{1,0},{2,3},{3,2},{4,5},{5,4},{6,7},{7,6},{8,9},{9,8},{10,11... | collective-permute-start | bytes 983048 | tf_op jit(solution)/shard_map/ppermute | solution.py:22
  90.4 22.6 %collective-permute-start.17 = (f32[2,10,32,128]{3,2,1,0:T(8,128)S(1)}, f32[2,10,32,128]{3,2,1,0:T(8,128)S(1)}, u32[]{:S(2)}, u32[]{:S(2)}) collective-permute-start(f32[2,10,32,128]{3,2,1,0:T(8,128)S(1)} %pad_maximum_fusion.1), channel_id=1, source_target_pairs={{0,64},{1,65},{2,66},{3,67},{4,68},{5,69},{6,70},{7,71},{8,72},{9,... | collective-permute-start | bytes 983048 | tf_op jit(solution)/shard_map/ppermute | solution.py:22
  91.8 21.1 %collective-permute-start.15 = (f32[2,10,32,128]{3,2,1,0:T(8,128)S(1)}, f32[2,10,32,128]{3,2,1,0:T(8,128)S(1)}, u32[]{:S(2)}, u32[]{:S(2)}) collective-permute-start(f32[2,10,32,128]{3,2,1,0:T(8,128)S(1)} %pad_maximum_fusion.1), channel_id=1, source_target_pairs={{0,65},{1,64},{2,67},{3,66},{4,69},{5,68},{6,71},{7,70},{8,73},{9,... | collective-permute-start | bytes 983048 | tf_op jit(solution)/shard_map/ppermute | solution.py:22
  92.9 20.1 %collective-permute-start.14 = (f32[2,10,32,128]{3,2,1,0:T(8,128)S(1)}, f32[2,10,32,128]{3,2,1,0:T(8,128)S(1)}, u32[]{:S(2)}, u32[]{:S(2)}) collective-permute-start(f32[2,10,32,128]{3,2,1,0:T(8,128)S(1)} %pad_maximum_fusion.1), channel_id=1, source_target_pairs={{1,66},{2,65},{3,68},{4,67},{5,70},{6,69},{7,72},{8,71},{9,74},{10... | collective-permute-start | bytes 983048 | tf_op jit(solution)/shard_map/ppermute | solution.py:22
  114.0 22.8 %collective-permute-start.18 = (f32[8,128,128]{2,1,0:T(8,128)S(1)}, f32[8,128,128]{2,1,0:T(8,128)S(1)}, u32[]{:S(2)}, u32[]{:S(2)}) collective-permute-start(f32[8,128,128]{2,1,0:T(8,128)S(1)} %get-tuple-element.78), channel_id=1, source_target_pairs={{0,1},{1,0},{2,3},{3,2},{4,5},{5,4},{6,7},{7,6},{8,9},{9,8},{10,11... | collective-permute-start | bytes 1572872 | tf_op jit(solution)/shard_map/ppermute | solution.py:22
  116.5 20.3 %collective-permute-start.19 = (f32[8,128,128]{2,1,0:T(8,128)S(1)}, f32[8,128,128]{2,1,0:T(8,128)S(1)}, u32[]{:S(2)}, u32[]{:S(2)}) collective-permute-start(f32[8,128,128]{2,1,0:T(8,128)S(1)} %get-tuple-element.79), channel_id=1, source_target_pairs={{1,2},{2,1},{3,4},{4,3},{5,6},{6,5},{7,8},{8,7},{9,10},{10,9},{11,... | collective-permute-start | bytes 1572872 | tf_op jit(solution)/shard_map/ppermute | solution.py:22
  124.4 15.1 %collective-permute-start.20 = (f32[8,128,128]{2,1,0:T(8,128)S(1)}, f32[8,128,128]{2,1,0:T(8,128)S(1)}, u32[]{:S(2)}, u32[]{:S(2)}) collective-permute-start(f32[8,128,128]{2,1,0:T(8,128)S(1)} %get-tuple-element.80), channel_id=1, source_target_pairs={{0,32},{1,33},{2,34},{3,35},{4,36},{5,37},{6,38},{7,39},{8,40},{9,... | collective-permute-start | bytes 1572872 | tf_op jit(solution)/shard_map/ppermute | solution.py:22
  126.9 20.9 %collective-permute-start.21 = (f32[8,128,128]{2,1,0:T(8,128)S(1)}, f32[8,128,128]{2,1,0:T(8,128)S(1)}, u32[]{:S(2)}, u32[]{:S(2)}) collective-permute-start(f32[8,128,128]{2,1,0:T(8,128)S(1)} %get-tuple-element.81), channel_id=1, source_target_pairs={{32,64},{33,65},{34,66},{35,67},{36,68},{37,69},{38,70},{39,71},{4... | collective-permute-start | bytes 1572872 | tf_op jit(solution)/shard_map/ppermute | solution.py:22
  (20 other events, 318.0 us)

commit v6 on v5

--- a/solution.py
+++ b/solution.py
@@ -527,6 +527,7 @@
             pltpu.SemaphoreType.DMA((blocks_x,)),
         ],
         moved=2 * fine_bytes,
+        limit=60,
     )(pos, block_owner, block_aggregate, right_side, restrict_weight)
 
     sums = (
@@ -565,7 +566,7 @@
         coarse_first_kernel,
         1,
         [vmem, vmem, hbm],
-        [vmem] * 2,
+        [whole(coarse_shape), vmem],
         [like(coarse_shape)] * 2,
         scalars=1,
         scratch=[pltpu.VMEM(slab, F32)] + cmat_scratch,
@@ -581,7 +582,7 @@
     inner = call(
         coarse_own_kernel,
         1,
-        [vmem, vmem, hbm],
+        [whole(coarse_shape), vmem, hbm],
         vmem,
         like(coarse_shape),
         scratch=cmat_scratch,

time: 151 us -> 151 us (level)
  waiting for transfers between devices: 59.4 us -> 47.1 us
  starting transfers between devices: 43.1 us -> 49.2 us
  Pallas kernels: 40.4 us -> 43.8 us
  local copies, waits for them, and re-layouts: 6.51 us -> 9.1 us
    ppermute x22, waiting for transfers between devices: 59.4 us -> 47.1 us  [moved_to(): return lax.ppermute(array, ('gx', 'gy'), pairs)]
    ppermute x22, starting transfers between devices: 43.1 us -> 49.2 us  [moved_to(): return lax.ppermute(array, ('gx', 'gy'), pairs)]
    pallas_call x1, Pallas kernels: 1.85 us -> 5.25 us  [body(): call(restrict_kernel, 1, [hbm, whole(restrict_weight.shape)], [vmem] * 6,...]
    unnamed x46 -> x44, local copies, waits for them, and re-layouts: 6.38 us -> 8.43 us
where the time goes in v6:
time: 151 us; the launch traced here: 150 us
  starting transfers between devices  49.2 us (33%)
  waiting for transfers between devices  47.1 us (31%)
  Pallas kernels  43.8 us (29%)
  local copies, waits for them, and re-layouts  9.1 us (6%)
    ppermute x22, starting transfers between devices, moved_to(): return lax.ppermute(array, ('gx', 'gy'), pairs)  49.2 us
    ppermute x22, waiting for transfers between devices, moved_to(): return lax.ppermute(array, ('gx', 'gy'), pairs)  47.1 us
    pallas_call x1, Pallas kernels, body(): call(fine_kernel, steps, [fine_block] + [mat_block] * 2 + [weight_block,...  9.71 us
    unnamed x44, local copies, waits for them, and re-layouts  8.43 us
    pallas_call x1, Pallas kernels, body(): call(finish_kernel, steps + 1, [now(fine_shape), now(prolong_weight.shape...  7.23 us
    pallas_call x2, Pallas kernels, body(): call(kernel, 1, [hbm, whole(face_weight.shape)] + [vmem] * 2, hbm, like(f...  5.39 us
    pallas_call x1, Pallas kernels, body(): call(restrict_kernel, 1, [hbm, whole(restrict_weight.shape)], [vmem] * 6,...  5.25 us
    pallas_call x1, Pallas kernels, body(): call(coarse_last_kernel, 1, [vmem] * 4 + [hbm, vmem], [vmem] * 2, [like(m...  4.27 us
  transfers between devices with their start and end apart: 22, of which 8 were waited for; matrix products, arithmetic and copies ran while one was open for 0% of the time, Pallas kernels for 21%

profile of v6, /device:TPU:1, one launch (start us, length us, event | category | flops | bytes accessed | tf_op | source)
XLA Modules:
  0.0 150.3 jit_solution(10915867793839333627)
XLA Ops:
  1.3 5.2 %shard_map.131 = (f32[2,10,32,128]{3,2,1,0:T(8,128)}, f32[2,10,32,128]{3,2,1,0:T(8,128)}, f32[2,10,32,128]{3,2,1,0:T(8,128)}, f32[2,10,32,128]{3,2,1,0:T(8,128)}...) custom-call(s32[6]{0:T(128)} %stack.33.pos, s32[8,8]{1,0:T(8,128)} %owner.5, s32[8,8]{1,0:T(8,128)} %agg.5, ...), custom_call_target="tpu_custom_call" | custom-call | bytes 335544320 | tf_op jit(solution)/shard_map/pallas_call | solution.py:517
  6.5 2.2 %collective-permute-start = (f32[2,10,32,128]{3,2,1,0:T(8,128)}, f32[2,10,32,128]{3,2,1,0:T(8,128)S(1)}, u32[]{:S(2)}, u32[]{:S(2)}) collective-permute-start(f32[2,10,32,128]{3,2,1,0:T(8,128)} %get-tuple-element.42), channel_id=1, source_target_pairs={{0,1},{1,0},{2,3},{3,2},{4,5},{5,4},{6,7},{7,6},{8,9},{9,8},{10,11... | collective-permute-start | bytes 983048 | tf_op jit(solution)/shard_map/ppermute | solution.py:22
  9.4 5.3 %collective-permute-start.2 = (f32[2,10,32,128]{3,2,1,0:T(8,128)}, f32[2,10,32,128]{3,2,1,0:T(8,128)S(1)}, u32[]{:S(2)}, u32[]{:S(2)}) collective-permute-start(f32[2,10,32,128]{3,2,1,0:T(8,128)} %get-tuple-element.44), channel_id=1, source_target_pairs={{0,65},{1,64},{2,67},{3,66},{4,69},{5,68},{6,71},{7,70},{8,73},{9,... | collective-permute-start | bytes 983048 | tf_op jit(solution)/shard_map/ppermute | solution.py:22
  16.9 2.2 %copy-done = f32[8,8,128,128]{3,2,1,0:T(8,128)S(1)} copy-done((f32[8,8,128,128]{3,2,1,0:T(8,128)S(1)}, f32[8,8,128,128]{3,2,1,0:T(8,128)}, u32[]{:S(2)}) %copy-start) | copy-done | bytes 4194328
  19.1 2.2 %copy-done.8 = f32[8,8,128,128]{3,2,1,0:T(8,128)S(1)} copy-done((f32[8,8,128,128]{3,2,1,0:T(8,128)S(1)}, f32[8,8,128,128]{3,2,1,0:T(8,128)}, u32[]{:S(2)}) %copy-start.8) | copy-done | bytes 4194328
  21.3 4.1 %shard_map.132 = (f32[8,8,128,128]{3,2,1,0:T(8,128)S(1)}, f32[8,128,128]{2,1,0:T(8,128)S(1)}, f32[8,128,128]{2,1,0:T(8,128)S(1)}, f32[8,128,128]{2,1,0:T(8,128)S(1)}, f32[8,128,128]{2,1,0:T(8,128)S(1)}) custom-call(s32[6]{0:T(128)S(1)} %copy-done.5, f32[8,8,128,128]{3,2,1,0:T(8,128)S(1)} %copy-done, f32[8,8,128,128]{3,2,1,0:T(8,128)S(1)} %copy-done.8), custom_call_target="tpu_custom_call" | custom-call | flops 42949672960 | bytes 503316480 | tf_op jit(solution)/shard_map/pallas_call | solution.py:542
  29.2 3.4 %collective-permute-start.7 = (f32[8,128,128]{2,1,0:T(8,128)S(1)}, f32[8,128,128]{2,1,0:T(8,128)S(1)}, u32[]{:S(2)}, u32[]{:S(2)}) collective-permute-start(f32[8,128,128]{2,1,0:T(8,128)S(1)} %get-tuple-element.58), channel_id=1, source_target_pairs={{32,64},{33,65},{34,66},{35,67},{36,68},{37,69},{38,70},{39,71},{4... | collective-permute-start | bytes 1572872 | tf_op jit(solution)/shard_map/ppermute | solution.py:22
  32.6 3.1 %collective-permute-done.2.pair_x = f32[2,10,32,128]{3,2,1,0:T(8,128)S(1)} collective-permute-done((f32[2,10,32,128]{3,2,1,0:T(8,128)}, f32[2,10,32,128]{3,2,1,0:T(8,128)S(1)}, u32[]{:S(2)}, u32[]{:S(2)}) %collective-permute-start.2) | collective-permute-done | bytes 327712 | tf_op jit(solution)/shard_map/ppermute | solution.py:22
  36.4 7.6 %collective-permute-start.5 = (f32[2,10,32,128]{3,2,1,0:T(8,128)S(1)}, f32[2,10,32,128]{3,2,1,0:T(8,128)S(1)}, u32[]{:S(2)}, u32[]{:S(2)}) collective-permute-start(f32[2,10,32,128]{3,2,1,0:T(8,128)S(1)} %get-tuple-element.56), channel_id=1, source_target_pairs={{0,32},{1,33},{2,34},{3,35},{4,36},{5,37},{6,38},{7,39},{8,40},{9,... | collective-permute-start | bytes 983048 | tf_op jit(solution)/shard_map/ppermute | solution.py:22
  45.2 3.3 %shard_map.134 = (f32[32,32,128]{2,1,0:T(8,128)S(1)}, f32[32,32,128]{2,1,0:T(8,128)}) custom-call(s32[6]{0:T(128)S(1)} %copy-done.5, f32[2,10,32,128]{3,2,1,0:T(8,128)S(1)} %get-tuple-element.61.keep, f32[2,10,32,128]{3,2,1,0:T(8,128)S(1)} %collective-permute-done.5.other, f32[32,128,128]{2,1,0:T(8,128)S(1)} %copy-done.12), custom_call_target="tpu_custom_call" | custom-call | flops 5368709120 | bytes 83886080 | tf_op jit(solution)/shard_map/pallas_call | solution.py:565
  54.8 2.9 %shard_map.135.inner_ref = f32[32,32,128]{2,1,0:T(8,128)S(1)} custom-call(f32[32,32,128]{2,1,0:T(8,128)S(1)} %copy-done.17, f32[32,32,128]{2,1,0:T(8,128)} %get-tuple-element.68.first_ref, f32[32,128,128]{2,1,0:T(8,128)S(1)} %copy-done.11), custom_call_target="tpu_custom_call" | custom-call | flops 5368709120 | bytes 83886080 | tf_op jit(solution)/shard_map/pallas_call | solution.py:582
  57.8 18.6 %collective-permute-done.8.pair_ref = f32[32,32,128]{2,1,0:T(8,128)} collective-permute-done((f32[32,32,128]{2,1,0:T(8,128)}, f32[32,32,128]{2,1,0:T(8,128)}, u32[]{:S(2)}, u32[]{:S(2)}) %collective-permute-start.8) | collective-permute-done | bytes 524320 | tf_op jit(solution)/shard_map/ppermute | solution.py:22
  76.4 4.3 %shard_map.136 = (f32[2,10,32,128]{3,2,1,0:T(8,128)S(1)}, f32[2,10,32,128]{3,2,1,0:T(8,128)S(1)}) custom-call(s32[6]{0:T(128)S(1)} %copy-done.5, s32[32,6]{1,0:T(8,128)S(1)} %copy.16.nbr, f32[32,32,128]{2,1,0:T(8,128)S(1)} %shard_map.135.inner_ref, f32[32,32,128]{2,1,0:T(8,128)} %collective-permute-done.8.pair_ref, ...), custom_call_target="tpu_custom_call" | custom-call | flops 5368709120 | bytes 83886080 | tf_op jit(solution)/shard_map/pallas_call | solution.py:593
  83.3 6.8 %collective-permute-start.13 = (f32[2,10,32,128]{3,2,1,0:T(8,128)S(1)}, f32[2,10,32,128]{3,2,1,0:T(8,128)S(1)}, u32[]{:S(2)}, u32[]{:S(2)}) collective-permute-start(f32[2,10,32,128]{3,2,1,0:T(8,128)S(1)} %pad_maximum_fusion.refs_5_), channel_id=1, source_target_pairs={{0,1},{1,0},{2,3},{3,2},{4,5},{5,4},{6,7},{7,6},{8,9},{9,8},{10,11... | collective-permute-start | bytes 983048 | tf_op jit(solution)/shard_map/ppermute | solution.py:22
  93.4 9.7 %shard_map.137.fine_ref = f32[8,8,128,128]{3,2,1,0:T(8,128)S(1)} custom-call(s32[6]{0:T(128)S(1)} %copy-done.5, f32[8,8,128,128]{3,2,1,0:T(8,128)S(1)} %copy-done.1, f32[8,8,128,128]{3,2,1,0:T(8,128)S(1)} %copy-done.9, f32[8,8,128,128]{3,2,1,0:T(8,128)S(1)} %copy-done.10, f32[8,8,4,128]{3,2,1,0:T(4,128)S(1)} %copy-done.2, f32[8,8,128,128]{3,2,1,0:T(8,128)} %copy-done.18, ...), custom_call_target="tpu_custom_call" | custom-call | flops 85899345920 | bytes 838860800 | tf_op jit(solution)/shard_map/pallas_call | solution.py:620
  104.5 7.1 %collective-permute-done.17.refs_4_ = f32[2,10,32,128]{3,2,1,0:T(8,128)S(1)} collective-permute-done((f32[2,10,32,128]{3,2,1,0:T(8,128)S(1)}, f32[2,10,32,128]{3,2,1,0:T(8,128)S(1)}, u32[]{:S(2)}, u32[]{:S(2)}) %collective-permute-start.17) | collective-permute-done | bytes 327712 | tf_op jit(solution)/shard_map/ppermute | solution.py:22
  112.7 2.3 %collective-permute-start.18 = (f32[8,128,128]{2,1,0:T(8,128)S(1)}, f32[8,128,128]{2,1,0:T(8,128)S(1)}, u32[]{:S(2)}, u32[]{:S(2)}) collective-permute-start(f32[8,128,128]{2,1,0:T(8,128)S(1)} %get-tuple-element.78), channel_id=1, source_target_pairs={{0,1},{1,0},{2,3},{3,2},{4,5},{5,4},{6,7},{7,6},{8,9},{9,8},{10,11... | collective-permute-start | bytes 1572872 | tf_op jit(solution)/shard_map/ppermute | solution.py:22
  115.7 7.2 %shard_map.138 = (f32[8,8,128,128]{3,2,1,0:T(8,128)}, f32[8,8,128,128]{3,2,1,0:T(8,128)}, f32[8,128,128]{2,1,0:T(8,128)S(1)}, f32[8,128,128]{2,1,0:T(8,128)S(1)}) custom-call(s32[6]{0:T(128)S(1)} %copy-done.5, s32[8,8]{1,0:T(8,128)S(1)} %copy-done.6, s32[8,8]{1,0:T(8,128)S(1)} %copy-done.7, f32[8,8,128,128]{3,2,1,0:T(8,128)S(1)} %shard_map.137.fine_ref, ...), custom_call_target="tpu_custom_call" | custom-call | flops 42949672960 | bytes 838860800 | tf_op jit(solution)/shard_map/pallas_call | solution.py:662
  123.0 2.0 %collective-permute-start.20 = (f32[8,128,128]{2,1,0:T(8,128)S(1)}, f32[8,128,128]{2,1,0:T(8,128)S(1)}, u32[]{:S(2)}, u32[]{:S(2)}) collective-permute-start(f32[8,128,128]{2,1,0:T(8,128)S(1)} %get-tuple-element.80), channel_id=1, source_target_pairs={{0,32},{1,33},{2,34},{3,35},{4,36},{5,37},{6,38},{7,39},{8,40},{9,... | collective-permute-start | bytes 1572872 | tf_op jit(solution)/shard_map/ppermute | solution.py:22
  125.0 5.4 %collective-permute-start.21 = (f32[8,128,128]{2,1,0:T(8,128)S(1)}, f32[8,128,128]{2,1,0:T(8,128)S(1)}, u32[]{:S(2)}, u32[]{:S(2)}) collective-permute-start(f32[8,128,128]{2,1,0:T(8,128)S(1)} %get-tuple-element.81), channel_id=1, source_target_pairs={{32,64},{33,65},{34,66},{35,67},{36,68},{37,69},{38,70},{39,71},{4... | collective-permute-start | bytes 1572872 | tf_op jit(solution)/shard_map/ppermute | solution.py:22
  130.4 5.3 %collective-permute-done.18.y_pair = f32[8,128,128]{2,1,0:T(8,128)S(1)} collective-permute-done((f32[8,128,128]{2,1,0:T(8,128)S(1)}, f32[8,128,128]{2,1,0:T(8,128)S(1)}, u32[]{:S(2)}, u32[]{:S(2)}) %collective-permute-start.18) | collective-permute-done | bytes 524320 | tf_op jit(solution)/shard_map/ppermute | solution.py:22
  135.7 2.7 %shard_map.140.part_ref = f32[8,8,128,128]{3,2,1,0:T(8,128)} custom-call(s32[6]{0:T(128)S(1)} %copy-done.5, f32[8,8,128,128]{3,2,1,0:T(8,128)} %get-tuple-element.77.part_ref, f32[8,8,4,128]{3,2,1,0:T(4,128)S(1)} %copy-done.2, f32[8,128,128]{2,1,0:T(8,128)S(1)} %collective-permute-done.18.y_pair, ...), custom_call_target="tpu_custom_call", output_to_operand_aliasing={{}: (1, {})} | custom-call | bytes 167772160 | tf_op jit(solution)/shard_map/pallas_call | solution.py:698
  138.5 9.1 %collective-permute-done.21.x_outer = f32[8,128,128]{2,1,0:T(8,128)S(1)} collective-permute-done((f32[8,128,128]{2,1,0:T(8,128)S(1)}, f32[8,128,128]{2,1,0:T(8,128)S(1)}, u32[]{:S(2)}, u32[]{:S(2)}) %collective-permute-start.21) | collective-permute-done | bytes 524320 | tf_op jit(solution)/shard_map/ppermute | solution.py:22
  147.6 2.7 %shard_map.141 = f32[8,8,128,128]{3,2,1,0:T(8,128)} custom-call(s32[6]{0:T(128)S(1)} %copy-done.5, f32[8,8,128,128]{3,2,1,0:T(8,128)} %shard_map.140.part_ref, f32[8,8,4,128]{3,2,1,0:T(4,128)S(1)} %copy-done.2, f32[8,128,128]{2,1,0:T(8,128)S(1)} %collective-permute-done.20.x_inner, ...), custom_call_target="tpu_custom_call", output_to_operand_aliasing={{}: (1, {})} | custom-call | bytes 167772160 | tf_op jit(solution)/shard_map/pallas_call | solution.py:698
  (80 shorter events, 24.4 us)
Async XLA Ops:
  6.5 20.9 %collective-permute-start = (f32[2,10,32,128]{3,2,1,0:T(8,128)}, f32[2,10,32,128]{3,2,1,0:T(8,128)S(1)}, u32[]{:S(2)}, u32[]{:S(2)}) collective-permute-start(f32[2,10,32,128]{3,2,1,0:T(8,128)} %get-tuple-element.42), channel_id=1, source_target_pairs={{0,1},{1,0},{2,3},{3,2},{4,5},{5,4},{6,7},{7,6},{8,9},{9,8},{10,11... | collective-permute-start | bytes 983048 | tf_op jit(solution)/shard_map/ppermute | solution.py:22
  8.7 20.5 %collective-permute-start.1 = (f32[2,10,32,128]{3,2,1,0:T(8,128)}, f32[2,10,32,128]{3,2,1,0:T(8,128)S(1)}, u32[]{:S(2)}, u32[]{:S(2)}) collective-permute-start(f32[2,10,32,128]{3,2,1,0:T(8,128)} %get-tuple-element.43), channel_id=1, source_target_pairs={{1,66},{2,65},{3,68},{4,67},{5,70},{6,69},{7,72},{8,71},{9,74},{10... | collective-permute-start | bytes 983048 | tf_op jit(solution)/shard_map/ppermute | solution.py:22
  9.4 26.3 %collective-permute-start.2 = (f32[2,10,32,128]{3,2,1,0:T(8,128)}, f32[2,10,32,128]{3,2,1,0:T(8,128)S(1)}, u32[]{:S(2)}, u32[]{:S(2)}) collective-permute-start(f32[2,10,32,128]{3,2,1,0:T(8,128)} %get-tuple-element.44), channel_id=1, source_target_pairs={{0,65},{1,64},{2,67},{3,66},{4,69},{5,68},{6,71},{7,70},{8,73},{9,... | collective-permute-start | bytes 983048 | tf_op jit(solution)/shard_map/ppermute | solution.py:22
  14.8 20.9 %collective-permute-start.3 = (f32[2,10,32,128]{3,2,1,0:T(8,128)}, f32[2,10,32,128]{3,2,1,0:T(8,128)S(1)}, u32[]{:S(2)}, u32[]{:S(2)}) collective-permute-start(f32[2,10,32,128]{3,2,1,0:T(8,128)} %get-tuple-element.45), channel_id=1, source_target_pairs={{1,2},{2,1},{3,4},{4,3},{5,6},{6,5},{7,8},{8,7},{9,10},{10,9},{11,... | collective-permute-start | bytes 983048 | tf_op jit(solution)/shard_map/ppermute | solution.py:22
  15.4 20.3 %collective-permute-start.4 = (f32[2,10,32,128]{3,2,1,0:T(8,128)}, f32[2,10,32,128]{3,2,1,0:T(8,128)S(1)}, u32[]{:S(2)}, u32[]{:S(2)}) collective-permute-start(f32[2,10,32,128]{3,2,1,0:T(8,128)} %get-tuple-element.46), channel_id=1, source_target_pairs={{0,64},{1,65},{2,66},{3,67},{4,68},{5,69},{6,70},{7,71},{8,72},{9,... | collective-permute-start | bytes 983048 | tf_op jit(solution)/shard_map/ppermute | solution.py:22
  27.4 16.5 %collective-permute-start.6 = (f32[8,128,128]{2,1,0:T(8,128)S(1)}, f32[8,128,128]{2,1,0:T(8,128)S(1)}, u32[]{:S(2)}, u32[]{:S(2)}) collective-permute-start(f32[8,128,128]{2,1,0:T(8,128)S(1)} %get-tuple-element.57), channel_id=1, source_target_pairs={{0,32},{1,33},{2,34},{3,35},{4,36},{5,37},{6,38},{7,39},{8,40},{9,... | collective-permute-start | bytes 1572872 | tf_op jit(solution)/shard_map/ppermute | solution.py:22
  29.2 14.7 %collective-permute-start.7 = (f32[8,128,128]{2,1,0:T(8,128)S(1)}, f32[8,128,128]{2,1,0:T(8,128)S(1)}, u32[]{:S(2)}, u32[]{:S(2)}) collective-permute-start(f32[8,128,128]{2,1,0:T(8,128)S(1)} %get-tuple-element.58), channel_id=1, source_target_pairs={{32,64},{33,65},{34,66},{35,67},{36,68},{37,69},{38,70},{39,71},{4... | collective-permute-start | bytes 1572872 | tf_op jit(solution)/shard_map/ppermute | solution.py:22
  36.4 8.8 %collective-permute-start.5 = (f32[2,10,32,128]{3,2,1,0:T(8,128)S(1)}, f32[2,10,32,128]{3,2,1,0:T(8,128)S(1)}, u32[]{:S(2)}, u32[]{:S(2)}) collective-permute-start(f32[2,10,32,128]{3,2,1,0:T(8,128)S(1)} %get-tuple-element.56), channel_id=1, source_target_pairs={{0,32},{1,33},{2,34},{3,35},{4,36},{5,37},{6,38},{7,39},{8,40},{9,... | collective-permute-start | bytes 983048 | tf_op jit(solution)/shard_map/ppermute | solution.py:22
  49.3 8.5 %collective-permute-start.9 = (f32[32,32,128]{2,1,0:T(8,128)}, f32[32,32,128]{2,1,0:T(8,128)}, u32[]{:S(2)}, u32[]{:S(2)}) collective-permute-start(f32[32,32,128]{2,1,0:T(8,128)} %get-tuple-element.68.first_ref), channel_id=1, source_target_pairs={{1,66},{2,65},{3,68},{4,67},{5,70},{6,69},{7,72},{8,71},{9,74},{10... | collective-permute-start | bytes 1572872 | tf_op jit(solution)/shard_map/ppermute | solution.py:22
  50.8 25.6 %collective-permute-start.8 = (f32[32,32,128]{2,1,0:T(8,128)}, f32[32,32,128]{2,1,0:T(8,128)}, u32[]{:S(2)}, u32[]{:S(2)}) collective-permute-start(f32[32,32,128]{2,1,0:T(8,128)} %get-tuple-element.68.first_ref), channel_id=1, source_target_pairs={{0,65},{1,64},{2,67},{3,66},{4,69},{5,68},{6,71},{7,70},{8,73},{9,... | collective-permute-start | bytes 1572872 | tf_op jit(solution)/shard_map/ppermute | solution.py:22
  52.8 27.8 %collective-permute-start.10 = (f32[8,128,128]{2,1,0:T(8,128)}, f32[8,128,128]{2,1,0:T(8,128)S(1)}, u32[]{:S(2)}, u32[]{:S(2)}) collective-permute-start(f32[8,128,128]{2,1,0:T(8,128)} %copy-done.15), channel_id=1, source_target_pairs={{0,1},{1,0},{2,3},{3,2},{4,5},{5,4},{6,7},{7,6},{8,9},{9,8},{10,11... | collective-permute-start | bytes 1572872 | tf_op jit(solution)/shard_map/ppermute | solution.py:22
  52.9 27.7 %collective-permute-start.11 = (f32[8,128,128]{2,1,0:T(8,128)}, f32[8,128,128]{2,1,0:T(8,128)S(1)}, u32[]{:S(2)}, u32[]{:S(2)}) collective-permute-start(f32[8,128,128]{2,1,0:T(8,128)} %copy-done.14), channel_id=1, source_target_pairs={{1,2},{2,1},{3,4},{4,3},{5,6},{6,5},{7,8},{8,7},{9,10},{10,9},{11,... | collective-permute-start | bytes 1572872 | tf_op jit(solution)/shard_map/ppermute | solution.py:22
  57.7 35.7 %copy-start.1 = (f32[8,8,128,128]{3,2,1,0:T(8,128)S(1)}, f32[8,8,128,128]{3,2,1,0:T(8,128)}, u32[]{:S(2)}) copy-start(f32[8,8,128,128]{3,2,1,0:T(8,128)} %r_ref.7) | copy-start | bytes 12582916
  57.7 35.7 %copy-start.2 = (f32[8,8,4,128]{3,2,1,0:T(4,128)S(1)}, f32[8,8,4,128]{3,2,1,0:T(4,128)}, u32[]{:S(2)}) copy-start(f32[8,8,4,128]{3,2,1,0:T(4,128)} %face_ref.7) | copy-start | bytes 393220
  80.6 2.0 %collective-permute-start.12 = (f32[2,10,32,128]{3,2,1,0:T(8,128)S(1)}, f32[2,10,32,128]{3,2,1,0:T(8,128)S(1)}, u32[]{:S(2)}, u32[]{:S(2)}) collective-permute-start(f32[2,10,32,128]{3,2,1,0:T(8,128)S(1)} %get-tuple-element.75), channel_id=1, source_target_pairs={{0,32},{1,33},{2,34},{3,35},{4,36},{5,37},{6,38},{7,39},{8,40},{9,... | collective-permute-start | bytes 983048 | tf_op jit(solution)/shard_map/ppermute | solution.py:22
  82.7 20.5 %collective-permute-start.16 = (f32[2,10,32,128]{3,2,1,0:T(8,128)S(1)}, f32[2,10,32,128]{3,2,1,0:T(8,128)S(1)}, u32[]{:S(2)}, u32[]{:S(2)}) collective-permute-start(f32[2,10,32,128]{3,2,1,0:T(8,128)S(1)} %pad_maximum_fusion.refs_5_), channel_id=1, source_target_pairs={{1,2},{2,1},{3,4},{4,3},{5,6},{6,5},{7,8},{8,7},{9,10},{10,9},{11,... | collective-permute-start | bytes 983048 | tf_op jit(solution)/shard_map/ppermute | solution.py:22
  83.3 21.2 %collective-permute-start.13 = (f32[2,10,32,128]{3,2,1,0:T(8,128)S(1)}, f32[2,10,32,128]{3,2,1,0:T(8,128)S(1)}, u32[]{:S(2)}, u32[]{:S(2)}) collective-permute-start(f32[2,10,32,128]{3,2,1,0:T(8,128)S(1)} %pad_maximum_fusion.refs_5_), channel_id=1, source_target_pairs={{0,1},{1,0},{2,3},{3,2},{4,5},{5,4},{6,7},{7,6},{8,9},{9,8},{10,11... | collective-permute-start | bytes 983048 | tf_op jit(solution)/shard_map/ppermute | solution.py:22
  90.2 21.4 %collective-permute-start.17 = (f32[2,10,32,128]{3,2,1,0:T(8,128)S(1)}, f32[2,10,32,128]{3,2,1,0:T(8,128)S(1)}, u32[]{:S(2)}, u32[]{:S(2)}) collective-permute-start(f32[2,10,32,128]{3,2,1,0:T(8,128)S(1)} %pad_maximum_fusion.1), channel_id=1, source_target_pairs={{0,64},{1,65},{2,66},{3,67},{4,68},{5,69},{6,70},{7,71},{8,72},{9,... | collective-permute-start | bytes 983048 | tf_op jit(solution)/shard_map/ppermute | solution.py:22
  91.7 20.0 %collective-permute-start.15 = (f32[2,10,32,128]{3,2,1,0:T(8,128)S(1)}, f32[2,10,32,128]{3,2,1,0:T(8,128)S(1)}, u32[]{:S(2)}, u32[]{:S(2)}) collective-permute-start(f32[2,10,32,128]{3,2,1,0:T(8,128)S(1)} %pad_maximum_fusion.1), channel_id=1, source_target_pairs={{0,65},{1,64},{2,67},{3,66},{4,69},{5,68},{6,71},{7,70},{8,73},{9,... | collective-permute-start | bytes 983048 | tf_op jit(solution)/shard_map/ppermute | solution.py:22
  92.7 18.9 %collective-permute-start.14 = (f32[2,10,32,128]{3,2,1,0:T(8,128)S(1)}, f32[2,10,32,128]{3,2,1,0:T(8,128)S(1)}, u32[]{:S(2)}, u32[]{:S(2)}) collective-permute-start(f32[2,10,32,128]{3,2,1,0:T(8,128)S(1)} %pad_maximum_fusion.1), channel_id=1, source_target_pairs={{1,66},{2,65},{3,68},{4,67},{5,70},{6,69},{7,72},{8,71},{9,74},{10... | collective-permute-start | bytes 983048 | tf_op jit(solution)/shard_map/ppermute | solution.py:22
  112.7 23.0 %collective-permute-start.18 = (f32[8,128,128]{2,1,0:T(8,128)S(1)}, f32[8,128,128]{2,1,0:T(8,128)S(1)}, u32[]{:S(2)}, u32[]{:S(2)}) collective-permute-start(f32[8,128,128]{2,1,0:T(8,128)S(1)} %get-tuple-element.78), channel_id=1, source_target_pairs={{0,1},{1,0},{2,3},{3,2},{4,5},{5,4},{6,7},{7,6},{8,9},{9,8},{10,11... | collective-permute-start | bytes 1572872 | tf_op jit(solution)/shard_map/ppermute | solution.py:22
  115.0 20.7 %collective-permute-start.19 = (f32[8,128,128]{2,1,0:T(8,128)S(1)}, f32[8,128,128]{2,1,0:T(8,128)S(1)}, u32[]{:S(2)}, u32[]{:S(2)}) collective-permute-start(f32[8,128,128]{2,1,0:T(8,128)S(1)} %get-tuple-element.79), channel_id=1, source_target_pairs={{1,2},{2,1},{3,4},{4,3},{5,6},{6,5},{7,8},{8,7},{9,10},{10,9},{11,... | collective-permute-start | bytes 1572872 | tf_op jit(solution)/shard_map/ppermute | solution.py:22
  123.0 15.5 %collective-permute-start.20 = (f32[8,128,128]{2,1,0:T(8,128)S(1)}, f32[8,128,128]{2,1,0:T(8,128)S(1)}, u32[]{:S(2)}, u32[]{:S(2)}) collective-permute-start(f32[8,128,128]{2,1,0:T(8,128)S(1)} %get-tuple-element.80), channel_id=1, source_target_pairs={{0,32},{1,33},{2,34},{3,35},{4,36},{5,37},{6,38},{7,39},{8,40},{9,... | collective-permute-start | bytes 1572872 | tf_op jit(solution)/shard_map/ppermute | solution.py:22
  125.0 22.6 %collective-permute-start.21 = (f32[8,128,128]{2,1,0:T(8,128)S(1)}, f32[8,128,128]{2,1,0:T(8,128)S(1)}, u32[]{:S(2)}, u32[]{:S(2)}) collective-permute-start(f32[8,128,128]{2,1,0:T(8,128)S(1)} %get-tuple-element.81), channel_id=1, source_target_pairs={{32,64},{33,65},{34,66},{35,67},{36,68},{37,69},{38,70},{39,71},{4... | collective-permute-start | bytes 1572872 | tf_op jit(solution)/shard_map/ppermute | solution.py:22
  (19 other events, 287.1 us)
